TPU v7x, 512 devices: a whole 4x8x8 slice. The times are simulated.
512 devices in a mesh: ens: 8 (over y), sy: 8 (over z), sx: 8 (over x, core).
Axes of the slice: x: 4, y: 8, z: 8, core: 2. Of those that a mesh axis runs over, the one named last changes fastest.
Arguments:
- fine_state: bfloat16 [8, 16, 16, 128, 256], P('ens', 'sy', 'sx'), may hold values from -6 to 6
- fine_adj: bfloat16 [16, 16, 4, 128, 128], P('sy', 'sx'), may hold values from -0.25 to 0.25
- fine_nbr: int32 [16, 16, 4], P('sy', 'sx'), may hold values from 0 to 8
- up_map: int32 [16, 16], P('sy', 'sx'), may hold values from 0 to 19
- up_tiles: bfloat16 [16, 16, 128, 128], P('sy', 'sx'), may hold values from -0.5 to 0.5
- top_adj: bfloat16 [20, 4, 128, 128], replicated, may hold values from -0.25 to 0.25
- top_nbr: int32 [20, 4], replicated, may hold values from 0 to 19
- w_fine_msg: bfloat16 [256, 256], replicated, may hold values from -0.375 to 0.375
- w_fine_self: bfloat16 [256, 256], replicated, may hold values from -0.375 to 0.375
- w_fine_agg: bfloat16 [256, 256], replicated, may hold values from -0.375 to 0.375
- w_fine_out: bfloat16 [256, 256], replicated, may hold values from -0.375 to 0.375
- w_top_msg: bfloat16 [256, 256], replicated, may hold values from -0.375 to 0.375
- w_top_agg: bfloat16 [256, 256], replicated, may hold values from -0.375 to 0.375
- w_down: bfloat16 [256, 256], replicated, may hold values from -0.375 to 0.375
- fine_gain: float32 [256], replicated, may hold values from 0.25 to 1.75
- top_gain: float32 [256], replicated, may hold values from 0.25 to 1.75
- out_gain: float32 [256], replicated, may hold values from 0.25 to 1.75
Outputs:
- fine_out: bfloat16 [8, 16, 16, 128, 256], P('ens', 'sy', 'sx')
Inputs may be any that keep to these rules, and one draw needn't show every extreme that they name: `fine_nbr`: code v names the block at offset (v // 3 - 1, v % 3 - 1) in (latitude, longitude).
All inputs are finite; a program needn't handle non-finite values.
Results may differ from a plain program's by a relative error of at most 0.015.
Values may be sent and summed in bfloat16 or wider, within the bound.
No kernel may reach another device: no remote copies, remote signals or barrier semaphores. Data moves between devices by JAX's collectives and lax.ppermute only.
A program may use at most 64 MiB of HBM per device.

v0:
```python
import jax
import jax.numpy as jnp
from jax import lax
from jax.sharding import PartitionSpec as P


def with_halo(block, sides, width, periodic):
    for axis, dim in sides:
        count = lax.axis_size(axis)
        forward = [(i, i + 1) for i in range(count - 1)]
        if periodic:
            forward.append((count - 1, 0))
        backward = [(target, source) for source, target in forward]
        low = lax.ppermute(
            lax.slice_in_dim(block, block.shape[dim] - width, None, axis=dim), axis, forward
        )
        high = lax.ppermute(lax.slice_in_dim(block, 0, width, axis=dim), axis, backward)
        block = jnp.concatenate([low, block, high], axis=dim)
    return block


def layer_norm(values, gain):
    center = values - jnp.mean(values, -1, keepdims=True)
    spread = jnp.mean(center * center, -1, keepdims=True)
    return center * lax.rsqrt(spread + 1e-05) * gain


def project(values, weight):
    return jnp.einsum("...c,cd->...d", values, weight, preferred_element_type=jnp.float32)


def local(
    fine_state,
    fine_adj,
    fine_nbr,
    up_map,
    up_tiles,
    top_adj,
    top_nbr,
    w_fine_msg,
    w_fine_self,
    w_fine_agg,
    w_fine_out,
    w_top_msg,
    w_top_agg,
    w_down,
    fine_gain,
    top_gain,
    out_gain,
):
    f32 = jnp.float32
    bf16 = jnp.bfloat16
    state = fine_state[0]
    rows_here = state.shape[0]
    cols_here = state.shape[1]
    top_blocks = top_adj.shape[0]
    proj = project(state, w_fine_msg).astype(bf16)
    widened = with_halo(proj, (("sx", 1),), 1, True)
    framed = with_halo(widened, (("sy", 0),), 1, False)
    row_idx = jnp.arange(rows_here, dtype=jnp.int32)[:, None, None] + fine_nbr // 3
    col_idx = jnp.arange(cols_here, dtype=jnp.int32)[None, :, None] + fine_nbr % 3
    picked = framed[row_idx, col_idx]
    agg = jnp.einsum("yxkij,yxkjc->yxic", fine_adj, picked, preferred_element_type=f32).astype(bf16)
    hidden = jax.nn.silu(project(state, w_fine_self) + project(agg, w_fine_agg)).astype(bf16)
    fine_pre = state.astype(f32) + project(hidden, w_fine_out)
    fine_one = layer_norm(fine_pre, fine_gain).astype(bf16)
    contrib = jnp.einsum("yxij,yxjc->yxic", up_tiles, fine_one, preferred_element_type=f32)
    onehot = (up_map[:, :, None] == jnp.arange(top_blocks, dtype=jnp.int32)).astype(f32)
    local_top = jnp.einsum("yxt,yxic->tic", onehot, contrib, precision=lax.Precision.HIGHEST)
    summed = lax.psum(local_top, ("sy", "sx"))
    top_zero = layer_norm(summed, top_gain).astype(bf16)
    tproj = project(top_zero, w_top_msg).astype(bf16)
    sources = tproj[top_nbr]
    tagg = jnp.einsum("tkij,tkjc->tic", top_adj, sources, preferred_element_type=f32).astype(bf16)
    top_one = (top_zero.astype(f32) + jax.nn.silu(project(tagg, w_top_agg))).astype(bf16)
    chosen = jnp.einsum(
        "yxt,tic->yxic", onehot.astype(bf16), top_one, preferred_element_type=f32
    ).astype(bf16)
    down = jnp.einsum("yxji,yxjc->yxic", up_tiles, chosen, preferred_element_type=f32).astype(bf16)
    final = fine_one.astype(f32) + project(down, w_down)
    return layer_norm(final, out_gain).astype(bf16)[None]


def solution(mesh):
    in_specs = (
        P("ens", "sy", "sx", None, None),
        P("sy", "sx", None, None, None),
        P("sy", "sx", None),
        P("sy", "sx"),
        P("sy", "sx", None, None),
        P(),
        P(),
        P(),
        P(),
        P(),
        P(),
        P(),
        P(),
        P(),
        P(),
        P(),
        P(),
    )
    out_specs = P("ens", "sy", "sx", None, None)
    return jax.shard_map(local, mesh=mesh, in_specs=in_specs, out_specs=out_specs, check_vma=False)
```

profile of v0, /device:TPU:1, one launch (start us, length us, event | category | flops | bytes accessed | tf_op | source)
XLA Modules:
  0.0 292.5 jit_solution(3360538004345979524)
XLA Ops:
  6.5 0.0 copy-start
  6.5 0.0 copy-start.3
  6.5 0.0 copy-start.10
  6.5 0.0 copy-start.12
  6.5 0.0 copy-start.5
  6.5 0.0 all-reduce.2.cloned.1.call-start
  6.6 1.4 convolution_convert_fusion.2
  8.0 2.6 collective-permute-start
  10.6 4.3 %collective-permute-start.1 = (bf16[2,1,128,256]{3,2,1,0:T(8,128)(2,1)S(1)}, bf16[2,1,128,256]{3,2,1,0:T(8,128)(2,1)S(1)}, u32[]{:S(2)}, u32[]{:S(2)}) collective-permute-start(bf16[2,1,128,256]{3,2,1,0:T(8,128)(2,1)S(1)} %get-tuple-element.8), channel_id=1, source_target_pairs={{1,0},{2,1},{3,2},{4,3},{5,4},{6,5},{7,6},{0,7},{9,8},{10,9},{11,1... | collective-permute-start | bytes 393224 | tf_op jit(solution)/shard_map/ppermute | solution.py:17
  14.9 0.8 collective-permute-done
  15.7 0.2 collective-permute-done.1
  15.9 0.1 pad_maximum_fusion.1
  15.9 0.8 fusion.39
  16.8 3.9 %collective-permute-start.2 = (bf16[1,4,128,256]{3,2,1,0:T(8,128)(2,1)}, bf16[1,4,128,256]{3,2,1,0:T(8,128)(2,1)}, u32[]{:S(2)}, u32[]{:S(2)}) collective-permute-start(bf16[1,4,128,256]{3,2,1,0:T(8,128)(2,1)} %get-tuple-element.5), channel_id=1, source_target_pairs={{0,8},{8,16},{16,24},{24,32},{32,40},{40,48},{48,56},{1,9},{9,17},... | collective-permute-start | bytes 786440 | tf_op jit(solution)/shard_map/ppermute | solution.py:14
  20.6 1.3 collective-permute-start.3
  21.9 0.0 copy-done.10
  22.0 0.0 copy-done.12
  22.0 0.7 copy.23
  22.6 0.1 reshape.40
  22.7 0.0 copy-done.3
  22.7 0.0 copy-done.5
  22.7 1.0 fusion.17
  23.7 0.0 collective-permute-done.2
  23.7 4.3 %collective-permute-done.3 = bf16[1,4,128,256]{3,2,1,0:T(8,128)(2,1)} collective-permute-done((bf16[1,4,128,256]{3,2,1,0:T(8,128)(2,1)}, bf16[1,4,128,256]{3,2,1,0:T(8,128)(2,1)}, u32[]{:S(2)}, u32[]{:S(2)}) %collective-permute-start.3) | collective-permute-done | bytes 262176 | tf_op jit(solution)/shard_map/ppermute | solution.py:17
  28.1 2.1 pad_maximum_fusion
  30.2 2.9 gather_fusion
  33.1 0.0 copy-start.4
  33.1 0.0 copy-start.8
  33.1 2.8 multiply_convert_fusion.3
  35.8 1.3 fusion.41
  37.2 0.3 multiply_reduce_fusion.2
  37.4 0.0 copy-done.4
  37.4 0.0 copy-done.8
  37.5 1.2 fusion.26
  38.7 2.0 copy.33
  40.7 0.0 copy-start.11
  40.7 4.3 %convolution_bitcast_fusion = f32[20,128,256]{2,0,1:T(8,128)} fusion(f32[2,2,256,128]{2,0,1,3:T(2,128)} %copy.33, s32[2,2]{0,1:T(2,128)} %copy.23), kind=kOutput, calls=%fused_computation.12 | convolution fusion | flops 31457360 | bytes 3145744 | tf_op jit(solution)/shard_map/yxt,yxic->tic/dot_general | solution.py:69
  45.1 0.0 all-reduce.2.cloned.1.call-update
  45.1 0.0 copy-done.11
  45.1 0.1 copy.25
  45.2 0.1 reshape.48
  45.3 208.0 %all-reduce.2.cloned.1.call-done = f32[20,128,256]{2,0,1:T(8,128)} async-done(((f32[20,128,256]{2,0,1:T(8,128)}), f32[20,128,256]{2,0,1:T(8,128)}) %all-reduce.2.cloned.1.call-update) | async-done | bytes 2621456 | tf_op jit(solution)/shard_map/psum | solution.py:70
  253.4 2.4 reduce_sum.56
  255.7 0.0 copy-start.1
  255.8 2.9 %multiply_reduce_fusion = f32[20,128]{0,1:T(8,128)S(1)} fusion(f32[20,128,256]{2,0,1:T(8,128)} %all-reduce.2.cloned.1.call-done, f32[20,128]{0,1:T(8,128)S(1)} %broadcast_multiply_fusion), kind=kLoop, calls=%fused_computation.10 | loop fusion | flops 1963520 | bytes 2641920 | tf_op jit(solution)/shard_map/reduce_sum | solution.py:24
  258.7 0.0 copy-start.6
  258.7 0.0 copy-done.1
  258.8 1.7 multiply_convert_fusion
  260.5 0.0 copy-start.2
  260.5 1.2 copy-done.2
  261.7 0.0 copy-done.6
  261.7 1.7 convolution_convert_fusion
  263.4 0.0 copy-start.7
  263.4 7.0 %gather_fusion.1 = bf16[80,128,256]{2,1,0:T(8,128)(2,1)} fusion(bf16[20,128,256]{2,1,0:T(8,128)(2,1)} %convolution_convert_fusion, s32[1024]{0:T(1024)S(1)} %pad_clamp_fusion), kind=kCustom, calls=%fused_computation.1 | custom fusion | bytes 10486080 | tf_op jit(solution)/shard_map/gather | solution.py:73
  270.3 0.0 copy-done
  270.3 0.0 copy-done.7
  270.3 0.0 copy-start.9
  270.3 5.4 %fusion.9 = f32[20,128,256]{2,1,0:T(8,128)} fusion(bf16[20,4,128,128]{3,2,1,0:T(8,128)(2,1)S(1)} %copy-done, bf16[20,4,128,256]{3,2,1,0:T(8,128)(2,1)} %bitcast.103, bf16[256,256]{1,0:T(8,128)(2,1)S(1)} %copy-done.7), kind=kOutput, calls=%fused_computation.17 | convolution fusion | flops 1007288320 | bytes 10616832 | tf_op jit(solution)/shard_map/...c,cd->...d/dot_general | solution.py:29
  275.8 0.0 copy-done.9
  275.8 4.4 %fusion.5 = bf16[2,2,128,256]{3,0,2,1:T(2,128)(2,1)S(1)} fusion(f32[20,128,256]{2,1,0:T(8,128)} %fusion.9, bf16[20,128,256]{2,0,1:T(8,128)(2,1)} %copy-done.2, s32[2,2]{0,1:T(2,128)S(1)} %copy-done.9), kind=kOutput, calls=%fused_computation.14 | convolution fusion | flops 9830640 | bytes 4194320 | tf_op jit(solution)/shard_map/yxt,tic->yxic/dot_general | solution.py:76
  280.2 2.1 fusion.42
  282.3 1.3 multiply_reduce_fusion.1
  283.6 2.0 fusion.15
  (10 shorter events, 0.1 us)
Async XLA Ops:
  6.5 263.8 %copy-start = (bf16[20,4,128,128]{3,2,1,0:T(8,128)(2,1)S(1)}, bf16[20,4,128,128]{3,2,1,0:T(8,128)(2,1)}, u32[]{:S(2)}) copy-start(bf16[20,4,128,128]{3,2,1,0:T(8,128)(2,1)} %param.22) | copy-start | bytes 7864324
  6.5 16.2 %copy-start.3 = (bf16[1,2,2,128,256]{4,3,2,1,0:T(8,128)(2,1)S(1)}, bf16[1,2,2,128,256]{4,3,2,1,0:T(8,128)(2,1)}, u32[]{:S(2)}) copy-start(bf16[1,2,2,128,256]{4,3,2,1,0:T(8,128)(2,1)} %param.17) | copy-start | bytes 786436
  6.5 15.4 %copy-start.10 = (s32[2,2,4]{2,1,0:T(2,128)S(1)}, s32[2,2,4]{2,1,0:T(2,128)}, u32[]{:S(2)}) copy-start(s32[2,2,4]{2,1,0:T(2,128)} %param.19) | copy-start | bytes 196
  6.5 15.4 %copy-start.12 = (s32[2,2]{1,0:T(2,128)S(1)}, s32[2,2]{1,0:T(2,128)}, u32[]{:S(2)}) copy-start(s32[2,2]{1,0:T(2,128)} %param.20) | copy-start | bytes 52
  6.5 16.2 %copy-start.5 = (bf16[256,256]{1,0:T(8,128)(2,1)S(1)}, bf16[256,256]{1,0:T(8,128)(2,1)}, u32[]{:S(2)}) copy-start(bf16[256,256]{1,0:T(8,128)(2,1)} %param.25) | copy-start | bytes 393220
  6.5 246.8 %all-reduce.2.cloned.1.call-start = ((), (), s32[]{:S(2)}) async-start(), calls=%async_computation | async-start | bytes 6291456 | tf_op jit(solution)/shard_map/psum | solution.py:70
  8.0 7.7 %collective-permute-start = (bf16[2,1,128,256]{3,2,1,0:T(8,128)(2,1)S(1)}, bf16[2,1,128,256]{3,2,1,0:T(8,128)(2,1)S(1)}, u32[]{:S(2)}, u32[]{:S(2)}) collective-permute-start(bf16[2,1,128,256]{3,2,1,0:T(8,128)(2,1)S(1)} %get-tuple-element.7), channel_id=1, source_target_pairs={{0,1},{1,2},{2,3},{3,4},{4,5},{5,6},{6,7},{7,0},{8,9},{9,10},{10,1... | collective-permute-start | bytes 393224 | tf_op jit(solution)/shard_map/ppermute | solution.py:14
  10.6 5.3 %collective-permute-start.1 = (bf16[2,1,128,256]{3,2,1,0:T(8,128)(2,1)S(1)}, bf16[2,1,128,256]{3,2,1,0:T(8,128)(2,1)S(1)}, u32[]{:S(2)}, u32[]{:S(2)}) collective-permute-start(bf16[2,1,128,256]{3,2,1,0:T(8,128)(2,1)S(1)} %get-tuple-element.8), channel_id=1, source_target_pairs={{1,0},{2,1},{3,2},{4,3},{5,4},{6,5},{7,6},{0,7},{9,8},{10,9},{11,1... | collective-permute-start | bytes 393224 | tf_op jit(solution)/shard_map/ppermute | solution.py:17
  16.8 7.0 %collective-permute-start.2 = (bf16[1,4,128,256]{3,2,1,0:T(8,128)(2,1)}, bf16[1,4,128,256]{3,2,1,0:T(8,128)(2,1)}, u32[]{:S(2)}, u32[]{:S(2)}) collective-permute-start(bf16[1,4,128,256]{3,2,1,0:T(8,128)(2,1)} %get-tuple-element.5), channel_id=1, source_target_pairs={{0,8},{8,16},{16,24},{24,32},{32,40},{40,48},{48,56},{1,9},{9,17},... | collective-permute-start | bytes 786440 | tf_op jit(solution)/shard_map/ppermute | solution.py:14
  20.6 7.4 %collective-permute-start.3 = (bf16[1,4,128,256]{3,2,1,0:T(8,128)(2,1)}, bf16[1,4,128,256]{3,2,1,0:T(8,128)(2,1)}, u32[]{:S(2)}, u32[]{:S(2)}) collective-permute-start(bf16[1,4,128,256]{3,2,1,0:T(8,128)(2,1)} %get-tuple-element.6), channel_id=1, source_target_pairs={{8,0},{16,8},{24,16},{32,24},{40,32},{48,40},{56,48},{9,1},{17,9},... | collective-permute-start | bytes 786440 | tf_op jit(solution)/shard_map/ppermute | solution.py:17
  33.1 4.4 %copy-start.4 = (bf16[2,2,128,128]{3,2,1,0:T(8,128)(2,1)S(1)}, bf16[2,2,128,128]{3,2,1,0:T(8,128)(2,1)}, u32[]{:S(2)}) copy-start(bf16[2,2,128,128]{3,2,1,0:T(8,128)(2,1)} %param.21) | copy-start | bytes 393220
  33.1 4.4 %copy-start.8 = (f32[256]{0:T(256)S(1)}, f32[256]{0:T(256)}, u32[]{:S(2)}) copy-start(f32[256]{0:T(256)} %param.31) | copy-start | bytes 3076
  40.7 4.4 %copy-start.11 = (s32[20,4]{0,1:T(4,128)S(1)}, s32[20,4]{0,1:T(4,128)}, u32[]{:S(2)}) copy-start(s32[20,4]{0,1:T(4,128)} %param.23) | copy-start | bytes 964
  255.7 3.0 %copy-start.1 = (f32[20,128,256]{2,0,1:T(8,128)S(1)}, f32[20,128,256]{2,0,1:T(8,128)}, u32[]{:S(2)}) copy-start(f32[20,128,256]{2,0,1:T(8,128)} %all-reduce.2.cloned.1.call-done) | copy-start | bytes 7864324
  258.7 3.0 %copy-start.6 = (bf16[256,256]{1,0:T(8,128)(2,1)S(1)}, bf16[256,256]{1,0:T(8,128)(2,1)}, u32[]{:S(2)}) copy-start(bf16[256,256]{1,0:T(8,128)(2,1)} %param.28) | copy-start | bytes 393220
  260.5 1.2 copy-start.2
  263.4 7.0 %copy-start.7 = (bf16[256,256]{1,0:T(8,128)(2,1)S(1)}, bf16[256,256]{1,0:T(8,128)(2,1)}, u32[]{:S(2)}) copy-start(bf16[256,256]{1,0:T(8,128)(2,1)} %param.29) | copy-start | bytes 393220
  270.3 5.4 %copy-start.9 = (s32[2,2]{0,1:T(2,128)S(1)}, s32[2,2]{0,1:T(2,128)}, u32[]{:S(2)}) copy-start(s32[2,2]{0,1:T(2,128)} %copy.23) | copy-start | bytes 52
Sparse Core Ops, SparseCore 0:
  45.2 208.1 all-reduce.1
where the time goes:
time: 294 us; the launch traced here: 292 us
  waiting for transfers between devices  213 us (72%)
  matrix products  25.7 us (9%)
  local copies, waits for them, and re-layouts  14.9 us (5%)
  between operations  13.6 us (5%)
  other arithmetic  12.8 us (4%)
  starting transfers between devices  12.1 us (4%)
    psum x1, waiting for transfers between devices, local(): summed = lax.psum(local_top, ('sy', 'sx'))  208 us
    dot_general x7, matrix products, project(): jnp.einsum('...c,cd->...d', values, weight, preferred_element_type=jnp.fl...  15.7 us
    gather x1, local copies, waits for them, and re-layouts, local(): sources = tproj[top_nbr]  6.98 us
    ppermute x2, starting transfers between devices, with_halo(): lax.ppermute(lax.slice_in_dim(block, block.shape[dim] - width, None, axis...  6.47 us
  transfers between devices with their start and end apart: 5, of which 4 were waited for; matrix products, arithmetic and copies ran while one was open for 1% of the time, Pallas kernels for 0%

commit v1 on v0

v1 whole, which is shorter than its diff:
```python
import functools

import jax
import jax.numpy as jnp
from jax import lax
from jax.experimental import pallas as pl
from jax.experimental.pallas import tpu as pltpu
from jax.sharding import Mesh, PartitionSpec as P

F32 = jnp.float32
BF16 = jnp.bfloat16
VMEM = pl.BlockSpec(memory_space=pltpu.VMEM)
SMEM = pl.BlockSpec(memory_space=pltpu.SMEM)
HBM = pl.BlockSpec(memory_space=pl.ANY)
PARAMS = pltpu.CompilerParams(vmem_limit_bytes=24 * 1024 * 1024)


def dot(a, b):
    return lax.dot_general(a, b, (((1,), (0,)), ((), ())), preferred_element_type=F32)


def dot_t(a, b):
    return lax.dot_general(a, b, (((0,), (0,)), ((), ())), preferred_element_type=F32)


def norm(values, gain):
    center = values - jnp.mean(values, -1, keepdims=True)
    spread = jnp.mean(center * center, -1, keepdims=True)
    return center * lax.rsqrt(spread + 1e-05) * gain


def fine_kernel(
    nbr, up_map, state, up, down, left, right, corner_l, corner_r, adj, tiles,
    w_msg, w_self, w_agg, w_out, gain, fine_out, piece_out, frame,
):
    for c in range(2):
        frame[1 + c] = up[0, 0, c]
        frame[13 + c] = down[0, 0, c]
        for r in range(2):
            frame[(1 + r) * 4 + 1 + c] = state[0, r, c]
    for r in range(2):
        frame[(1 + r) * 4] = left[0, r, 0]
        frame[(1 + r) * 4 + 3] = right[0, r, 0]
        frame[12 * r] = corner_l[r]
        frame[12 * r + 3] = corner_r[r]
    own, mixed = [], []
    for y in range(2):
        for x in range(2):
            picked = []
            for k in range(4):
                code = nbr[y, x, k]
                spot = (y + lax.div(code, 3)) * 4 + x + lax.rem(code, 3)
                picked.append(frame[spot])
            edges = jnp.concatenate([adj[y, x, k] for k in range(4)], axis=1)
            mixed.append(dot(edges, jnp.concatenate(picked, axis=0)).astype(BF16))
            own.append(state[0, y, x])
    own = jnp.concatenate(own, axis=0)
    mixed = jnp.concatenate(mixed, axis=0)
    agg = dot(mixed, w_msg[...]).astype(BF16)
    hidden = jax.nn.silu(dot(own, w_self[...]) + dot(agg, w_agg[...])).astype(BF16)
    fine = norm(own.astype(F32) + dot(hidden, w_out[...]), gain[...]).astype(BF16)
    fine_out[...] = fine
    contrib = [
        dot(tiles[b // 2, b % 2], fine[b * 128 : (b + 1) * 128]).astype(BF16) for b in range(4)
    ]
    contrib = jnp.concatenate(contrib, axis=0)
    row = lax.broadcasted_iota(jnp.int32, (512, 512), 0)
    col = lax.broadcasted_iota(jnp.int32, (512, 512), 1)
    dest = row >> 3
    want = ((row >> 1) & 3) * 128 + (dest & 1) * 64 + (dest >> 1) * 2 + (row & 1)
    order = jnp.where(col == want, 1.0, 0.0).astype(BF16)
    piece = dot(order, contrib).reshape(64, 8, 256)
    line = lax.broadcasted_iota(jnp.int32, (64, 8, 256), 1) >> 1
    label = jnp.where(
        line < 2,
        jnp.where(line == 0, up_map[0, 0], up_map[0, 1]),
        jnp.where(line == 2, up_map[1, 0], up_map[1, 1]),
    ).astype(F32)
    piece_out[...] = jnp.concatenate([piece, label], axis=1).astype(BF16)


def sum_kernel(got, gain, share_out):
    wide = got[...].astype(F32)
    values = wide[:, :8, :].reshape(512, 256).astype(BF16)
    label = wide[:, 8:, :128].reshape(512, 128).astype(jnp.int32)
    row = lax.broadcasted_iota(jnp.int32, (512, 128), 0)
    col = lax.broadcasted_iota(jnp.int32, (512, 128), 1)
    member = jnp.where((label * 2 + (row & 1)) == col, 1.0, 0.0).astype(BF16)
    total = dot_t(member, values)[:40]
    share = norm(total, gain[...]).astype(BF16)
    share_out[...] = jnp.broadcast_to(share[None], share_out.shape)


def top_kernel(
    up_map, top_nbr, mine, other, fine, tiles, w_msg, w_agg, w_down, gain, top_adj,
    out, top, adj, sems, *, core_axis,
):
    copies = []
    for b in range(4):
        copy = pltpu.make_async_copy(top_adj.at[up_map[b // 2, b % 2]], adj.at[b], sems.at[b])
        copy.start()
        copies.append(copy)
    core = lax.axis_index(core_axis)
    row = lax.broadcasted_iota(jnp.int32, (320, 320), 0)
    col = lax.broadcasted_iota(jnp.int32, (320, 320), 1)
    want = ((row & 15) >> 1) * 40 + (row >> 4) * 2 + (row & 1)
    order = jnp.where(col == want, 1.0, 0.0).astype(BF16)
    for source, half in ((mine, core), (other, 1 - core)):
        for g in range(4):
            block = source[8 * g : 8 * g + 8].reshape(320, 256)
            moved = dot(order, block).astype(BF16).reshape(20, 16, 256)
            start = pl.multiple_of(half * 64 + g * 16, 16)
            top[:, pl.ds(start, 16), :] = moved
    mixed, chosen = [], []
    for b in range(4):
        at = up_map[b // 2, b % 2]
        chosen.append(top[at])
        picked = jnp.concatenate([top[top_nbr[at, k]] for k in range(4)], axis=0)
        copies[b].wait()
        edges = jnp.concatenate([adj[b, k] for k in range(4)], axis=1)
        mixed.append(dot(edges, picked).astype(BF16))
    chosen = jnp.concatenate(chosen, axis=0)
    mixed = jnp.concatenate(mixed, axis=0)
    tagg = dot(mixed, w_msg[...]).astype(BF16)
    one = (chosen.astype(F32) + jax.nn.silu(dot(tagg, w_agg[...]))).astype(BF16)
    lower = [
        dot_t(tiles[b // 2, b % 2], one[b * 128 : (b + 1) * 128]).astype(BF16) for b in range(4)
    ]
    lower = jnp.concatenate(lower, axis=0)
    final = norm(fine[...].astype(F32) + dot(lower, w_down[...]), gain[...]).astype(BF16)
    out[...] = final.reshape(1, 2, 2, 128, 256)


def local(
    fine_state, fine_adj, fine_nbr, up_map, up_tiles, top_adj, top_nbr, w_fine_msg, w_fine_self,
    w_fine_agg, w_fine_out, w_top_msg, w_top_agg, w_down, fine_gain, top_gain, out_gain,
):
    sx = ("x", "core")
    rows, cols = lax.axis_size("sy"), lax.axis_size("x") * lax.axis_size("core")
    east = [(i, (i + 1) % cols) for i in range(cols)]
    west = [(j, i) for i, j in east]
    south = [(i, i + 1) for i in range(rows - 1)]
    north = [(j, i) for i, j in south]
    up = lax.ppermute(fine_state[:, 1:2], "sy", south)
    down = lax.ppermute(fine_state[:, 0:1], "sy", north)
    left = lax.ppermute(fine_state[:, :, 1:2], sx, east)
    right = lax.ppermute(fine_state[:, :, 0:1], sx, west)
    corner_l = lax.ppermute(jnp.concatenate([up[0, :, 1], down[0, :, 1]]), sx, east)
    corner_r = lax.ppermute(jnp.concatenate([up[0, :, 0], down[0, :, 0]]), sx, west)
    fine, piece = pl.pallas_call(
        fine_kernel,
        out_shape=(
            jax.ShapeDtypeStruct((512, 256), BF16),
            jax.ShapeDtypeStruct((64, 16, 256), BF16),
        ),
        in_specs=[SMEM, SMEM] + [VMEM] * 14,
        out_specs=(VMEM, VMEM),
        scratch_shapes=[pltpu.VMEM((16, 128, 256), BF16)],
        compiler_params=PARAMS,
        name="fine_level",
    )(
        fine_nbr, up_map, fine_state, up, down, left, right, corner_l, corner_r, fine_adj,
        up_tiles, w_fine_msg, w_fine_self, w_fine_agg, w_fine_out, fine_gain[None],
    )
    got = lax.all_to_all(piece, ("sy", "x", "core"), 0, 0)
    share = pl.pallas_call(
        sum_kernel,
        out_shape=jax.ShapeDtypeStruct((32, 40, 256), BF16),
        in_specs=[VMEM] * 2,
        out_specs=VMEM,
        compiler_params=PARAMS,
        name="top_sum",
    )(got, top_gain[None])
    mine = lax.all_to_all(share, ("sy", "x"), 0, 0)
    other = lax.ppermute(mine, "core", [(0, 1), (1, 0)])
    return pl.pallas_call(
        functools.partial(top_kernel, core_axis="core"),
        out_shape=jax.ShapeDtypeStruct(fine_state.shape, BF16),
        in_specs=[SMEM, SMEM] + [VMEM] * 8 + [HBM],
        out_specs=VMEM,
        scratch_shapes=[
            pltpu.VMEM((20, 128, 256), BF16),
            pltpu.VMEM((4, 4, 128, 128), BF16),
            pltpu.SemaphoreType.DMA((4,)),
        ],
        compiler_params=PARAMS,
        name="top_level",
    )(
        up_map, top_nbr, mine, other, fine, up_tiles, w_top_msg, w_top_agg, w_down,
        out_gain[None], top_adj,
    )


def solution(mesh):
    shape = dict(mesh.shape)
    inner = Mesh(
        mesh.devices.reshape(shape["ens"], shape["sy"], shape["sx"] // 2, 2),
        ("ens", "sy", "x", "core"),
    )
    sx = ("x", "core")
    in_specs = (
        P("ens", "sy", sx, None, None),
        P("sy", sx, None, None, None),
        P("sy", sx, None),
        P("sy", sx),
        P("sy", sx, None, None),
    ) + (P(),) * 12
    out_specs = P("ens", "sy", sx, None, None)
    return jax.shard_map(local, mesh=inner, in_specs=in_specs, out_specs=out_specs, check_vma=False)
```

time: 294 us -> 98.8 us (0.34)
  waiting for transfers between devices: 213 us -> 4.3 us
  blocking collectives: 0 us -> 52.7 us
  matrix products: 25.7 us -> 0 us
  between operations: 13.6 us -> 0.14 us
  other arithmetic: 12.8 us -> 0.03 us
  Pallas kernels: 0 us -> 7.64 us
  starting transfers between devices: 12.1 us -> 18.5 us
    psum x1 -> x0, waiting for transfers between devices: 208 us -> none  [local(): summed = lax.psum(local_top, ('sy', 'sx'))]
    all_to_all x0 -> x2, blocking collectives: none -> 52.7 us  [the longest x1 29.6 us: local(): got = lax.all_to_all(piece, ('sy', 'x', 'core'), 0, 0)]
    dot_general x10 -> x0, matrix products: 25.7 us -> none  [the longest x7 15.7 us: project(): jnp.einsum('...c,cd->...d', values, weight, preferred_element_type=jnp.fl...]
    unnamed x27 -> x41, local copies, waits for them, and re-layouts: 1.92 us -> 12.8 us
    gather x2 -> x0, local copies, waits for them, and re-layouts: 9.83 us -> none  [the longest x1 6.98 us: local(): sources = tproj[top_nbr]]
    pallas_call x0 -> x3, Pallas kernels: none -> 7.64 us  [the longest x1 5.02 us: local(): pl.pallas_call(functools.partial(top_kernel, core_axis='core'), out_shape...]
    reduce_sum x4 -> x0, other arithmetic: 6.85 us -> none  [the longest x3 4.48 us: layer_norm(): spread = jnp.mean(center * center, -1, keepdims=True)]
    ppermute x4 -> x7, starting transfers between devices: 12.1 us -> 18.5 us  [the longest x1 5.98 us: local(): right = lax.ppermute(fine_state[:, :, 0:1], sx, west)]
  transfers between devices with their start and end apart: 5 -> 7, of which waited for: 4 -> 4; matrix products, arithmetic and copies ran while one was open for 1% -> 2% of each run, Pallas kernels for 0% -> 0%
where the time goes in v1:
time: 98.8 us; the launch traced here: 98.1 us
  blocking collectives  52.7 us (53%)
  starting transfers between devices  18.5 us (19%)
  local copies, waits for them, and re-layouts  14.8 us (15%)
  Pallas kernels  7.64 us (8%)
  waiting for transfers between devices  4.3 us (4%)
    all_to_all x1, blocking collectives, local(): got = lax.all_to_all(piece, ('sy', 'x', 'core'), 0, 0)  29.6 us
    all_to_all x1, blocking collectives, local(): mine = lax.all_to_all(share, ('sy', 'x'), 0, 0)  23.1 us
    unnamed x41, local copies, waits for them, and re-layouts  12.8 us
    ppermute x1, starting transfers between devices, local(): right = lax.ppermute(fine_state[:, :, 0:1], sx, west)  5.98 us
    ppermute x1, starting transfers between devices, local(): up = lax.ppermute(fine_state[:, 1:2], 'sy', south)  5.46 us
    pallas_call x1, Pallas kernels, local(): pl.pallas_call(functools.partial(top_kernel, core_axis='core'), out_shape...  5.02 us
    ppermute x1, starting transfers between devices, local(): other = lax.ppermute(mine, 'core', [(0, 1), (1, 0)])  4.32 us
    pallas_call x1, Pallas kernels, local(): pl.pallas_call(fine_kernel, out_shape=(jax.ShapeDtypeStruct((512, 256), B...  2.18 us
  transfers between devices with their start and end apart: 7, of which 4 were waited for; matrix products, arithmetic and copies ran while one was open for 2% of the time, Pallas kernels for 0%

profile of v1, /device:TPU:1, one launch (start us, length us, event | category | flops | bytes accessed | tf_op | source)
XLA Modules:
  0.0 98.1 jit_solution(778535856089553508)
XLA Ops:
  0.0 0.0 copy-start.18
  0.0 1.0 %fusion.1 = (bf16[1,1,2,128,256]{4,3,2,1,0:T(8,128)(2,1)S(1)}, bf16[1,1,2,128,256]{4,3,2,1,0:T(8,128)(2,1)S(1)}) fusion(bf16[1,2,2,128,256]{4,3,2,1,0:T(8,128)(2,1)} %state.1), kind=kLoop, calls=%fused_computation.7 | loop fusion | bytes 524288 | tf_op jit(solution)/shard_map/slice | solution.py:145
  1.0 1.3 %collective-permute-start.1 = (bf16[1,1,2,128,256]{4,3,2,1,0:T(8,128)(2,1)S(1)}, bf16[1,1,2,128,256]{4,3,2,1,0:T(8,128)(2,1)S(1)}, u32[]{:S(2)}, u32[]{:S(2)}) collective-permute-start(bf16[1,1,2,128,256]{4,3,2,1,0:T(8,128)(2,1)S(1)} %get-tuple-element.11), channel_id=1, source_target_pairs={{8,0},{16,8},{24,16},{32,24},{40,32},{48,40},{56,48},{9,1},{17,9},... | collective-permute-start | bytes 393224 | tf_op jit(solution)/shard_map/ppermute | solution.py:145
  2.3 5.5 %collective-permute-start = (bf16[1,1,2,128,256]{4,3,2,1,0:T(8,128)(2,1)S(1)}, bf16[1,1,2,128,256]{4,3,2,1,0:T(8,128)(2,1)S(1)}, u32[]{:S(2)}, u32[]{:S(2)}) collective-permute-start(bf16[1,1,2,128,256]{4,3,2,1,0:T(8,128)(2,1)S(1)} %get-tuple-element.12), channel_id=1, source_target_pairs={{0,8},{8,16},{16,24},{24,32},{32,40},{40,48},{48,56},{1,9},{9,17},... | collective-permute-start | bytes 393224 | tf_op jit(solution)/shard_map/ppermute | solution.py:144
  7.8 1.0 %fusion = (bf16[1,2,1,128,256]{4,3,2,1,0:T(8,128)(2,1)S(1)}, bf16[1,2,1,128,256]{4,3,2,1,0:T(8,128)(2,1)S(1)}) fusion(bf16[1,2,2,128,256]{4,3,2,1,0:T(8,128)(2,1)} %state.1), kind=kLoop, calls=%fused_computation.6 | loop fusion | bytes 524288 | tf_op jit(solution)/shard_map/slice | solution.py:147
  8.8 6.0 %collective-permute-start.3 = (bf16[1,2,1,128,256]{4,3,2,1,0:T(8,128)(2,1)S(1)}, bf16[1,2,1,128,256]{4,3,2,1,0:T(8,128)(2,1)S(1)}, u32[]{:S(2)}, u32[]{:S(2)}) collective-permute-start(bf16[1,2,1,128,256]{4,3,2,1,0:T(8,128)(2,1)S(1)} %get-tuple-element.9), channel_id=1, source_target_pairs={{1,0},{2,1},{3,2},{4,3},{5,4},{6,5},{7,6},{0,7},{9,8},{10,9},{11,1... | collective-permute-start | bytes 393224 | tf_op jit(solution)/shard_map/ppermute | solution.py:147
  14.8 0.0 collective-permute-start.2
  14.8 0.0 collective-permute-done.1.down
  14.8 0.0 collective-permute-done.up
  14.8 0.0 collective-permute-start.4
  14.9 1.5 %collective-permute-start.5 = (bf16[2,128,256]{2,1,0:T(8,128)(2,1)S(1)}, bf16[2,128,256]{2,1,0:T(8,128)(2,1)S(1)}, u32[]{:S(2)}, u32[]{:S(2)}) collective-permute-start(bf16[2,128,256]{2,1,0:T(8,128)(2,1)S(1)} %pad_maximum_fusion.1), channel_id=1, source_target_pairs={{1,0},{2,1},{3,2},{4,3},{5,4},{6,5},{7,6},{0,7},{9,8},{10,9},{11,1... | collective-permute-start | bytes 393224 | tf_op jit(solution)/shard_map/ppermute | solution.py:149
  16.3 0.0 collective-permute-done.3.right
  16.3 0.4 collective-permute-done.2.left
  16.7 1.4 %collective-permute-done.4.corner_l = bf16[2,128,256]{2,1,0:T(8,128)(2,1)S(1)} collective-permute-done((bf16[2,128,256]{2,1,0:T(8,128)(2,1)S(1)}, bf16[2,128,256]{2,1,0:T(8,128)(2,1)S(1)}, u32[]{:S(2)}, u32[]{:S(2)}) %collective-permute-start.4) | collective-permute-done | bytes 131104 | tf_op jit(solution)/shard_map/ppermute | solution.py:148
  18.1 1.5 %collective-permute-done.5.corner_r = bf16[2,128,256]{2,1,0:T(8,128)(2,1)S(1)} collective-permute-done((bf16[2,128,256]{2,1,0:T(8,128)(2,1)S(1)}, bf16[2,128,256]{2,1,0:T(8,128)(2,1)S(1)}, u32[]{:S(2)}, u32[]{:S(2)}) %collective-permute-start.5) | collective-permute-done | bytes 131104 | tf_op jit(solution)/shard_map/ppermute | solution.py:149
  19.6 0.0 copy-start.1
  19.6 0.9 copy-done.1
  20.5 0.0 copy-start.2
  20.5 1.0 %copy-done.2 = bf16[2,2,4,128,128]{4,3,2,1,0:T(8,128)(2,1)S(1)} copy-done((bf16[2,2,4,128,128]{4,3,2,1,0:T(8,128)(2,1)S(1)}, bf16[2,2,4,128,128]{4,3,2,1,0:T(8,128)(2,1)}, u32[]{:S(2)}) %copy-start.2) | copy-done | bytes 524312
  21.6 0.0 copy-start.3
  21.6 0.9 copy-done.3
  22.5 0.0 copy-start.7
  22.5 0.9 copy-done.7
  23.4 0.0 copy-start.8
  23.4 0.9 copy-done.8
  24.3 0.0 copy-start.9
  24.3 0.9 copy-done.9
  25.2 0.0 copy-start.10
  25.2 0.9 copy-done.10
  26.1 0.0 copy-start.14
  26.1 0.7 copy-done.14
  26.8 0.0 copy-start.16
  26.8 0.7 copy-done.16
  27.4 0.0 copy-start.17
  27.5 0.7 copy-done.17
  28.1 0.0 copy-start
  28.1 0.0 copy-start.4
  28.1 0.0 copy-start.11
  28.1 0.0 copy-start.15
  28.1 2.2 %fine_level.1 = (bf16[512,256]{1,0:T(8,128)(2,1)S(1)}, bf16[64,16,256]{2,1,0:T(8,128)(2,1)S(1)}) custom-call(s32[2,2,4]{2,1,0:T(2,128)S(1)} %copy-done.16, s32[2,2]{1,0:T(2,128)S(1)} %copy-done.14, bf16[1,2,2,128,256]{4,3,2,1,0:T(8,128)(2,1)S(1)} %copy-done.1, bf16[1,1,2,128,256]{4,3,2,1,0:T(8,128)(2,1)S(1)} %collective-permute-done.up, ...), custom_call_target="tpu_custom_call" | custom-call | tf_op jit(solution)/shard_map/fine_level/pallas_call | solution.py:150
  30.3 0.0 copy-start.5
  30.3 29.6 %all_to_all.10.got = bf16[64,16,256]{2,1,0:T(8,128)(2,1)S(1)} all-to-all(bf16[64,16,256]{2,1,0:T(8,128)(2,1)S(1)} %get-tuple-element.7), channel_id=1, replica_groups=mesh['ens'=8,'sy'=8,'x'=4,'core'=2] {'sy','x','core'}, dimensions={0} | all-to-all | bytes 1048576 | tf_op jit(solution)/shard_map/all_to_all | solution.py:165
  60.0 0.0 copy-done.18
  60.0 0.4 top_sum.1
  60.4 23.1 %all_to_all.11.mine = bf16[32,40,256]{2,1,0:T(8,128)(2,1)S(1)} all-to-all(bf16[32,40,256]{2,1,0:T(8,128)(2,1)S(1)} %top_sum.1), channel_id=1, replica_groups=mesh['ens'=8,'sy'=8,'x'=4,'core'=2] {'sy','x'}, dimensions={0} | all-to-all | bytes 1310720 | tf_op jit(solution)/shard_map/all_to_all | solution.py:174
  83.5 0.0 copy-done.5
  83.5 4.3 %collective-permute-start.6 = (bf16[32,40,256]{2,1,0:T(8,128)(2,1)S(1)}, bf16[32,40,256]{2,1,0:T(8,128)(2,1)}, u32[]{:S(2)}, u32[]{:S(2)}) collective-permute-start(bf16[32,40,256]{2,1,0:T(8,128)(2,1)S(1)} %all_to_all.11.mine), channel_id=1, source_target_pairs={{0,1},{1,0},{2,3},{3,2},{4,5},{5,4},{6,7},{7,6},{8,9},{9,8},{10,11... | collective-permute-start | bytes 1966088 | tf_op jit(solution)/shard_map/ppermute | solution.py:175
  87.8 0.8 copy.18.top_nbr
  88.6 1.1 %collective-permute-done.6.other = bf16[32,40,256]{2,1,0:T(8,128)(2,1)} collective-permute-done((bf16[32,40,256]{2,1,0:T(8,128)(2,1)S(1)}, bf16[32,40,256]{2,1,0:T(8,128)(2,1)}, u32[]{:S(2)}, u32[]{:S(2)}) %collective-permute-start.6) | collective-permute-done | bytes 655392 | tf_op jit(solution)/shard_map/ppermute | solution.py:175
  89.7 0.0 copy-done
  89.7 0.0 copy-done.4
  89.7 0.0 copy-done.11
  89.7 0.0 copy-done.15
  89.7 0.0 copy-start.6
  89.7 0.9 copy-done.6
  90.6 0.0 copy-start.12
  90.6 0.9 copy-done.12
  91.5 0.0 copy-start.13
  91.5 0.9 copy-done.13
  92.4 0.0 copy-start.19
  92.4 0.7 copy-done.19
  93.1 5.0 %top_level.1 = bf16[1,2,2,128,256]{4,3,2,1,0:T(8,128)(2,1)} custom-call(s32[2,2]{1,0:T(2,128)S(1)} %copy-done.15, s32[20,4]{1,0:T(8,128)S(1)} %copy.18.top_nbr, bf16[32,40,256]{2,1,0:T(8,128)(2,1)S(1)} %all_to_all.11.mine, bf16[32,40,256]{2,1,0:T(8,128)(2,1)} %collective-permute-done.6.other, bf16[512,256]{1,0:T(8,128)(2,1)S(1)} %copy-done.6, ...), custom_call_target="tpu_custom_call" | custom-call | tf_op jit(solution)/shard_map/top_level/pallas_call | solution.py:176
  (4 shorter events, 0.1 us)
Async XLA Ops:
  0.0 60.0 %copy-start.18 = (f32[256]{0:T(256)S(1)}, f32[256]{0:T(256)}, u32[]{:S(2)}) copy-start(f32[256]{0:T(256)} %param.32) | copy-start | bytes 3076
  1.0 13.8 %collective-permute-start.1 = (bf16[1,1,2,128,256]{4,3,2,1,0:T(8,128)(2,1)S(1)}, bf16[1,1,2,128,256]{4,3,2,1,0:T(8,128)(2,1)S(1)}, u32[]{:S(2)}, u32[]{:S(2)}) collective-permute-start(bf16[1,1,2,128,256]{4,3,2,1,0:T(8,128)(2,1)S(1)} %get-tuple-element.11), channel_id=1, source_target_pairs={{8,0},{16,8},{24,16},{32,24},{40,32},{48,40},{56,48},{9,1},{17,9},... | collective-permute-start | bytes 393224 | tf_op jit(solution)/shard_map/ppermute | solution.py:145
  2.3 12.5 %collective-permute-start = (bf16[1,1,2,128,256]{4,3,2,1,0:T(8,128)(2,1)S(1)}, bf16[1,1,2,128,256]{4,3,2,1,0:T(8,128)(2,1)S(1)}, u32[]{:S(2)}, u32[]{:S(2)}) collective-permute-start(bf16[1,1,2,128,256]{4,3,2,1,0:T(8,128)(2,1)S(1)} %get-tuple-element.12), channel_id=1, source_target_pairs={{0,8},{8,16},{16,24},{24,32},{32,40},{40,48},{48,56},{1,9},{9,17},... | collective-permute-start | bytes 393224 | tf_op jit(solution)/shard_map/ppermute | solution.py:144
  8.8 7.6 %collective-permute-start.3 = (bf16[1,2,1,128,256]{4,3,2,1,0:T(8,128)(2,1)S(1)}, bf16[1,2,1,128,256]{4,3,2,1,0:T(8,128)(2,1)S(1)}, u32[]{:S(2)}, u32[]{:S(2)}) collective-permute-start(bf16[1,2,1,128,256]{4,3,2,1,0:T(8,128)(2,1)S(1)} %get-tuple-element.9), channel_id=1, source_target_pairs={{1,0},{2,1},{3,2},{4,3},{5,4},{6,5},{7,6},{0,7},{9,8},{10,9},{11,1... | collective-permute-start | bytes 393224 | tf_op jit(solution)/shard_map/ppermute | solution.py:147
  14.8 2.0 %collective-permute-start.2 = (bf16[1,2,1,128,256]{4,3,2,1,0:T(8,128)(2,1)S(1)}, bf16[1,2,1,128,256]{4,3,2,1,0:T(8,128)(2,1)S(1)}, u32[]{:S(2)}, u32[]{:S(2)}) collective-permute-start(bf16[1,2,1,128,256]{4,3,2,1,0:T(8,128)(2,1)S(1)} %get-tuple-element.10), channel_id=1, source_target_pairs={{0,1},{1,2},{2,3},{3,4},{4,5},{5,6},{6,7},{7,0},{8,9},{9,10},{10,1... | collective-permute-start | bytes 393224 | tf_op jit(solution)/shard_map/ppermute | solution.py:146
  14.8 3.2 %collective-permute-start.4 = (bf16[2,128,256]{2,1,0:T(8,128)(2,1)S(1)}, bf16[2,128,256]{2,1,0:T(8,128)(2,1)S(1)}, u32[]{:S(2)}, u32[]{:S(2)}) collective-permute-start(bf16[2,128,256]{2,1,0:T(8,128)(2,1)S(1)} %pad_maximum_fusion), channel_id=1, source_target_pairs={{0,1},{1,2},{2,3},{3,4},{4,5},{5,6},{6,7},{7,0},{8,9},{9,10},{10,1... | collective-permute-start | bytes 393224 | tf_op jit(solution)/shard_map/ppermute | solution.py:148
  14.9 4.7 %collective-permute-start.5 = (bf16[2,128,256]{2,1,0:T(8,128)(2,1)S(1)}, bf16[2,128,256]{2,1,0:T(8,128)(2,1)S(1)}, u32[]{:S(2)}, u32[]{:S(2)}) collective-permute-start(bf16[2,128,256]{2,1,0:T(8,128)(2,1)S(1)} %pad_maximum_fusion.1), channel_id=1, source_target_pairs={{1,0},{2,1},{3,2},{4,3},{5,4},{6,5},{7,6},{0,7},{9,8},{10,9},{11,1... | collective-permute-start | bytes 393224 | tf_op jit(solution)/shard_map/ppermute | solution.py:149
  19.6 1.0 copy-start.1
  20.5 1.0 %copy-start.2 = (bf16[2,2,4,128,128]{4,3,2,1,0:T(8,128)(2,1)S(1)}, bf16[2,2,4,128,128]{4,3,2,1,0:T(8,128)(2,1)}, u32[]{:S(2)}) copy-start(bf16[2,2,4,128,128]{4,3,2,1,0:T(8,128)(2,1)} %adj.1) | copy-start | bytes 1572868
  21.6 0.9 copy-start.3
  22.5 0.9 copy-start.7
  23.4 0.9 copy-start.8
  24.3 0.9 copy-start.9
  25.2 0.9 copy-start.10
  26.1 0.7 copy-start.14
  26.8 0.7 copy-start.16
  27.4 0.7 copy-start.17
  28.1 61.5 %copy-start = (bf16[20,4,128,128]{3,2,1,0:T(8,128)(2,1)S(1)}, bf16[20,4,128,128]{3,2,1,0:T(8,128)(2,1)}, u32[]{:S(2)}) copy-start(bf16[20,4,128,128]{3,2,1,0:T(8,128)(2,1)} %top_adj.1) | copy-start | bytes 7864324
  28.1 61.5 %copy-start.4 = (bf16[2,2,128,128]{3,2,1,0:T(8,128)(2,1)S(1)}, bf16[2,2,128,128]{3,2,1,0:T(8,128)(2,1)}, u32[]{:S(2)}) copy-start(bf16[2,2,128,128]{3,2,1,0:T(8,128)(2,1)} %tiles.3) | copy-start | bytes 393220
  28.1 61.5 %copy-start.11 = (bf16[256,256]{1,0:T(8,128)(2,1)S(1)}, bf16[256,256]{1,0:T(8,128)(2,1)}, u32[]{:S(2)}) copy-start(bf16[256,256]{1,0:T(8,128)(2,1)} %w_msg.3) | copy-start | bytes 393220
  28.1 61.5 %copy-start.15 = (s32[2,2]{1,0:T(2,128)S(1)}, s32[2,2]{1,0:T(2,128)}, u32[]{:S(2)}) copy-start(s32[2,2]{1,0:T(2,128)} %up_map.3) | copy-start | bytes 52
  30.3 53.2 %copy-start.5 = (bf16[512,256]{1,0:T(8,128)(2,1)}, bf16[512,256]{1,0:T(8,128)(2,1)S(1)}, u32[]{:S(2)}) copy-start(bf16[512,256]{1,0:T(8,128)(2,1)S(1)} %get-tuple-element.8.fine) | copy-start | bytes 786436
  83.5 6.2 %collective-permute-start.6 = (bf16[32,40,256]{2,1,0:T(8,128)(2,1)S(1)}, bf16[32,40,256]{2,1,0:T(8,128)(2,1)}, u32[]{:S(2)}, u32[]{:S(2)}) collective-permute-start(bf16[32,40,256]{2,1,0:T(8,128)(2,1)S(1)} %all_to_all.11.mine), channel_id=1, source_target_pairs={{0,1},{1,0},{2,3},{3,2},{4,5},{5,4},{6,7},{7,6},{8,9},{9,8},{10,11... | collective-permute-start | bytes 1966088 | tf_op jit(solution)/shard_map/ppermute | solution.py:175
  89.7 1.0 copy-start.6
  90.6 0.9 copy-start.12
  91.5 0.9 copy-start.13
  92.4 0.7 copy-start.19

commit v2 on v1

v2 whole, which is shorter than its diff:
```python
import functools

import jax
import jax.numpy as jnp
from jax import lax
from jax.experimental import pallas as pl
from jax.experimental.pallas import tpu as pltpu
from jax.sharding import Mesh, PartitionSpec as P

F32 = jnp.float32
BF16 = jnp.bfloat16
VMEM = pl.BlockSpec(memory_space=pltpu.VMEM)
HBM = pl.BlockSpec(memory_space=pltpu.HBM)
MIB = 1024 * 1024


def dot(a, b):
    return lax.dot_general(a, b, (((1,), (0,)), ((), ())), preferred_element_type=F32)


def dot_t(a, b):
    return lax.dot_general(a, b, (((0,), (0,)), ((), ())), preferred_element_type=F32)


def norm(values, gain):
    center = values - jnp.mean(values, -1, keepdims=True)
    spread = jnp.mean(center * center, -1, keepdims=True)
    return center * lax.rsqrt(spread + 1e-05) * gain


def far(array):
    return pltpu.with_memory_space_constraint(array, pltpu.HBM)


def start_all(pairs, sems):
    copies = [pltpu.make_async_copy(src, dst, sems.at[n]) for n, (src, dst) in enumerate(pairs)]
    for copy in copies:
        copy.start()
    return copies


def cut_kernel(state, last_row, first_row, last_col, first_col, sems):
    pairs = [
        (state.at[:, 1:2], last_row),
        (state.at[:, 0:1], first_row),
        (state.at[:, :, 1:2], last_col),
        (state.at[:, :, 0:1], first_col),
    ]
    for copy in start_all(pairs, sems):
        copy.wait()


def stage_kernel(
    state_in, w_self_in, nbr_in, map_in, adj_in, tiles_in, w_msg_in, w_agg_in, w_out_in, gain_in,
    state, own_part, nbr, up_map, adj, tiles, w_msg, w_agg, w_out, gain, w_self, sems,
):
    pairs = [
        (state_in, state), (w_self_in, w_self), (nbr_in, nbr), (map_in, up_map), (adj_in, adj),
        (tiles_in, tiles), (w_msg_in, w_msg), (w_agg_in, w_agg), (w_out_in, w_out),
        (gain_in, gain),
    ]
    copies = start_all(pairs, sems)
    copies[0].wait()
    copies[1].wait()
    own = jnp.concatenate([state[0, b // 2, b % 2] for b in range(4)], axis=0)
    own_part[...] = dot(own, w_self[...])
    for copy in copies[2:]:
        copy.wait()


def fine_kernel(
    up, down, left, right, corner_l, corner_r, state, own_part, nbr_in, map_in, adj, tiles,
    w_msg, w_agg, w_out, gain, fine_out, piece_out, frame, nbr, up_map, sems,
):
    copies = start_all([(nbr_in, nbr), (map_in, up_map)], sems)
    for c in range(2):
        frame[1 + c] = up[0, 0, c]
        frame[13 + c] = down[0, 0, c]
        for r in range(2):
            frame[(1 + r) * 4 + 1 + c] = state[0, r, c]
    for r in range(2):
        frame[(1 + r) * 4] = left[0, r, 0]
        frame[(1 + r) * 4 + 3] = right[0, r, 0]
        frame[12 * r] = corner_l[r]
        frame[12 * r + 3] = corner_r[r]
    for copy in copies:
        copy.wait()
    own, mixed = [], []
    for y in range(2):
        for x in range(2):
            picked = []
            for k in range(4):
                code = nbr[y, x, k]
                spot = (y + lax.div(code, 3)) * 4 + x + lax.rem(code, 3)
                picked.append(frame[spot])
            edges = jnp.concatenate([adj[y, x, k] for k in range(4)], axis=1)
            mixed.append(dot(edges, jnp.concatenate(picked, axis=0)).astype(BF16))
            own.append(frame[(1 + y) * 4 + 1 + x])
    own = jnp.concatenate(own, axis=0)
    mixed = jnp.concatenate(mixed, axis=0)
    agg = dot(mixed, w_msg[...]).astype(BF16)
    hidden = jax.nn.silu(own_part[...] + dot(agg, w_agg[...])).astype(BF16)
    fine = norm(own.astype(F32) + dot(hidden, w_out[...]), gain[...]).astype(BF16)
    fine_out[...] = fine
    contrib = [
        dot(tiles[b // 2, b % 2], fine[b * 128 : (b + 1) * 128]).astype(BF16) for b in range(4)
    ]
    row = lax.broadcasted_iota(jnp.int32, (128, 128), 0)
    col = lax.broadcasted_iota(jnp.int32, (128, 128), 1)
    dest = row >> 3
    want = ((row >> 1) & 3) * 32 + (dest & 1) * 16 + (dest >> 1) * 2 + (row & 1)
    order = jnp.where(col == want, 1.0, 0.0).astype(BF16)
    piece = []
    for g in range(4):
        spots = [(b, 64 * core + 16 * g) for b in range(4) for core in range(2)]
        rows = jnp.concatenate([contrib[b][at : at + 16] for b, at in spots], axis=0)
        piece.append(dot(order, rows))
    piece = jnp.concatenate(piece, axis=0).reshape(64, 8, 256)
    line = lax.broadcasted_iota(jnp.int32, (64, 8, 128), 1) >> 1
    label = jnp.where(
        line < 2,
        jnp.where(line == 0, up_map[0, 0], up_map[0, 1]),
        jnp.where(line == 2, up_map[1, 0], up_map[1, 1]),
    ).astype(F32)
    parts = [piece[:, :, :128], piece[:, :, 128:], label]
    piece_out[...] = jnp.concatenate(parts, axis=1).astype(BF16)


def sum_kernel(got, gain, share_out):
    wide = got[...].astype(F32)
    values = jnp.concatenate([wide[:, :8], wide[:, 8:16]], axis=2).reshape(512, 256).astype(BF16)
    label = wide[:, 16:].reshape(512, 128).astype(jnp.int32)
    row = lax.broadcasted_iota(jnp.int32, (512, 128), 0)
    col = lax.broadcasted_iota(jnp.int32, (512, 128), 1)
    member = jnp.where((label * 2 + (row & 1)) == col, 1.0, 0.0).astype(BF16)
    total = dot_t(member, values)[:40]
    share = norm(total, gain[...]).astype(BF16)
    share_out[...] = jnp.broadcast_to(share[None], share_out.shape)


def spread_rows(source, top):
    row = lax.broadcasted_iota(jnp.int32, (160, 160), 0)
    col = lax.broadcasted_iota(jnp.int32, (160, 160), 1)
    want = ((row & 7) >> 1) * 40 + (row >> 3) * 2 + (row & 1)
    order = jnp.where(col == want, 1.0, 0.0).astype(BF16)
    for g in range(4):
        moved = [
            dot(order, source[8 * g + 4 * h : 8 * g + 4 * h + 4].reshape(160, 256))
            for h in range(2)
        ]
        moved = jnp.concatenate([part.reshape(20, 8, 256) for part in moved], axis=1)
        top[:, 16 * g : 16 * g + 16, :] = moved.astype(BF16)


def gather_parts(up_map, top_nbr, edges, top):
    mixed = []
    for b in range(4):
        at = up_map[b // 2, b % 2]
        picked = jnp.concatenate([top[top_nbr[k, at]] for k in range(4)], axis=0)
        mixed.append(dot(edges[b], picked))
    return jnp.concatenate(mixed, axis=0)


def half_kernel(
    map_in, nbr_in, mine, adj_in, fine_in, tiles_in, w_msg_in, w_agg_in, w_down_in, gain_in,
    edges, mixed, chosen, fine, tiles, w_msg, w_agg, w_down, gain,
    top, near, adj, up_map, top_nbr, sems, *, core_axis,
):
    first = start_all([(map_in, up_map), (nbr_in, top_nbr)], sems)
    rest = [
        (fine_in, fine), (tiles_in, tiles), (w_msg_in, w_msg), (w_agg_in, w_agg),
        (w_down_in, w_down), (gain_in, gain),
    ]
    rest = start_all(rest, sems.at[pl.ds(6, 6)])
    for copy in first:
        copy.wait()
    pairs = [(adj_in.at[up_map[b // 2, b % 2]], adj.at[b]) for b in range(4)]
    copies = start_all(pairs, sems.at[pl.ds(2, 4)])
    spread_rows(mine, top)
    core = lax.axis_index(core_axis)
    for b in range(4):
        copies[b].wait()
        low = jnp.concatenate([adj[b, k][:, :64] for k in range(4)], axis=1)
        high = jnp.concatenate([adj[b, k][:, 64:] for k in range(4)], axis=1)
        near[b] = jnp.where(core == 0, low, high)
        edges[b] = jnp.where(core == 0, high, low)
        chosen[b] = top[up_map[b // 2, b % 2]]
    mixed[...] = gather_parts(up_map, top_nbr, near, top)
    for copy in rest:
        copy.wait()


def top_kernel(
    map_in, nbr_in, other, edges, mixed, chosen, fine, tiles, w_msg, w_agg, w_down, gain,
    out, top, whole, up_map, top_nbr, sems, *, core_axis,
):
    copies = start_all([(map_in, up_map), (nbr_in, top_nbr)], sems)
    spread_rows(other, top)
    for copy in copies:
        copy.wait()
    core = lax.axis_index(core_axis)
    here = pl.ds(pl.multiple_of(core * 64, 64), 64)
    there = pl.ds(pl.multiple_of((1 - core) * 64, 64), 64)
    for b in range(4):
        whole[b, here, :] = chosen[b]
        whole[b, there, :] = top[up_map[b // 2, b % 2]]
    both = mixed[...] + gather_parts(up_map, top_nbr, edges, top)
    tagg = dot(both.astype(BF16), w_msg[...]).astype(BF16)
    zero = jnp.concatenate([whole[b] for b in range(4)], axis=0).astype(F32)
    one = (zero + jax.nn.silu(dot(tagg, w_agg[...]))).astype(BF16)
    lower = [
        dot_t(tiles[b // 2, b % 2], one[b * 128 : (b + 1) * 128]).astype(BF16) for b in range(4)
    ]
    lower = jnp.concatenate(lower, axis=0)
    final = norm(fine[...].astype(F32) + dot(lower, w_down[...]), gain[...]).astype(BF16)
    out[...] = final.reshape(1, 2, 2, 128, 256)


def call(body, ins, outs, scratch, name, busy=0, limit=24):
    return pl.pallas_call(
        body,
        out_shape=tuple(jax.ShapeDtypeStruct(shape, kind) for shape, kind in outs),
        in_specs=ins,
        out_specs=(VMEM,) * len(outs),
        scratch_shapes=scratch,
        compiler_params=pltpu.CompilerParams(vmem_limit_bytes=limit * MIB),
        cost_estimate=pl.CostEstimate(flops=0, bytes_accessed=busy, transcendentals=0),
        name=name,
    )


def local(
    fine_state, fine_adj, fine_nbr, up_map, up_tiles, top_adj, top_nbr, w_fine_msg, w_fine_self,
    w_fine_agg, w_fine_out, w_top_msg, w_top_agg, w_down, fine_gain, top_gain, out_gain,
):
    sx = ("x", "core")
    rows, cols = lax.axis_size("sy"), lax.axis_size("x") * lax.axis_size("core")
    east = [(i, (i + 1) % cols) for i in range(cols)]
    west = [(j, i) for i, j in east]
    south = [(i, i + 1) for i in range(rows - 1)]
    north = [(j, i) for i, j in south]
    weight = ((256, 256), BF16)
    tile_set = ((2, 2, 128, 128), BF16)
    part = ((512, 256), F32)
    gain = ((1, 256), F32)
    row_cut, col_cut = ((1, 1, 2, 128, 256), BF16), ((1, 2, 1, 128, 256), BF16)
    dma = pltpu.SemaphoreType.DMA
    last_row, first_row, last_col, first_col = call(
        cut_kernel, [HBM], [row_cut, row_cut, col_cut, col_cut], [dma((4,))], "cut", 1 << 20
    )(far(fine_state))
    up = lax.ppermute(last_row, "sy", south)
    down = lax.ppermute(first_row, "sy", north)
    left = lax.ppermute(last_col, sx, east)
    right = lax.ppermute(first_col, sx, west)
    corner_l = lax.ppermute(jnp.concatenate([up[0, :, 1], down[0, :, 1]]), sx, east)
    corner_r = lax.ppermute(jnp.concatenate([up[0, :, 0], down[0, :, 0]]), sx, west)
    staged = [
        fine_nbr, up_map, fine_adj, up_tiles, w_fine_msg, w_fine_agg, w_fine_out, fine_gain[None],
    ]
    held = call(
        stage_kernel,
        [HBM] * 10,
        [(fine_state.shape, BF16), part] + [(array.shape, array.dtype) for array in staged],
        [pltpu.VMEM(*weight), dma((10,))],
        "stage",
        1 << 23,
    )(*[far(array) for array in [fine_state, w_fine_self] + staged])
    fine, piece = call(
        fine_kernel,
        [VMEM] * 16,
        [((512, 256), BF16), ((64, 24, 128), BF16)],
        [
            pltpu.VMEM((16, 128, 256), BF16), pltpu.SMEM((2, 2, 4), jnp.int32),
            pltpu.SMEM((2, 2), jnp.int32), dma((2,)),
        ],
        "fine_level",
        1 << 23,
    )(up, down, left, right, corner_l, corner_r, *held)
    got = lax.all_to_all(piece, ("sy", "x", "core"), 0, 0)
    (share,) = call(
        sum_kernel, [VMEM] * 2, [((32, 40, 256), BF16)], [], "top_sum", 1 << 20
    )(got, top_gain[None])
    mine = lax.all_to_all(share, ("sy", "x"), 0, 0)
    other = lax.ppermute(mine, "core", [(0, 1), (1, 0)])
    tables = [pltpu.SMEM((2, 2), jnp.int32), pltpu.SMEM((4, 20), jnp.int32)]
    top = pltpu.VMEM((20, 64, 256), BF16)
    half_set = ((4, 128, 256), BF16)
    half = call(
        functools.partial(half_kernel, core_axis="core"),
        [HBM] * 2 + [VMEM] + [HBM] * 7,
        [
            half_set, part, ((4, 64, 256), BF16), ((512, 256), BF16), tile_set, weight, weight, weight, gain,
        ],
        [top, pltpu.VMEM(*half_set), pltpu.VMEM((4, 4, 128, 128), BF16)] + tables + [dma((12,))],
        "top_half",
        1 << 23,
    )(
        up_map, top_nbr.T, mine, top_adj, fine, up_tiles, w_top_msg, w_top_agg, w_down,
        out_gain[None],
    )
    (out,) = call(
        functools.partial(top_kernel, core_axis="core"),
        [HBM] * 2 + [VMEM] * 10,
        [(fine_state.shape, BF16)],
        [top, pltpu.VMEM(*half_set)] + tables + [dma((2,))],
        "top_level",
        1 << 23,
    )(up_map, top_nbr.T, other, *half)
    return out


def solution(mesh):
    shape = dict(mesh.shape)
    inner = Mesh(
        mesh.devices.reshape(shape["ens"], shape["sy"], shape["sx"] // 2, 2),
        ("ens", "sy", "x", "core"),
    )
    sx = ("x", "core")
    in_specs = (
        P("ens", "sy", sx, None, None),
        P("sy", sx, None, None, None),
        P("sy", sx, None),
        P("sy", sx),
        P("sy", sx, None, None),
    ) + (P(),) * 12
    out_specs = P("ens", "sy", sx, None, None)
    return jax.shard_map(local, mesh=inner, in_specs=in_specs, out_specs=out_specs, check_vma=False)
```

time: 98.8 us -> 81.8 us (0.83)
  local copies, waits for them, and re-layouts: 14.8 us -> 0.07 us
  blocking collectives: 52.7 us -> 49.7 us
  Pallas kernels: 7.64 us -> 9.67 us
    unnamed x41 -> x18, local copies, waits for them, and re-layouts: 12.8 us -> 0.05 us
    ppermute x4, starting transfers between devices: 12.7 us -> 9.5 us  [the longest x1 4.83 us: local(): up = lax.ppermute(last_row, 'sy', south)]
    ppermute x1, starting transfers between devices: 0.02 us -> 3.2 us  [local(): lax.ppermute(jnp.concatenate([up[0, :, 1], down[0, :, 1]]), sx, east)]
    all_to_all x1, blocking collectives: 29.6 us -> 26.7 us  [local(): got = lax.all_to_all(piece, ('sy', 'x', 'core'), 0, 0)]
    pallas_call x3 -> x6, Pallas kernels: 7.64 us -> 9.67 us  [the longest x1 2.41 us: local(): call(functools.partial(half_kernel, core_axis='core'), [HBM] * 2 + [VMEM]...]
    slice x2 -> x0, local copies, waits for them, and re-layouts: 1.99 us -> none  [the longest x1 1 us: local(): down = lax.ppermute(fine_state[:, 0:1], 'sy', north)]
    ppermute x1, waiting for transfers between devices: 1.37 us -> 0.01 us  [local(): lax.ppermute(jnp.concatenate([up[0, :, 1], down[0, :, 1]]), sx, east)]
    ppermute x4, waiting for transfers between devices: 0.37 us -> 1.66 us  [the longest x1 1.65 us: local(): down = lax.ppermute(first_row, 'sy', north)]
  transfers between devices with their start and end apart: 7 -> 7, of which waited for: 4 -> 2; matrix products, arithmetic and copies ran while one was open for 2% -> 0% of each run, Pallas kernels for 0% -> 5%
where the time goes in v2:
time: 81.8 us; the launch traced here: 81.6 us
  blocking collectives  49.7 us (61%)
  starting transfers between devices  17.7 us (22%)
  Pallas kernels  9.67 us (12%)
  waiting for transfers between devices  4.19 us (5%)
    all_to_all x1, blocking collectives, local(): got = lax.all_to_all(piece, ('sy', 'x', 'core'), 0, 0)  26.7 us
    all_to_all x1, blocking collectives, local(): mine = lax.all_to_all(share, ('sy', 'x'), 0, 0)  23 us
    ppermute x1, starting transfers between devices, local(): up = lax.ppermute(last_row, 'sy', south)  4.83 us
    ppermute x1, starting transfers between devices, local(): other = lax.ppermute(mine, 'core', [(0, 1), (1, 0)])  4.31 us
    ppermute x1, starting transfers between devices, local(): lax.ppermute(jnp.concatenate([up[0, :, 1], down[0, :, 1]]), sx, east)  3.2 us
    ppermute x1, waiting for transfers between devices, local(): lax.ppermute(jnp.concatenate([up[0, :, 0], down[0, :, 0]]), sx, west)  2.52 us
    pallas_call x1, Pallas kernels, local(): call(functools.partial(half_kernel, core_axis='core'), [HBM] * 2 + [VMEM]...  2.41 us
    pallas_call x1, Pallas kernels, local(): call(functools.partial(top_kernel, core_axis='core'), [HBM] * 2 + [VMEM]...  2.38 us
  transfers between devices with their start and end apart: 7, of which 2 were waited for; matrix products, arithmetic and copies ran while one was open for 0% of the time, Pallas kernels for 5%

profile of v2, /device:TPU:1, one launch (start us, length us, event | category | flops | bytes accessed | tf_op | source)
XLA Modules:
  0.0 81.6 jit_solution(4056512262124326570)
XLA Ops:
  0.0 1.1 %cut.1 = (bf16[1,1,2,128,256]{4,3,2,1,0:T(8,128)(2,1)S(1)}, bf16[1,1,2,128,256]{4,3,2,1,0:T(8,128)(2,1)S(1)}, bf16[1,2,1,128,256]{4,3,2,1,0:T(8,128)(2,1)S(1)}, bf16[1,2,1,128,256]{4,3,2,1,0:T(8,128)(2,1)S(1)}) custom-call(bf16[1,2,2,128,256]{4,3,2,1,0:T(8,128)(2,1)} %state_in.1), custom_call_target="tpu_custom_call" | custom-call | bytes 1048576 | tf_op jit(solution)/shard_map/cut/pallas_call | solution.py:248
  1.1 4.8 %collective-permute-start = (bf16[1,1,2,128,256]{4,3,2,1,0:T(8,128)(2,1)S(1)}, bf16[1,1,2,128,256]{4,3,2,1,0:T(8,128)(2,1)S(1)}, u32[]{:S(2)}, u32[]{:S(2)}) collective-permute-start(bf16[1,1,2,128,256]{4,3,2,1,0:T(8,128)(2,1)S(1)} %get-tuple-element.30), channel_id=1, source_target_pairs={{0,8},{8,16},{16,24},{24,32},{32,40},{40,48},{48,56},{1,9},{9,17},... | collective-permute-start | bytes 393224 | tf_op jit(solution)/shard_map/ppermute | solution.py:251
  6.0 1.3 %collective-permute-start.1 = (bf16[1,1,2,128,256]{4,3,2,1,0:T(8,128)(2,1)S(1)}, bf16[1,1,2,128,256]{4,3,2,1,0:T(8,128)(2,1)S(1)}, u32[]{:S(2)}, u32[]{:S(2)}) collective-permute-start(bf16[1,1,2,128,256]{4,3,2,1,0:T(8,128)(2,1)S(1)} %get-tuple-element.31), channel_id=1, source_target_pairs={{8,0},{16,8},{24,16},{32,24},{40,32},{48,40},{56,48},{9,1},{17,9},... | collective-permute-start | bytes 393224 | tf_op jit(solution)/shard_map/ppermute | solution.py:252
  7.3 2.1 %collective-permute-start.2 = (bf16[1,2,1,128,256]{4,3,2,1,0:T(8,128)(2,1)S(1)}, bf16[1,2,1,128,256]{4,3,2,1,0:T(8,128)(2,1)S(1)}, u32[]{:S(2)}, u32[]{:S(2)}) collective-permute-start(bf16[1,2,1,128,256]{4,3,2,1,0:T(8,128)(2,1)S(1)} %get-tuple-element.32), channel_id=1, source_target_pairs={{0,1},{1,2},{2,3},{3,4},{4,5},{5,6},{6,7},{7,0},{8,9},{9,10},{10,1... | collective-permute-start | bytes 393224 | tf_op jit(solution)/shard_map/ppermute | solution.py:253
  9.3 1.3 %collective-permute-start.3 = (bf16[1,2,1,128,256]{4,3,2,1,0:T(8,128)(2,1)S(1)}, bf16[1,2,1,128,256]{4,3,2,1,0:T(8,128)(2,1)S(1)}, u32[]{:S(2)}, u32[]{:S(2)}) collective-permute-start(bf16[1,2,1,128,256]{4,3,2,1,0:T(8,128)(2,1)S(1)} %get-tuple-element.33), channel_id=1, source_target_pairs={{1,0},{2,1},{3,2},{4,3},{5,4},{6,5},{7,6},{0,7},{9,8},{10,9},{11,1... | collective-permute-start | bytes 393224 | tf_op jit(solution)/shard_map/ppermute | solution.py:254
  10.7 0.0 collective-permute-done.up
  10.7 1.7 %collective-permute-done.1.down = bf16[1,1,2,128,256]{4,3,2,1,0:T(8,128)(2,1)S(1)} collective-permute-done((bf16[1,1,2,128,256]{4,3,2,1,0:T(8,128)(2,1)S(1)}, bf16[1,1,2,128,256]{4,3,2,1,0:T(8,128)(2,1)S(1)}, u32[]{:S(2)}, u32[]{:S(2)}) %collective-permute-start.1) | collective-permute-done | bytes 131104 | tf_op jit(solution)/shard_map/ppermute | solution.py:252
  12.4 0.0 copy-start.7
  12.4 3.2 %collective-permute-start.4 = (bf16[2,128,256]{2,1,0:T(8,128)(2,1)S(1)}, bf16[2,128,256]{2,1,0:T(8,128)(2,1)S(1)}, u32[]{:S(2)}, u32[]{:S(2)}) collective-permute-start(bf16[2,128,256]{2,1,0:T(8,128)(2,1)S(1)} %pad_maximum_fusion), channel_id=1, source_target_pairs={{0,1},{1,2},{2,3},{3,4},{4,5},{5,6},{6,7},{7,0},{8,9},{9,10},{10,1... | collective-permute-start | bytes 393224 | tf_op jit(solution)/shard_map/ppermute | solution.py:255
  15.6 0.7 collective-permute-start.5
  16.3 1.4 %stage.1 = (bf16[1,2,2,128,256]{4,3,2,1,0:T(8,128)(2,1)S(1)}, f32[512,256]{1,0:T(8,128)S(1)}, s32[2,2,4]{2,1,0:T(2,128)S(1)}, s32[2,2]{1,0:T(2,128)S(1)}, bf16[2...) custom-call(bf16[1,2,2,128,256]{4,3,2,1,0:T(8,128)(2,1)} %state_in.1, ...), custom_call_target="tpu_custom_call" | custom-call | bytes 8388608 | tf_op jit(solution)/shard_map/stage/pallas_call | solution.py:260
  17.7 0.0 collective-permute-done.2.left
  17.7 0.0 collective-permute-done.3.right
  17.8 0.0 collective-permute-done.4.corner_l
  17.8 2.5 %collective-permute-done.5.corner_r = bf16[2,128,256]{2,1,0:T(8,128)(2,1)S(1)} collective-permute-done((bf16[2,128,256]{2,1,0:T(8,128)(2,1)S(1)}, bf16[2,128,256]{2,1,0:T(8,128)(2,1)S(1)}, u32[]{:S(2)}, u32[]{:S(2)}) %collective-permute-start.5) | collective-permute-done | bytes 131104 | tf_op jit(solution)/shard_map/ppermute | solution.py:256
  20.3 0.0 copy-start
  20.3 0.0 copy-start.1
  20.3 0.0 copy-start.2
  20.3 0.0 copy-start.3
  20.3 0.0 copy-start.4
  20.3 0.0 copy-start.5
  20.3 0.0 copy-start.6
  20.3 0.0 copy-start.8
  20.3 1.9 %fine_level.1 = (bf16[512,256]{1,0:T(8,128)(2,1)S(1)}, bf16[64,24,128]{2,1,0:T(8,128)(2,1)S(1)}) custom-call(bf16[1,1,2,128,256]{4,3,2,1,0:T(8,128)(2,1)S(1)} %collective-permute-done.up, bf16[1,1,2,128,256]{4,3,2,1,0:T(8,128)(2,1)S(1)} %collective-permute-done.1.down, bf16[1,2,1,128,256]{4,3,2,1,0:T(8,128)(2,1)S(1)} %collective-permute-done.2.left, ...), custom_call_target="tpu_custom_call" | custom-call | bytes 8388608 | tf_op jit(solution)/shard_map/fine_level/pallas_call | solution.py:268
  22.2 26.7 %all_to_all.10.got = bf16[64,24,128]{2,1,0:T(8,128)(2,1)S(1)} all-to-all(bf16[64,24,128]{2,1,0:T(8,128)(2,1)S(1)} %get-tuple-element.44), channel_id=1, replica_groups=mesh['ens'=8,'sy'=8,'x'=4,'core'=2] {'sy','x','core'}, dimensions={0} | all-to-all | bytes 786432 | tf_op jit(solution)/shard_map/all_to_all | solution.py:279
  48.9 0.0 copy-done.7
  48.9 0.4 top_sum.1
  49.4 23.0 %all_to_all.11.mine = bf16[32,40,256]{2,1,0:T(8,128)(2,1)S(1)} all-to-all(bf16[32,40,256]{2,1,0:T(8,128)(2,1)S(1)} %top_sum.1), channel_id=1, replica_groups=mesh['ens'=8,'sy'=8,'x'=4,'core'=2] {'sy','x'}, dimensions={0} | all-to-all | bytes 1310720 | tf_op jit(solution)/shard_map/all_to_all | solution.py:283
  72.3 4.3 %collective-permute-start.6 = (bf16[32,40,256]{2,1,0:T(8,128)(2,1)S(1)}, bf16[32,40,256]{2,1,0:T(8,128)(2,1)S(1)}, u32[]{:S(2)}, u32[]{:S(2)}) collective-permute-start(bf16[32,40,256]{2,1,0:T(8,128)(2,1)S(1)} %all_to_all.11.mine), channel_id=1, source_target_pairs={{0,1},{1,0},{2,3},{3,2},{4,5},{5,4},{6,7},{7,6},{8,9},{9,8},{10,11... | collective-permute-start | bytes 1966088 | tf_op jit(solution)/shard_map/ppermute | solution.py:284
  76.7 0.0 copy-done
  76.7 0.0 copy-done.1
  76.7 0.0 copy-done.2
  76.7 0.0 copy-done.3
  76.7 0.0 copy-done.4
  76.7 0.0 copy-done.5
  76.7 0.0 copy-done.6
  76.7 0.0 copy-done.8
  76.7 2.4 %top_half.1 = (bf16[4,128,256]{2,1,0:T(8,128)(2,1)S(1)}, f32[512,256]{1,0:T(8,128)S(1)}, bf16[4,64,256]{2,1,0:T(8,128)(2,1)S(1)}, bf16[512,256]{1,0:T(8,128)(2,1...) custom-call(s32[2,2]{1,0:T(2,128)S(1)} %copy-done.5, ...), custom_call_target="tpu_custom_call" | custom-call | bytes 8388608 | tf_op jit(solution)/shard_map/top_half/pallas_call | solution.py:288
  79.2 0.0 collective-permute-done.6.other
  79.2 2.4 %top_level.1 = bf16[1,2,2,128,256]{4,3,2,1,0:T(8,128)(2,1)} custom-call(s32[2,2]{1,0:T(2,128)S(1)} %copy-done.5, s32[4,20]{1,0:T(4,128)S(1)} %bitcast.13, bf16[32,40,256]{2,1,0:T(8,128)(2,1)S(1)} %collective-permute-done.6.other, bf16[4,128,256]{2,1,0:T(8,128)(2,1)S(1)} %get-tuple-element.46.edges, f32[512,256]{1,0:T(8,128)S(1)} %get-tuple-element.47.mixed, ...), custom_call_target="tpu_custom_call" | custom-call | bytes 8388608 | tf_op jit(solution)/shard_map/top_level/pallas_call | solution.py:301
  (4 shorter events, 0.0 us)
Async XLA Ops:
  1.1 9.5 %collective-permute-start = (bf16[1,1,2,128,256]{4,3,2,1,0:T(8,128)(2,1)S(1)}, bf16[1,1,2,128,256]{4,3,2,1,0:T(8,128)(2,1)S(1)}, u32[]{:S(2)}, u32[]{:S(2)}) collective-permute-start(bf16[1,1,2,128,256]{4,3,2,1,0:T(8,128)(2,1)S(1)} %get-tuple-element.30), channel_id=1, source_target_pairs={{0,8},{8,16},{16,24},{24,32},{32,40},{40,48},{48,56},{1,9},{9,17},... | collective-permute-start | bytes 393224 | tf_op jit(solution)/shard_map/ppermute | solution.py:251
  6.0 6.3 %collective-permute-start.1 = (bf16[1,1,2,128,256]{4,3,2,1,0:T(8,128)(2,1)S(1)}, bf16[1,1,2,128,256]{4,3,2,1,0:T(8,128)(2,1)S(1)}, u32[]{:S(2)}, u32[]{:S(2)}) collective-permute-start(bf16[1,1,2,128,256]{4,3,2,1,0:T(8,128)(2,1)S(1)} %get-tuple-element.31), channel_id=1, source_target_pairs={{8,0},{16,8},{24,16},{32,24},{40,32},{48,40},{56,48},{9,1},{17,9},... | collective-permute-start | bytes 393224 | tf_op jit(solution)/shard_map/ppermute | solution.py:252
  7.3 10.5 %collective-permute-start.2 = (bf16[1,2,1,128,256]{4,3,2,1,0:T(8,128)(2,1)S(1)}, bf16[1,2,1,128,256]{4,3,2,1,0:T(8,128)(2,1)S(1)}, u32[]{:S(2)}, u32[]{:S(2)}) collective-permute-start(bf16[1,2,1,128,256]{4,3,2,1,0:T(8,128)(2,1)S(1)} %get-tuple-element.32), channel_id=1, source_target_pairs={{0,1},{1,2},{2,3},{3,4},{4,5},{5,6},{6,7},{7,0},{8,9},{9,10},{10,1... | collective-permute-start | bytes 393224 | tf_op jit(solution)/shard_map/ppermute | solution.py:253
  9.3 8.4 %collective-permute-start.3 = (bf16[1,2,1,128,256]{4,3,2,1,0:T(8,128)(2,1)S(1)}, bf16[1,2,1,128,256]{4,3,2,1,0:T(8,128)(2,1)S(1)}, u32[]{:S(2)}, u32[]{:S(2)}) collective-permute-start(bf16[1,2,1,128,256]{4,3,2,1,0:T(8,128)(2,1)S(1)} %get-tuple-element.33), channel_id=1, source_target_pairs={{1,0},{2,1},{3,2},{4,3},{5,4},{6,5},{7,6},{0,7},{9,8},{10,9},{11,1... | collective-permute-start | bytes 393224 | tf_op jit(solution)/shard_map/ppermute | solution.py:254
  12.4 36.6 %copy-start.7 = (f32[256]{0:T(256)S(1)}, f32[256]{0:T(256)}, u32[]{:S(2)}) copy-start(f32[256]{0:T(256)} %param.32) | copy-start | bytes 3076
  12.4 5.4 %collective-permute-start.4 = (bf16[2,128,256]{2,1,0:T(8,128)(2,1)S(1)}, bf16[2,128,256]{2,1,0:T(8,128)(2,1)S(1)}, u32[]{:S(2)}, u32[]{:S(2)}) collective-permute-start(bf16[2,128,256]{2,1,0:T(8,128)(2,1)S(1)} %pad_maximum_fusion), channel_id=1, source_target_pairs={{0,1},{1,2},{2,3},{3,4},{4,5},{5,6},{6,7},{7,0},{8,9},{9,10},{10,1... | collective-permute-start | bytes 393224 | tf_op jit(solution)/shard_map/ppermute | solution.py:255
  15.6 4.7 %collective-permute-start.5 = (bf16[2,128,256]{2,1,0:T(8,128)(2,1)S(1)}, bf16[2,128,256]{2,1,0:T(8,128)(2,1)S(1)}, u32[]{:S(2)}, u32[]{:S(2)}) collective-permute-start(bf16[2,128,256]{2,1,0:T(8,128)(2,1)S(1)} %pad_maximum_fusion.1), channel_id=1, source_target_pairs={{1,0},{2,1},{3,2},{4,3},{5,4},{6,5},{7,6},{0,7},{9,8},{10,9},{11,1... | collective-permute-start | bytes 393224 | tf_op jit(solution)/shard_map/ppermute | solution.py:256
  20.3 56.4 %copy-start = (bf16[20,4,128,128]{3,2,1,0:T(8,128)(2,1)S(1)}, bf16[20,4,128,128]{3,2,1,0:T(8,128)(2,1)}, u32[]{:S(2)}) copy-start(bf16[20,4,128,128]{3,2,1,0:T(8,128)(2,1)} %adj_in.3) | copy-start | bytes 7864324
  20.3 56.4 %copy-start.1 = (bf16[2,2,128,128]{3,2,1,0:T(8,128)(2,1)S(1)}, bf16[2,2,128,128]{3,2,1,0:T(8,128)(2,1)}, u32[]{:S(2)}) copy-start(bf16[2,2,128,128]{3,2,1,0:T(8,128)(2,1)} %tiles_in.3) | copy-start | bytes 393220
  20.3 56.4 %copy-start.2 = (bf16[256,256]{1,0:T(8,128)(2,1)S(1)}, bf16[256,256]{1,0:T(8,128)(2,1)}, u32[]{:S(2)}) copy-start(bf16[256,256]{1,0:T(8,128)(2,1)} %w_msg_in.3) | copy-start | bytes 393220
  20.3 56.4 %copy-start.3 = (bf16[256,256]{1,0:T(8,128)(2,1)S(1)}, bf16[256,256]{1,0:T(8,128)(2,1)}, u32[]{:S(2)}) copy-start(bf16[256,256]{1,0:T(8,128)(2,1)} %w_agg_in.3) | copy-start | bytes 393220
  20.3 56.4 %copy-start.4 = (bf16[256,256]{1,0:T(8,128)(2,1)S(1)}, bf16[256,256]{1,0:T(8,128)(2,1)}, u32[]{:S(2)}) copy-start(bf16[256,256]{1,0:T(8,128)(2,1)} %w_down_in.1) | copy-start | bytes 393220
  20.3 56.4 %copy-start.5 = (s32[2,2]{1,0:T(2,128)S(1)}, s32[2,2]{1,0:T(2,128)}, u32[]{:S(2)}) copy-start(s32[2,2]{1,0:T(2,128)} %map_in.5) | copy-start | bytes 52
  20.3 56.4 %copy-start.6 = (s32[20,4]{0,1:T(4,128)S(1)}, s32[20,4]{0,1:T(4,128)}, u32[]{:S(2)}) copy-start(s32[20,4]{0,1:T(4,128)} %param.23) | copy-start | bytes 964
  20.3 56.4 %copy-start.8 = (f32[256]{0:T(256)S(1)}, f32[256]{0:T(256)}, u32[]{:S(2)}) copy-start(f32[256]{0:T(256)} %param.33) | copy-start | bytes 3076
  72.3 6.8 %collective-permute-start.6 = (bf16[32,40,256]{2,1,0:T(8,128)(2,1)S(1)}, bf16[32,40,256]{2,1,0:T(8,128)(2,1)S(1)}, u32[]{:S(2)}, u32[]{:S(2)}) collective-permute-start(bf16[32,40,256]{2,1,0:T(8,128)(2,1)S(1)} %all_to_all.11.mine), channel_id=1, source_target_pairs={{0,1},{1,0},{2,3},{3,2},{4,5},{5,4},{6,7},{7,6},{8,9},{9,8},{10,11... | collective-permute-start | bytes 1966088 | tf_op jit(solution)/shard_map/ppermute | solution.py:284

commit v3 on v2

--- a/solution.py
+++ b/solution.py
@@ -51,25 +51,39 @@
 
 
 def stage_kernel(
-    state_in, w_self_in, nbr_in, map_in, adj_in, tiles_in, w_msg_in, w_agg_in, w_out_in, gain_in,
-    state, own_part, nbr, up_map, adj, tiles, w_msg, w_agg, w_out, gain, w_self, sems,
+    state_in, w_self_in, map_in, nbr_in, adj_in, tiles_in, w_msg_in, w_agg_in, w_out_in, gain_in,
+    top_adj, state, own_part, up_map, nbr, adj, tiles, w_msg, w_agg, w_out, gain,
+    turned, near, away, w_self, table, edges, sems, *, core_axis,
 ):
+    first = pltpu.make_async_copy(map_in, table, sems.at[10])
+    first.start()
     pairs = [
-        (state_in, state), (w_self_in, w_self), (nbr_in, nbr), (map_in, up_map), (adj_in, adj),
+        (state_in, state), (w_self_in, w_self), (map_in, up_map), (nbr_in, nbr), (adj_in, adj),
         (tiles_in, tiles), (w_msg_in, w_msg), (w_agg_in, w_agg), (w_out_in, w_out),
         (gain_in, gain),
     ]
     copies = start_all(pairs, sems)
+    first.wait()
+    pairs = [(top_adj.at[table[b // 2, b % 2]], edges.at[b]) for b in range(4)]
+    edge_copies = start_all(pairs, sems.at[pl.ds(11, 4)])
     copies[0].wait()
     copies[1].wait()
     own = jnp.concatenate([state[0, b // 2, b % 2] for b in range(4)], axis=0)
     own_part[...] = dot(own, w_self[...])
     for copy in copies[2:]:
         copy.wait()
+    core = lax.axis_index(core_axis)
+    for b in range(4):
+        turned[b // 2, b % 2] = tiles[b // 2, b % 2].T
+        edge_copies[b].wait()
+        low = jnp.concatenate([edges[b, k][:, :64] for k in range(4)], axis=1)
+        high = jnp.concatenate([edges[b, k][:, 64:] for k in range(4)], axis=1)
+        near[b] = jnp.where(core == 0, low, high)
+        away[b] = jnp.where(core == 0, high, low)
 
 
 def fine_kernel(
-    up, down, left, right, corner_l, corner_r, state, own_part, nbr_in, map_in, adj, tiles,
+    up, down, left, right, corner_l, corner_r, state, own_part, map_in, nbr_in, adj, tiles,
     w_msg, w_agg, w_out, gain, fine_out, piece_out, frame, nbr, up_map, sems,
 ):
     copies = start_all([(nbr_in, nbr), (map_in, up_map)], sems)
@@ -81,8 +95,8 @@
     for r in range(2):
         frame[(1 + r) * 4] = left[0, r, 0]
         frame[(1 + r) * 4 + 3] = right[0, r, 0]
-        frame[12 * r] = corner_l[r]
-        frame[12 * r + 3] = corner_r[r]
+        frame[12 - 12 * r] = corner_l[r]
+        frame[15 - 12 * r] = corner_r[r]
     for copy in copies:
         copy.wait()
     own, mixed = [], []
@@ -138,90 +152,74 @@
     share_out[...] = jnp.broadcast_to(share[None], share_out.shape)
 
 
-def spread_rows(source, top):
+def order_kernel(got, out):
     row = lax.broadcasted_iota(jnp.int32, (160, 160), 0)
     col = lax.broadcasted_iota(jnp.int32, (160, 160), 1)
     want = ((row & 7) >> 1) * 40 + (row >> 3) * 2 + (row & 1)
     order = jnp.where(col == want, 1.0, 0.0).astype(BF16)
-    for g in range(4):
-        moved = [
-            dot(order, source[8 * g + 4 * h : 8 * g + 4 * h + 4].reshape(160, 256))
-            for h in range(2)
-        ]
-        moved = jnp.concatenate([part.reshape(20, 8, 256) for part in moved], axis=1)
-        top[:, 16 * g : 16 * g + 16, :] = moved.astype(BF16)
-
-
-def gather_parts(up_map, top_nbr, edges, top):
+    moved = [dot(order, got[4 * h : 4 * h + 4].reshape(160, 256)) for h in range(2)]
+    moved = jnp.concatenate([part.reshape(20, 8, 256) for part in moved], axis=1)
+    out[...] = jnp.broadcast_to(moved.astype(BF16)[None], out.shape)
+
+
+def half_block(source, at):
+    return jnp.concatenate([source[x, at] for x in range(4)], axis=0)
+
+
+def gather_parts(up_map, top_nbr, edges, source):
     mixed = []
     for b in range(4):
         at = up_map[b // 2, b % 2]
-        picked = jnp.concatenate([top[top_nbr[k, at]] for k in range(4)], axis=0)
+        picked = jnp.concatenate([half_block(source, top_nbr[k, at]) for k in range(4)], axis=0)
         mixed.append(dot(edges[b], picked))
     return jnp.concatenate(mixed, axis=0)
 
 
-def half_kernel(
-    map_in, nbr_in, mine, adj_in, fine_in, tiles_in, w_msg_in, w_agg_in, w_down_in, gain_in,
-    edges, mixed, chosen, fine, tiles, w_msg, w_agg, w_down, gain,
-    top, near, adj, up_map, top_nbr, sems, *, core_axis,
-):
-    first = start_all([(map_in, up_map), (nbr_in, top_nbr)], sems)
-    rest = [
-        (fine_in, fine), (tiles_in, tiles), (w_msg_in, w_msg), (w_agg_in, w_agg),
-        (w_down_in, w_down), (gain_in, gain),
-    ]
-    rest = start_all(rest, sems.at[pl.ds(6, 6)])
-    for copy in first:
-        copy.wait()
-    pairs = [(adj_in.at[up_map[b // 2, b % 2]], adj.at[b]) for b in range(4)]
-    copies = start_all(pairs, sems.at[pl.ds(2, 4)])
-    spread_rows(mine, top)
-    core = lax.axis_index(core_axis)
-    for b in range(4):
-        copies[b].wait()
-        low = jnp.concatenate([adj[b, k][:, :64] for k in range(4)], axis=1)
-        high = jnp.concatenate([adj[b, k][:, 64:] for k in range(4)], axis=1)
-        near[b] = jnp.where(core == 0, low, high)
-        edges[b] = jnp.where(core == 0, high, low)
-        chosen[b] = top[up_map[b // 2, b % 2]]
-    mixed[...] = gather_parts(up_map, top_nbr, near, top)
-    for copy in rest:
-        copy.wait()
+def half_kernel(map_in, nbr_in, mine, near, mixed, chosen, up_map, top_nbr, sems):
+    for copy in start_all([(map_in, up_map), (nbr_in, top_nbr)], sems):
+        copy.wait()
+    for b in range(4):
+        chosen[b] = half_block(mine, up_map[b // 2, b % 2])
+    mixed[...] = gather_parts(up_map, top_nbr, near, mine)
 
 
 def top_kernel(
-    map_in, nbr_in, other, edges, mixed, chosen, fine, tiles, w_msg, w_agg, w_down, gain,
-    out, top, whole, up_map, top_nbr, sems, *, core_axis,
+    map_in, nbr_in, other, away, mixed, chosen, fine, turned, w_msg, w_agg, w_down, gain,
+    out, whole, up_map, top_nbr, sems, *, core_axis,
 ):
     copies = start_all([(map_in, up_map), (nbr_in, top_nbr)], sems)
-    spread_rows(other, top)
-    for copy in copies:
-        copy.wait()
     core = lax.axis_index(core_axis)
     here = pl.ds(pl.multiple_of(core * 64, 64), 64)
     there = pl.ds(pl.multiple_of((1 - core) * 64, 64), 64)
     for b in range(4):
         whole[b, here, :] = chosen[b]
-        whole[b, there, :] = top[up_map[b // 2, b % 2]]
-    both = mixed[...] + gather_parts(up_map, top_nbr, edges, top)
+    for copy in copies:
+        copy.wait()
+    for b in range(4):
+        whole[b, there, :] = half_block(other, up_map[b // 2, b % 2])
+    both = mixed[...] + gather_parts(up_map, top_nbr, away, other)
     tagg = dot(both.astype(BF16), w_msg[...]).astype(BF16)
     zero = jnp.concatenate([whole[b] for b in range(4)], axis=0).astype(F32)
     one = (zero + jax.nn.silu(dot(tagg, w_agg[...]))).astype(BF16)
-    lower = [
-        dot_t(tiles[b // 2, b % 2], one[b * 128 : (b + 1) * 128]).astype(BF16) for b in range(4)
-    ]
-    lower = jnp.concatenate(lower, axis=0)
-    final = norm(fine[...].astype(F32) + dot(lower, w_down[...]), gain[...]).astype(BF16)
-    out[...] = final.reshape(1, 2, 2, 128, 256)
-
-
-def call(body, ins, outs, scratch, name, busy=0, limit=24):
+    copies = []
+    for b in range(4):
+        rows = slice(b * 128, (b + 1) * 128)
+        lower = dot(turned[b // 2, b % 2], one[rows]).astype(BF16)
+        final = norm(fine[rows].astype(F32) + dot(lower, w_down[...]), gain[...])
+        whole[b] = final.astype(BF16)
+        copy = pltpu.make_async_copy(whole.at[b], out.at[0, b // 2, b % 2], sems.at[2 + b])
+        copy.start()
+        copies.append(copy)
+    for copy in copies:
+        copy.wait()
+
+
+def call(body, ins, outs, scratch, name, busy=0, limit=24, place=VMEM):
     return pl.pallas_call(
         body,
         out_shape=tuple(jax.ShapeDtypeStruct(shape, kind) for shape, kind in outs),
         in_specs=ins,
-        out_specs=(VMEM,) * len(outs),
+        out_specs=(place,) * len(outs),
         scratch_shapes=scratch,
         compiler_params=pltpu.CompilerParams(vmem_limit_bytes=limit * MIB),
         cost_estimate=pl.CostEstimate(flops=0, bytes_accessed=busy, transcendentals=0),
@@ -237,6 +235,7 @@
     rows, cols = lax.axis_size("sy"), lax.axis_size("x") * lax.axis_size("core")
     east = [(i, (i + 1) % cols) for i in range(cols)]
     west = [(j, i) for i, j in east]
+    twin = [(0, 1), (1, 0)]
     south = [(i, i + 1) for i in range(rows - 1)]
     north = [(j, i) for i, j in south]
     weight = ((256, 256), BF16)
@@ -248,23 +247,30 @@
     last_row, first_row, last_col, first_col = call(
         cut_kernel, [HBM], [row_cut, row_cut, col_cut, col_cut], [dma((4,))], "cut", 1 << 20
     )(far(fine_state))
+    down = lax.ppermute(first_row, "sy", north)
     up = lax.ppermute(last_row, "sy", south)
-    down = lax.ppermute(first_row, "sy", north)
     left = lax.ppermute(last_col, sx, east)
     right = lax.ppermute(first_col, sx, west)
-    corner_l = lax.ppermute(jnp.concatenate([up[0, :, 1], down[0, :, 1]]), sx, east)
-    corner_r = lax.ppermute(jnp.concatenate([up[0, :, 0], down[0, :, 0]]), sx, west)
+    half_set = ((4, 128, 256), BF16)
     staged = [
-        fine_nbr, up_map, fine_adj, up_tiles, w_fine_msg, w_fine_agg, w_fine_out, fine_gain[None],
+        up_map, fine_nbr, fine_adj, up_tiles, w_fine_msg, w_fine_agg, w_fine_out, fine_gain[None],
     ]
-    held = call(
-        stage_kernel,
-        [HBM] * 10,
-        [(fine_state.shape, BF16), part] + [(array.shape, array.dtype) for array in staged],
-        [pltpu.VMEM(*weight), dma((10,))],
+    *held, turned, near, away = call(
+        functools.partial(stage_kernel, core_axis="core"),
+        [HBM] * 11,
+        [(fine_state.shape, BF16), part]
+        + [(array.shape, array.dtype) for array in staged]
+        + [tile_set, half_set, half_set],
+        [
+            pltpu.VMEM(*weight), pltpu.SMEM((2, 2), jnp.int32),
+            pltpu.VMEM((4, 4, 128, 128), BF16), dma((15,)),
+        ],
         "stage",
         1 << 23,
-    )(*[far(array) for array in [fine_state, w_fine_self] + staged])
+    )(*[far(array) for array in [fine_state, w_fine_self] + staged + [top_adj]])
+    down, up, held = lax.optimization_barrier((down, up, held))
+    corner_l = lax.ppermute(jnp.concatenate([down[0, :, 1], up[0, :, 1]]), sx, east)
+    corner_r = lax.ppermute(jnp.concatenate([down[0, :, 0], up[0, :, 0]]), sx, west)
     fine, piece = call(
         fine_kernel,
         [VMEM] * 16,
@@ -276,36 +282,39 @@
         "fine_level",
         1 << 23,
     )(up, down, left, right, corner_l, corner_r, *held)
-    got = lax.all_to_all(piece, ("sy", "x", "core"), 0, 0)
+    chips = lax.axis_size("x") * rows
+    back = [2 * chip + core for chip in range(chips - 1, -1, -1) for core in range(2)]
+    got = lax.all_to_all(piece, ("x", "sy", "core"), 0, 0, axis_index_groups=[back])
     (share,) = call(
-        sum_kernel, [VMEM] * 2, [((32, 40, 256), BF16)], [], "top_sum", 1 << 20
+        sum_kernel, [VMEM] * 2, [((8, 40, 256), BF16)], [], "top_sum", 1 << 20
     )(got, top_gain[None])
-    mine = lax.all_to_all(share, ("sy", "x"), 0, 0)
-    other = lax.ppermute(mine, "core", [(0, 1), (1, 0)])
+    column = lax.all_to_all(share, "sy", 0, 0, axis_index_groups=[list(range(rows - 1, -1, -1))])
+    (column,) = call(
+        order_kernel, [VMEM], [((4, 20, 16, 256), BF16)], [], "top_order", 1 << 20
+    )(column)
+    mine = lax.all_to_all(column, "x", 0, 0, axis_index_groups=[list(range(cols // 2 - 1, -1, -1))])
+    other = lax.ppermute(mine, "core", twin)
     tables = [pltpu.SMEM((2, 2), jnp.int32), pltpu.SMEM((4, 20), jnp.int32)]
-    top = pltpu.VMEM((20, 64, 256), BF16)
-    half_set = ((4, 128, 256), BF16)
-    half = call(
-        functools.partial(half_kernel, core_axis="core"),
-        [HBM] * 2 + [VMEM] + [HBM] * 7,
-        [
-            half_set, part, ((4, 64, 256), BF16), ((512, 256), BF16), tile_set, weight, weight, weight, gain,
-        ],
-        [top, pltpu.VMEM(*half_set), pltpu.VMEM((4, 4, 128, 128), BF16)] + tables + [dma((12,))],
+    mixed, chosen = call(
+        half_kernel,
+        [HBM] * 2 + [VMEM] * 2,
+        [part, ((4, 64, 256), BF16)],
+        tables + [dma((2,))],
         "top_half",
         1 << 23,
-    )(
-        up_map, top_nbr.T, mine, top_adj, fine, up_tiles, w_top_msg, w_top_agg, w_down,
-        out_gain[None],
-    )
+    )(up_map, top_nbr.T, mine, near)
     (out,) = call(
         functools.partial(top_kernel, core_axis="core"),
         [HBM] * 2 + [VMEM] * 10,
         [(fine_state.shape, BF16)],
-        [top, pltpu.VMEM(*half_set)] + tables + [dma((2,))],
+        [pltpu.VMEM(*half_set)] + tables + [dma((6,))],
         "top_level",
         1 << 23,
-    )(up_map, top_nbr.T, other, *half)
+        place=HBM,
+    )(
+        up_map, top_nbr.T, other, away, mixed, chosen, fine, turned, w_top_msg, w_top_agg,
+        w_down, out_gain[None],
+    )
     return out
 
 

time: 81.8 us -> 78.7 us (0.962)
  blocking collectives: 49.7 us -> 45.8 us
  starting transfers between devices: 17.7 us -> 20.9 us
  waiting for transfers between devices: 4.19 us -> 2.28 us
    all_to_all x2 -> x3, blocking collectives: 49.7 us -> 45.8 us  [the longest x1 24.3 us: local(): lax.all_to_all(piece, ('x', 'sy', 'core'), 0, 0, axis_index_groups=[back])]
    ppermute x1, starting transfers between devices: 1.31 us -> 3.94 us  [local(): right = lax.ppermute(first_col, sx, west)]
    ppermute x1, waiting for transfers between devices: 1.65 us -> 0.01 us  [local(): down = lax.ppermute(first_row, 'sy', north)]
    pallas_call x3 -> x4, Pallas kernels: 4.3 us -> 3.76 us  [the longest x1 2.3 us: local(): call(functools.partial(stage_kernel, core_axis='core'), [HBM] * 11, [(fin...]
  transfers between devices with their start and end apart: 7 -> 7, of which waited for: 2 -> 3; matrix products, arithmetic and copies ran while one was open for 0% -> 0% of each run, Pallas kernels for 5% -> 4%
where the time goes in v3:
time: 78.7 us; the launch traced here: 78.4 us
  blocking collectives  45.8 us (58%)
  starting transfers between devices  20.9 us (27%)
  Pallas kernels  9.01 us (11%)
  waiting for transfers between devices  2.28 us (3%)
    all_to_all x1, blocking collectives, local(): lax.all_to_all(piece, ('x', 'sy', 'core'), 0, 0, axis_index_groups=[back])  24.3 us
    all_to_all x1, blocking collectives, local(): lax.all_to_all(share, 'sy', 0, 0, axis_index_groups=[list(range(rows - 1,...  11.1 us
    all_to_all x1, blocking collectives, local(): lax.all_to_all(column, 'x', 0, 0, axis_index_groups=[list(range(cols // 2...  10.5 us
    ppermute x1, starting transfers between devices, local(): up = lax.ppermute(last_row, 'sy', south)  5.46 us
    ppermute x1, starting transfers between devices, local(): other = lax.ppermute(mine, 'core', twin)  5.2 us
    ppermute x1, starting transfers between devices, local(): right = lax.ppermute(first_col, sx, west)  3.94 us
    ppermute x1, starting transfers between devices, local(): lax.ppermute(jnp.concatenate([down[0, :, 0], up[0, :, 0]]), sx, west)  2.94 us
    pallas_call x1, Pallas kernels, local(): call(functools.partial(stage_kernel, core_axis='core'), [HBM] * 11, [(fin...  2.3 us
  transfers between devices with their start and end apart: 7, of which 3 were waited for; matrix products, arithmetic and copies ran while one was open for 0% of the time, Pallas kernels for 4%

profile of v3, /device:TPU:1, one launch (start us, length us, event | category | flops | bytes accessed | tf_op | source)
XLA Modules:
  0.0 78.4 jit_solution(1449813387183615825)
XLA Ops:
  0.0 1.1 %cut.1 = (bf16[1,1,2,128,256]{4,3,2,1,0:T(8,128)(2,1)S(1)}, bf16[1,1,2,128,256]{4,3,2,1,0:T(8,128)(2,1)S(1)}, bf16[1,2,1,128,256]{4,3,2,1,0:T(8,128)(2,1)S(1)}, bf16[1,2,1,128,256]{4,3,2,1,0:T(8,128)(2,1)S(1)}) custom-call(bf16[1,2,2,128,256]{4,3,2,1,0:T(8,128)(2,1)} %state_in.1), custom_call_target="tpu_custom_call" | custom-call | bytes 1048576 | tf_op jit(solution)/shard_map/cut/pallas_call | solution.py:247
  1.1 1.3 %collective-permute-start = (bf16[1,1,2,128,256]{4,3,2,1,0:T(8,128)(2,1)S(1)}, bf16[1,1,2,128,256]{4,3,2,1,0:T(8,128)(2,1)S(1)}, u32[]{:S(2)}, u32[]{:S(2)}) collective-permute-start(bf16[1,1,2,128,256]{4,3,2,1,0:T(8,128)(2,1)S(1)} %get-tuple-element.38), channel_id=1, source_target_pairs={{8,0},{16,8},{24,16},{32,24},{40,32},{48,40},{56,48},{9,1},{17,9},... | collective-permute-start | bytes 393224 | tf_op jit(solution)/shard_map/ppermute | solution.py:250
  2.4 5.5 %collective-permute-start.1 = (bf16[1,1,2,128,256]{4,3,2,1,0:T(8,128)(2,1)S(1)}, bf16[1,1,2,128,256]{4,3,2,1,0:T(8,128)(2,1)S(1)}, u32[]{:S(2)}, u32[]{:S(2)}) collective-permute-start(bf16[1,1,2,128,256]{4,3,2,1,0:T(8,128)(2,1)S(1)} %get-tuple-element.39), channel_id=1, source_target_pairs={{0,8},{8,16},{16,24},{24,32},{32,40},{40,48},{48,56},{1,9},{9,17},... | collective-permute-start | bytes 393224 | tf_op jit(solution)/shard_map/ppermute | solution.py:251
  7.9 2.1 %collective-permute-start.2 = (bf16[1,2,1,128,256]{4,3,2,1,0:T(8,128)(2,1)S(1)}, bf16[1,2,1,128,256]{4,3,2,1,0:T(8,128)(2,1)S(1)}, u32[]{:S(2)}, u32[]{:S(2)}) collective-permute-start(bf16[1,2,1,128,256]{4,3,2,1,0:T(8,128)(2,1)S(1)} %get-tuple-element.52), channel_id=1, source_target_pairs={{0,1},{1,2},{2,3},{3,4},{4,5},{5,6},{6,7},{7,0},{8,9},{9,10},{10,1... | collective-permute-start | bytes 393224 | tf_op jit(solution)/shard_map/ppermute | solution.py:252
  10.0 3.9 %collective-permute-start.3 = (bf16[1,2,1,128,256]{4,3,2,1,0:T(8,128)(2,1)S(1)}, bf16[1,2,1,128,256]{4,3,2,1,0:T(8,128)(2,1)S(1)}, u32[]{:S(2)}, u32[]{:S(2)}) collective-permute-start(bf16[1,2,1,128,256]{4,3,2,1,0:T(8,128)(2,1)S(1)} %get-tuple-element.53), channel_id=1, source_target_pairs={{1,0},{2,1},{3,2},{4,3},{5,4},{6,5},{7,6},{0,7},{9,8},{10,9},{11,1... | collective-permute-start | bytes 393224 | tf_op jit(solution)/shard_map/ppermute | solution.py:253
  13.9 2.3 %stage.1 = (bf16[1,2,2,128,256]{4,3,2,1,0:T(8,128)(2,1)S(1)}, f32[512,256]{1,0:T(8,128)S(1)}, s32[2,2]{1,0:T(2,128)S(1)}, s32[2,2,4]{2,1,0:T(2,128)S(1)}, bf16[2...) custom-call(bf16[1,2,2,128,256]{4,3,2,1,0:T(8,128)(2,1)} %state_in.1, ...), custom_call_target="tpu_custom_call" | custom-call | bytes 8388608 | tf_op jit(solution)/shard_map/stage/pallas_call | solution.py:258
  16.2 0.0 copy-start.6
  16.2 0.0 collective-permute-done.down
  16.2 0.0 collective-permute-done.1.up
  16.3 0.0 collective-permute-start.4
  16.4 0.0 copy-start.3
  16.4 0.0 copy-start.4
  16.4 2.9 %collective-permute-start.5 = (bf16[2,128,256]{2,1,0:T(8,128)(2,1)S(1)}, bf16[2,128,256]{2,1,0:T(8,128)(2,1)S(1)}, u32[]{:S(2)}, u32[]{:S(2)}) collective-permute-start(bf16[2,128,256]{2,1,0:T(8,128)(2,1)S(1)} %pad_maximum_fusion.1), channel_id=1, source_target_pairs={{1,0},{2,1},{3,2},{4,3},{5,4},{6,5},{7,6},{0,7},{9,8},{10,9},{11,1... | collective-permute-start | bytes 393224 | tf_op jit(solution)/shard_map/ppermute | solution.py:273
  19.3 0.0 collective-permute-done.2.left
  19.3 0.0 collective-permute-done.3.right
  19.3 0.8 collective-permute-done.4.corner_l
  20.1 0.7 collective-permute-done.5.corner_r
  20.8 1.9 %fine_level.1 = (bf16[512,256]{1,0:T(8,128)(2,1)S(1)}, bf16[64,24,128]{2,1,0:T(8,128)(2,1)S(1)}) custom-call(bf16[1,1,2,128,256]{4,3,2,1,0:T(8,128)(2,1)S(1)} %collective-permute-done.1.up, bf16[1,1,2,128,256]{4,3,2,1,0:T(8,128)(2,1)S(1)} %collective-permute-done.down, bf16[1,2,1,128,256]{4,3,2,1,0:T(8,128)(2,1)S(1)} %collective-permute-done.2.left, ...), custom_call_target="tpu_custom_call" | custom-call | bytes 8388608 | tf_op jit(solution)/shard_map/fine_level/pallas_call | solution.py:274
  22.7 0.0 copy-start
  22.7 0.0 copy-start.1
  22.7 0.0 copy-start.2
  22.7 0.0 copy-start.5
  22.7 24.3 %all_to_all.15.got = bf16[64,24,128]{2,1,0:T(8,128)(2,1)S(1)} all-to-all(bf16[64,24,128]{2,1,0:T(8,128)(2,1)S(1)} %get-tuple-element.64), channel_id=1, replica_groups={{62,63,54,55,46,47,38,39,30,31,22,23,14,15,6,7,60,61,52,53,44,45,36,37,..., dimensions={0} | all-to-all | bytes 786432 | tf_op jit(solution)/shard_map/all_to_all | solution.py:287
  47.0 0.0 copy-done.6
  47.0 0.4 top_sum.1
  47.4 11.1 %all_to_all.16.got = bf16[8,40,256]{2,1,0:T(8,128)(2,1)S(1)} all-to-all(bf16[8,40,256]{2,1,0:T(8,128)(2,1)S(1)} %top_sum.1), channel_id=1, replica_groups={{56,48,40,32,24,16,8,0},{57,49,41,33,25,17,9,1},{58,50,42,34,26,18,10,2..., dimensions={0} | all-to-all | bytes 327680 | tf_op jit(solution)/shard_map/all_to_all | solution.py:291
  58.5 0.2 top_order.1
  58.7 10.5 %all_to_all.17.mine = bf16[4,20,16,256]{3,2,1,0:T(8,128)(2,1)S(1)} all-to-all(bf16[4,20,16,256]{3,2,1,0:T(8,128)(2,1)S(1)} %top_order.1), channel_id=1, replica_groups={{6,4,2,0},{7,5,3,1},{14,12,10,8},{15,13,11,9},{22,20,18,16},{23,21,19,1..., dimensions={0} | all-to-all | bytes 1310720 | tf_op jit(solution)/shard_map/all_to_all | solution.py:295
  69.2 5.2 %collective-permute-start.6 = (bf16[4,20,16,256]{3,2,1,0:T(8,128)(2,1)S(1)}, bf16[4,20,16,256]{3,2,1,0:T(8,128)(2,1)S(1)}, u32[]{:S(2)}, u32[]{:S(2)}) collective-permute-start(bf16[4,20,16,256]{3,2,1,0:T(8,128)(2,1)S(1)} %all_to_all.17.mine), channel_id=1, source_target_pairs={{0,1},{1,0},{2,3},{3,2},{4,5},{5,4},{6,7},{7,6},{8,9},{9,8},{10,11... | collective-permute-start | bytes 1966088 | tf_op jit(solution)/shard_map/ppermute | solution.py:296
  74.4 0.0 copy-done.3
  74.4 0.0 copy-done.4
  74.4 0.9 %top_half.1 = (f32[512,256]{1,0:T(8,128)S(1)}, bf16[4,64,256]{2,1,0:T(8,128)(2,1)S(1)}) custom-call(s32[2,2]{1,0:T(2,128)S(1)} %copy-done.3, s32[4,20]{1,0:T(4,128)S(1)} %bitcast.12, bf16[4,20,16,256]{3,2,1,0:T(8,128)(2,1)S(1)} %all_to_all.17.mine, bf16[4,128,256]{2,1,0:T(8,128)(2,1)S(1)} %get-tuple-element.66.near), custom_call_target="tpu_custom_call" | custom-call | bytes 8388608 | tf_op jit(solution)/shard_map/top_half/pallas_call | solution.py:298
  75.3 0.8 %collective-permute-done.6.other = bf16[4,20,16,256]{3,2,1,0:T(8,128)(2,1)S(1)} collective-permute-done((bf16[4,20,16,256]{3,2,1,0:T(8,128)(2,1)S(1)}, bf16[4,20,16,256]{3,2,1,0:T(8,128)(2,1)S(1)}, u32[]{:S(2)}, u32[]{:S(2)}) %collective-permute-start.6) | collective-permute-done | bytes 655392 | tf_op jit(solution)/shard_map/ppermute | solution.py:296
  76.1 0.0 copy-done
  76.1 0.0 copy-done.1
  76.1 0.0 copy-done.2
  76.1 0.0 copy-done.5
  76.1 2.3 %top_level.1 = bf16[1,2,2,128,256]{4,3,2,1,0:T(8,128)(2,1)} custom-call(s32[2,2]{1,0:T(2,128)S(1)} %copy-done.3, s32[4,20]{1,0:T(4,128)S(1)} %bitcast.13, bf16[4,20,16,256]{3,2,1,0:T(8,128)(2,1)S(1)} %collective-permute-done.6.other, bf16[4,128,256]{2,1,0:T(8,128)(2,1)S(1)} %get-tuple-element.65.away, f32[512,256]{1,0:T(8,128)S(1)} %get-tuple-element.67.mixed, ...), custom_call_target="tpu_custom_call" | custom-call | bytes 8388608 | tf_op jit(solution)/shard_map/top_level/pallas_call | solution.py:306
  (3 shorter events, 0.1 us)
Async XLA Ops:
  1.1 15.1 %collective-permute-start = (bf16[1,1,2,128,256]{4,3,2,1,0:T(8,128)(2,1)S(1)}, bf16[1,1,2,128,256]{4,3,2,1,0:T(8,128)(2,1)S(1)}, u32[]{:S(2)}, u32[]{:S(2)}) collective-permute-start(bf16[1,1,2,128,256]{4,3,2,1,0:T(8,128)(2,1)S(1)} %get-tuple-element.38), channel_id=1, source_target_pairs={{8,0},{16,8},{24,16},{32,24},{40,32},{48,40},{56,48},{9,1},{17,9},... | collective-permute-start | bytes 393224 | tf_op jit(solution)/shard_map/ppermute | solution.py:250
  2.4 13.8 %collective-permute-start.1 = (bf16[1,1,2,128,256]{4,3,2,1,0:T(8,128)(2,1)S(1)}, bf16[1,1,2,128,256]{4,3,2,1,0:T(8,128)(2,1)S(1)}, u32[]{:S(2)}, u32[]{:S(2)}) collective-permute-start(bf16[1,1,2,128,256]{4,3,2,1,0:T(8,128)(2,1)S(1)} %get-tuple-element.39), channel_id=1, source_target_pairs={{0,8},{8,16},{16,24},{24,32},{32,40},{40,48},{48,56},{1,9},{9,17},... | collective-permute-start | bytes 393224 | tf_op jit(solution)/shard_map/ppermute | solution.py:251
  7.9 11.4 %collective-permute-start.2 = (bf16[1,2,1,128,256]{4,3,2,1,0:T(8,128)(2,1)S(1)}, bf16[1,2,1,128,256]{4,3,2,1,0:T(8,128)(2,1)S(1)}, u32[]{:S(2)}, u32[]{:S(2)}) collective-permute-start(bf16[1,2,1,128,256]{4,3,2,1,0:T(8,128)(2,1)S(1)} %get-tuple-element.52), channel_id=1, source_target_pairs={{0,1},{1,2},{2,3},{3,4},{4,5},{5,6},{6,7},{7,0},{8,9},{9,10},{10,1... | collective-permute-start | bytes 393224 | tf_op jit(solution)/shard_map/ppermute | solution.py:252
  10.0 9.4 %collective-permute-start.3 = (bf16[1,2,1,128,256]{4,3,2,1,0:T(8,128)(2,1)S(1)}, bf16[1,2,1,128,256]{4,3,2,1,0:T(8,128)(2,1)S(1)}, u32[]{:S(2)}, u32[]{:S(2)}) collective-permute-start(bf16[1,2,1,128,256]{4,3,2,1,0:T(8,128)(2,1)S(1)} %get-tuple-element.53), channel_id=1, source_target_pairs={{1,0},{2,1},{3,2},{4,3},{5,4},{6,5},{7,6},{0,7},{9,8},{10,9},{11,1... | collective-permute-start | bytes 393224 | tf_op jit(solution)/shard_map/ppermute | solution.py:253
  16.2 30.7 %copy-start.6 = (f32[256]{0:T(256)S(1)}, f32[256]{0:T(256)}, u32[]{:S(2)}) copy-start(f32[256]{0:T(256)} %param.32) | copy-start | bytes 3076
  16.3 3.8 %collective-permute-start.4 = (bf16[2,128,256]{2,1,0:T(8,128)(2,1)S(1)}, bf16[2,128,256]{2,1,0:T(8,128)(2,1)S(1)}, u32[]{:S(2)}, u32[]{:S(2)}) collective-permute-start(bf16[2,128,256]{2,1,0:T(8,128)(2,1)S(1)} %pad_maximum_fusion), channel_id=1, source_target_pairs={{0,1},{1,2},{2,3},{3,4},{4,5},{5,6},{6,7},{7,0},{8,9},{9,10},{10,1... | collective-permute-start | bytes 393224 | tf_op jit(solution)/shard_map/ppermute | solution.py:272
  16.4 58.0 %copy-start.3 = (s32[2,2]{1,0:T(2,128)S(1)}, s32[2,2]{1,0:T(2,128)}, u32[]{:S(2)}) copy-start(s32[2,2]{1,0:T(2,128)} %map_in.5) | copy-start | bytes 52
  16.4 58.0 %copy-start.4 = (s32[20,4]{0,1:T(4,128)S(1)}, s32[20,4]{0,1:T(4,128)}, u32[]{:S(2)}) copy-start(s32[20,4]{0,1:T(4,128)} %param.23) | copy-start | bytes 964
  16.4 4.4 %collective-permute-start.5 = (bf16[2,128,256]{2,1,0:T(8,128)(2,1)S(1)}, bf16[2,128,256]{2,1,0:T(8,128)(2,1)S(1)}, u32[]{:S(2)}, u32[]{:S(2)}) collective-permute-start(bf16[2,128,256]{2,1,0:T(8,128)(2,1)S(1)} %pad_maximum_fusion.1), channel_id=1, source_target_pairs={{1,0},{2,1},{3,2},{4,3},{5,4},{6,5},{7,6},{0,7},{9,8},{10,9},{11,1... | collective-permute-start | bytes 393224 | tf_op jit(solution)/shard_map/ppermute | solution.py:273
  22.7 53.4 %copy-start = (bf16[256,256]{1,0:T(8,128)(2,1)S(1)}, bf16[256,256]{1,0:T(8,128)(2,1)}, u32[]{:S(2)}) copy-start(bf16[256,256]{1,0:T(8,128)(2,1)} %w_msg.1) | copy-start | bytes 393220
  22.7 53.4 %copy-start.1 = (bf16[256,256]{1,0:T(8,128)(2,1)S(1)}, bf16[256,256]{1,0:T(8,128)(2,1)}, u32[]{:S(2)}) copy-start(bf16[256,256]{1,0:T(8,128)(2,1)} %w_agg.1) | copy-start | bytes 393220
  22.7 53.4 %copy-start.2 = (bf16[256,256]{1,0:T(8,128)(2,1)S(1)}, bf16[256,256]{1,0:T(8,128)(2,1)}, u32[]{:S(2)}) copy-start(bf16[256,256]{1,0:T(8,128)(2,1)} %w_down.1) | copy-start | bytes 393220
  22.7 53.4 %copy-start.5 = (f32[256]{0:T(256)S(1)}, f32[256]{0:T(256)}, u32[]{:S(2)}) copy-start(f32[256]{0:T(256)} %param.33) | copy-start | bytes 3076
  69.2 6.9 %collective-permute-start.6 = (bf16[4,20,16,256]{3,2,1,0:T(8,128)(2,1)S(1)}, bf16[4,20,16,256]{3,2,1,0:T(8,128)(2,1)S(1)}, u32[]{:S(2)}, u32[]{:S(2)}) collective-permute-start(bf16[4,20,16,256]{3,2,1,0:T(8,128)(2,1)S(1)} %all_to_all.17.mine), channel_id=1, source_target_pairs={{0,1},{1,0},{2,3},{3,2},{4,5},{5,4},{6,7},{7,6},{8,9},{9,8},{10,11... | collective-permute-start | bytes 1966088 | tf_op jit(solution)/shard_map/ppermute | solution.py:296

commit v4 on v3

--- a/solution.py
+++ b/solution.py
@@ -52,41 +52,28 @@
 
 def stage_kernel(
     state_in, w_self_in, map_in, nbr_in, adj_in, tiles_in, w_msg_in, w_agg_in, w_out_in, gain_in,
-    top_adj, state, own_part, up_map, nbr, adj, tiles, w_msg, w_agg, w_out, gain,
-    turned, near, away, w_self, table, edges, sems, *, core_axis,
-):
-    first = pltpu.make_async_copy(map_in, table, sems.at[10])
-    first.start()
+    state, own_part, up_map, nbr, adj, tiles, w_msg, w_agg, w_out, gain, w_self, sems,
+):
     pairs = [
         (state_in, state), (w_self_in, w_self), (map_in, up_map), (nbr_in, nbr), (adj_in, adj),
         (tiles_in, tiles), (w_msg_in, w_msg), (w_agg_in, w_agg), (w_out_in, w_out),
         (gain_in, gain),
     ]
     copies = start_all(pairs, sems)
-    first.wait()
-    pairs = [(top_adj.at[table[b // 2, b % 2]], edges.at[b]) for b in range(4)]
-    edge_copies = start_all(pairs, sems.at[pl.ds(11, 4)])
     copies[0].wait()
     copies[1].wait()
     own = jnp.concatenate([state[0, b // 2, b % 2] for b in range(4)], axis=0)
     own_part[...] = dot(own, w_self[...])
     for copy in copies[2:]:
         copy.wait()
-    core = lax.axis_index(core_axis)
-    for b in range(4):
-        turned[b // 2, b % 2] = tiles[b // 2, b % 2].T
-        edge_copies[b].wait()
-        low = jnp.concatenate([edges[b, k][:, :64] for k in range(4)], axis=1)
-        high = jnp.concatenate([edges[b, k][:, 64:] for k in range(4)], axis=1)
-        near[b] = jnp.where(core == 0, low, high)
-        away[b] = jnp.where(core == 0, high, low)
-
-
-def fine_kernel(
-    up, down, left, right, corner_l, corner_r, state, own_part, map_in, nbr_in, adj, tiles,
-    w_msg, w_agg, w_out, gain, fine_out, piece_out, frame, nbr, up_map, sems,
-):
-    copies = start_all([(nbr_in, nbr), (map_in, up_map)], sems)
+
+
+def near_kernel(
+    map_in, nbr_in, up, down, left, right, state, adj, tiles, top_adj,
+    mixed, corner_edges, label, sent, turned, near, away, frame, up_map, nbr, edges, sems,
+    *, core_axis,
+):
+    copies = start_all([(map_in, up_map), (nbr_in, nbr)], sems)
     for c in range(2):
         frame[1 + c] = up[0, 0, c]
         frame[13 + c] = down[0, 0, c]
@@ -95,60 +82,96 @@
     for r in range(2):
         frame[(1 + r) * 4] = left[0, r, 0]
         frame[(1 + r) * 4 + 3] = right[0, r, 0]
-        frame[12 - 12 * r] = corner_l[r]
-        frame[15 - 12 * r] = corner_r[r]
+        frame[12 * r] = jnp.zeros((128, 256), BF16)
+        frame[12 * r + 3] = jnp.zeros((128, 256), BF16)
     for copy in copies:
         copy.wait()
-    own, mixed = [], []
+    pairs = [(top_adj.at[up_map[b // 2, b % 2]], edges.at[b]) for b in range(4)]
+    copies = start_all(pairs, sems.at[pl.ds(2, 4)])
+    lane = lax.broadcasted_iota(jnp.int32, (64, 128), 1)
+    block = lane >> 5
+    joined = jnp.where(
+        block < 2,
+        jnp.where(block == 0, up_map[0, 0], up_map[0, 1]),
+        jnp.where(block == 2, up_map[1, 0], up_map[1, 1]),
+    )
+    label[...] = jnp.where((lane & 31) == joined, 1.0, 0.0)
+    row = lax.broadcasted_iota(jnp.int32, (128, 128), 0)
+    col = lax.broadcasted_iota(jnp.int32, (128, 128), 1)
+    want = (row & 1) * 64 + (row & 62) + (row >> 6)
+    order = jnp.where(col == want, 1.0, 0.0).astype(BF16)
     for y in range(2):
         for x in range(2):
+            b = 2 * y + x
             picked = []
             for k in range(4):
                 code = nbr[y, x, k]
                 spot = (y + lax.div(code, 3)) * 4 + x + lax.rem(code, 3)
                 picked.append(frame[spot])
-            edges = jnp.concatenate([adj[y, x, k] for k in range(4)], axis=1)
-            mixed.append(dot(edges, jnp.concatenate(picked, axis=0)).astype(BF16))
-            own.append(frame[(1 + y) * 4 + 1 + x])
+                tile = adj[y, x, k]
+                corner = jnp.where(code == 6 * y + 2 * x, tile, jnp.zeros_like(tile))
+                corner_edges[b, :, 128 * k : 128 * k + 128] = corner
+            tile_row = jnp.concatenate([adj[y, x, k] for k in range(4)], axis=1)
+            mixed[128 * b : 128 * b + 128] = dot(tile_row, jnp.concatenate(picked, axis=0))
+    core = lax.axis_index(core_axis)
+    for b in range(4):
+        turned[b // 2, b % 2] = tiles[b // 2, b % 2].T
+        sent[b] = dot(order, tiles[b // 2, b % 2]).astype(BF16)
+        copies[b].wait()
+        low = jnp.concatenate([edges[b, k][:, :64] for k in range(4)], axis=1)
+        high = jnp.concatenate([edges[b, k][:, 64:] for k in range(4)], axis=1)
+        near[b] = jnp.where(core == 0, low, high)
+        away[b] = jnp.where(core == 0, high, low)
+
+
+def fine_kernel(
+    corner_l, corner_r, mixed_in, corner_edges, label, sent, state, own_part,
+    w_msg, w_agg, w_out, gain, fine_out, piece_out, lines,
+):
+    own, mixed = [], []
+    for y in range(2):
+        for x in range(2):
+            b = 2 * y + x
+            corner = (corner_r if x else corner_l)[1 - y]
+            picked = jnp.concatenate([corner] * 4, axis=0)
+            total = mixed_in[128 * b : 128 * b + 128] + dot(corner_edges[b], picked)
+            mixed.append(total.astype(BF16))
+            own.append(state[0, y, x])
     own = jnp.concatenate(own, axis=0)
     mixed = jnp.concatenate(mixed, axis=0)
     agg = dot(mixed, w_msg[...]).astype(BF16)
     hidden = jax.nn.silu(own_part[...] + dot(agg, w_agg[...])).astype(BF16)
     fine = norm(own.astype(F32) + dot(hidden, w_out[...]), gain[...]).astype(BF16)
     fine_out[...] = fine
-    contrib = [
-        dot(tiles[b // 2, b % 2], fine[b * 128 : (b + 1) * 128]).astype(BF16) for b in range(4)
-    ]
-    row = lax.broadcasted_iota(jnp.int32, (128, 128), 0)
-    col = lax.broadcasted_iota(jnp.int32, (128, 128), 1)
-    dest = row >> 3
-    want = ((row >> 1) & 3) * 32 + (dest & 1) * 16 + (dest >> 1) * 2 + (row & 1)
-    order = jnp.where(col == want, 1.0, 0.0).astype(BF16)
-    piece = []
-    for g in range(4):
-        spots = [(b, 64 * core + 16 * g) for b in range(4) for core in range(2)]
-        rows = jnp.concatenate([contrib[b][at : at + 16] for b, at in spots], axis=0)
-        piece.append(dot(order, rows))
-    piece = jnp.concatenate(piece, axis=0).reshape(64, 8, 256)
-    line = lax.broadcasted_iota(jnp.int32, (64, 8, 128), 1) >> 1
-    label = jnp.where(
-        line < 2,
-        jnp.where(line == 0, up_map[0, 0], up_map[0, 1]),
-        jnp.where(line == 2, up_map[1, 0], up_map[1, 1]),
-    ).astype(F32)
-    parts = [piece[:, :, :128], piece[:, :, 128:], label]
-    piece_out[...] = jnp.concatenate(parts, axis=1).astype(BF16)
-
-
-def sum_kernel(got, gain, share_out):
-    wide = got[...].astype(F32)
-    values = jnp.concatenate([wide[:, :8], wide[:, 8:16]], axis=2).reshape(512, 256).astype(BF16)
-    label = wide[:, 16:].reshape(512, 128).astype(jnp.int32)
-    row = lax.broadcasted_iota(jnp.int32, (512, 128), 0)
-    col = lax.broadcasted_iota(jnp.int32, (512, 128), 1)
-    member = jnp.where((label * 2 + (row & 1)) == col, 1.0, 0.0).astype(BF16)
-    total = dot_t(member, values)[:40]
-    share = norm(total, gain[...]).astype(BF16)
+    for b in range(4):
+        contrib = dot(sent[b], fine[b * 128 : (b + 1) * 128])
+        for h in range(2):
+            for i in range(2):
+                part = contrib[64 * i : 64 * i + 64, 128 * h : 128 * h + 128]
+                lines[pl.ds(8 * h + 2 * b + i, 64, stride=18), :] = part
+    lines[pl.ds(16, 64, stride=18), :] = label[...]
+    lines[pl.ds(17, 64, stride=18), :] = jnp.zeros((64, 128), F32)
+    piece_out[...] = lines[...].astype(BF16)
+
+
+def sum_kernel(got, gain, share_out, lines):
+    lines[...] = got[...].astype(F32)
+    take = lambda n: lines[pl.ds(n, 64, stride=18), :]
+    label = take(16)
+    member, values = [], []
+    for b in range(4):
+        member.append(pltpu.roll(label, (128 - 32 * b) % 128, 1) if b else label)
+        wide = [take(8 * h + 2 * b + i) for i in range(2) for h in range(2)]
+        values.append(jnp.concatenate(wide, axis=1))
+    member = jnp.concatenate(member, axis=0).astype(BF16)
+    values = jnp.concatenate(values, axis=0).astype(BF16)
+    total = dot_t(member, values)[:32]
+    both = [norm(total[:, 256 * i : 256 * i + 256], gain[...]) for i in range(2)]
+    both = jnp.concatenate(both, axis=0).astype(BF16)
+    row = lax.broadcasted_iota(jnp.int32, (40, 64), 0)
+    col = lax.broadcasted_iota(jnp.int32, (40, 64), 1)
+    order = jnp.where(col == (row & 1) * 32 + (row >> 1), 1.0, 0.0).astype(BF16)
+    share = dot(order, both).astype(BF16)
     share_out[...] = jnp.broadcast_to(share[None], share_out.shape)
 
 
@@ -255,39 +278,52 @@
     staged = [
         up_map, fine_nbr, fine_adj, up_tiles, w_fine_msg, w_fine_agg, w_fine_out, fine_gain[None],
     ]
-    *held, turned, near, away = call(
-        functools.partial(stage_kernel, core_axis="core"),
-        [HBM] * 11,
-        [(fine_state.shape, BF16), part]
-        + [(array.shape, array.dtype) for array in staged]
-        + [tile_set, half_set, half_set],
-        [
-            pltpu.VMEM(*weight), pltpu.SMEM((2, 2), jnp.int32),
-            pltpu.VMEM((4, 4, 128, 128), BF16), dma((15,)),
-        ],
+    held = call(
+        stage_kernel,
+        [HBM] * 10,
+        [(fine_state.shape, BF16), part] + [(array.shape, array.dtype) for array in staged],
+        [pltpu.VMEM(*weight), dma((10,))],
         "stage",
         1 << 23,
-    )(*[far(array) for array in [fine_state, w_fine_self] + staged + [top_adj]])
+    )(*[far(array) for array in [fine_state, w_fine_self] + staged])
     down, up, held = lax.optimization_barrier((down, up, held))
     corner_l = lax.ppermute(jnp.concatenate([down[0, :, 1], up[0, :, 1]]), sx, east)
     corner_r = lax.ppermute(jnp.concatenate([down[0, :, 0], up[0, :, 0]]), sx, west)
+    state, own_part, map_here, nbr_here, adj, tiles, *weights = held
+    mixed, corner_edges, label, sent, turned, near, away = call(
+        functools.partial(near_kernel, core_axis="core"),
+        [VMEM] * 9 + [HBM],
+        [
+            part, ((4, 128, 512), BF16), ((64, 128), F32), ((4, 128, 128), BF16), tile_set,
+            half_set, half_set,
+        ],
+        [
+            pltpu.VMEM((16, 128, 256), BF16), pltpu.SMEM((2, 2), jnp.int32),
+            pltpu.SMEM((2, 2, 4), jnp.int32), pltpu.VMEM((4, 4, 128, 128), BF16), dma((6,)),
+        ],
+        "near",
+        1 << 23,
+    )(map_here, nbr_here, up, down, left, right, state, adj, tiles, far(top_adj))
     fine, piece = call(
         fine_kernel,
-        [VMEM] * 16,
-        [((512, 256), BF16), ((64, 24, 128), BF16)],
-        [
-            pltpu.VMEM((16, 128, 256), BF16), pltpu.SMEM((2, 2, 4), jnp.int32),
-            pltpu.SMEM((2, 2), jnp.int32), dma((2,)),
-        ],
+        [VMEM] * 12,
+        [((512, 256), BF16), ((64 * 18, 128), BF16)],
+        [pltpu.VMEM((64 * 18, 128), F32)],
         "fine_level",
         1 << 23,
-    )(up, down, left, right, corner_l, corner_r, *held)
+    )(corner_l, corner_r, mixed, corner_edges, label, sent, state, own_part, *weights)
+    piece = piece.reshape(64, 9, 2, 128)
     chips = lax.axis_size("x") * rows
     back = [2 * chip + core for chip in range(chips - 1, -1, -1) for core in range(2)]
     got = lax.all_to_all(piece, ("x", "sy", "core"), 0, 0, axis_index_groups=[back])
     (share,) = call(
-        sum_kernel, [VMEM] * 2, [((8, 40, 256), BF16)], [], "top_sum", 1 << 20
-    )(got, top_gain[None])
+        sum_kernel,
+        [VMEM] * 2,
+        [((8, 40, 256), BF16)],
+        [pltpu.VMEM((64 * 18, 128), F32)],
+        "top_sum",
+        1 << 20,
+    )(got.reshape(64 * 18, 128), top_gain[None])
     column = lax.all_to_all(share, "sy", 0, 0, axis_index_groups=[list(range(rows - 1, -1, -1))])
     (column,) = call(
         order_kernel, [VMEM], [((4, 20, 16, 256), BF16)], [], "top_order", 1 << 20

time: 78.7 us -> 75.4 us (0.958)
  blocking collectives: 45.8 us -> 43.1 us
  waiting for transfers between devices: 2.28 us -> 0.85 us
  Pallas kernels: 9.01 us -> 9.89 us
    all_to_all x1, blocking collectives: 24.3 us -> 21.6 us  [local(): lax.all_to_all(piece, ('x', 'sy', 'core'), 0, 0, axis_index_groups=[back])]
    pallas_call x3 -> x4, Pallas kernels: 4.58 us -> 5.47 us  [the longest x1 2.38 us: local(): call(functools.partial(near_kernel, core_axis='core'), [VMEM] * 9 + [HBM]...]
  transfers between devices with their start and end apart: 7 -> 7, of which waited for: 3 -> 1; matrix products, arithmetic and copies ran while one was open for 0% -> 0% of each run, Pallas kernels for 4% -> 6%
where the time goes in v4:
time: 75.4 us; the launch traced here: 75.1 us
  blocking collectives  43.1 us (57%)
  starting transfers between devices  20.9 us (28%)
  Pallas kernels  9.89 us (13%)
  waiting for transfers between devices  0.85 us (1%)
    all_to_all x1, blocking collectives, local(): lax.all_to_all(piece, ('x', 'sy', 'core'), 0, 0, axis_index_groups=[back])  21.6 us
    all_to_all x1, blocking collectives, local(): lax.all_to_all(share, 'sy', 0, 0, axis_index_groups=[list(range(rows - 1,...  10.8 us
    all_to_all x1, blocking collectives, local(): lax.all_to_all(column, 'x', 0, 0, axis_index_groups=[list(range(cols // 2...  10.7 us
    ppermute x1, starting transfers between devices, local(): up = lax.ppermute(last_row, 'sy', south)  5.46 us
    ppermute x1, starting transfers between devices, local(): other = lax.ppermute(mine, 'core', twin)  5.2 us
    ppermute x1, starting transfers between devices, local(): right = lax.ppermute(first_col, sx, west)  3.94 us
    ppermute x1, starting transfers between devices, local(): lax.ppermute(jnp.concatenate([down[0, :, 0], up[0, :, 0]]), sx, west)  2.94 us
    pallas_call x1, Pallas kernels, local(): call(functools.partial(near_kernel, core_axis='core'), [VMEM] * 9 + [HBM]...  2.38 us
  transfers between devices with their start and end apart: 7, of which 1 were waited for; matrix products, arithmetic and copies ran while one was open for 0% of the time, Pallas kernels for 6%

profile of v4, /device:TPU:1, one launch (start us, length us, event | category | flops | bytes accessed | tf_op | source)
XLA Modules:
  0.0 75.1 jit_solution(5387058883449797444)
XLA Ops:
  0.0 1.1 %cut.1 = (bf16[1,1,2,128,256]{4,3,2,1,0:T(8,128)(2,1)S(1)}, bf16[1,1,2,128,256]{4,3,2,1,0:T(8,128)(2,1)S(1)}, bf16[1,2,1,128,256]{4,3,2,1,0:T(8,128)(2,1)S(1)}, bf16[1,2,1,128,256]{4,3,2,1,0:T(8,128)(2,1)S(1)}) custom-call(bf16[1,2,2,128,256]{4,3,2,1,0:T(8,128)(2,1)} %state_in.1), custom_call_target="tpu_custom_call" | custom-call | bytes 1048576 | tf_op jit(solution)/shard_map/cut/pallas_call | solution.py:270
  1.1 1.3 %collective-permute-start = (bf16[1,1,2,128,256]{4,3,2,1,0:T(8,128)(2,1)S(1)}, bf16[1,1,2,128,256]{4,3,2,1,0:T(8,128)(2,1)S(1)}, u32[]{:S(2)}, u32[]{:S(2)}) collective-permute-start(bf16[1,1,2,128,256]{4,3,2,1,0:T(8,128)(2,1)S(1)} %get-tuple-element.42), channel_id=1, source_target_pairs={{8,0},{16,8},{24,16},{32,24},{40,32},{48,40},{56,48},{9,1},{17,9},... | collective-permute-start | bytes 393224 | tf_op jit(solution)/shard_map/ppermute | solution.py:273
  2.4 5.5 %collective-permute-start.1 = (bf16[1,1,2,128,256]{4,3,2,1,0:T(8,128)(2,1)S(1)}, bf16[1,1,2,128,256]{4,3,2,1,0:T(8,128)(2,1)S(1)}, u32[]{:S(2)}, u32[]{:S(2)}) collective-permute-start(bf16[1,1,2,128,256]{4,3,2,1,0:T(8,128)(2,1)S(1)} %get-tuple-element.43), channel_id=1, source_target_pairs={{0,8},{8,16},{16,24},{24,32},{32,40},{40,48},{48,56},{1,9},{9,17},... | collective-permute-start | bytes 393224 | tf_op jit(solution)/shard_map/ppermute | solution.py:274
  7.9 2.1 %collective-permute-start.4 = (bf16[1,2,1,128,256]{4,3,2,1,0:T(8,128)(2,1)S(1)}, bf16[1,2,1,128,256]{4,3,2,1,0:T(8,128)(2,1)S(1)}, u32[]{:S(2)}, u32[]{:S(2)}) collective-permute-start(bf16[1,2,1,128,256]{4,3,2,1,0:T(8,128)(2,1)S(1)} %get-tuple-element.58), channel_id=1, source_target_pairs={{0,1},{1,2},{2,3},{3,4},{4,5},{5,6},{6,7},{7,0},{8,9},{9,10},{10,1... | collective-permute-start | bytes 393224 | tf_op jit(solution)/shard_map/ppermute | solution.py:275
  10.0 3.9 %collective-permute-start.5 = (bf16[1,2,1,128,256]{4,3,2,1,0:T(8,128)(2,1)S(1)}, bf16[1,2,1,128,256]{4,3,2,1,0:T(8,128)(2,1)S(1)}, u32[]{:S(2)}, u32[]{:S(2)}) collective-permute-start(bf16[1,2,1,128,256]{4,3,2,1,0:T(8,128)(2,1)S(1)} %get-tuple-element.59), channel_id=1, source_target_pairs={{1,0},{2,1},{3,2},{4,3},{5,4},{6,5},{7,6},{0,7},{9,8},{10,9},{11,1... | collective-permute-start | bytes 393224 | tf_op jit(solution)/shard_map/ppermute | solution.py:276
  13.9 1.4 %stage.1 = (bf16[1,2,2,128,256]{4,3,2,1,0:T(8,128)(2,1)S(1)}, f32[512,256]{1,0:T(8,128)S(1)}, s32[2,2]{1,0:T(2,128)S(1)}, s32[2,2,4]{2,1,0:T(2,128)S(1)}, bf16[2...) custom-call(bf16[1,2,2,128,256]{4,3,2,1,0:T(8,128)(2,1)} %state_in.1, ...), custom_call_target="tpu_custom_call" | custom-call | bytes 8388608 | tf_op jit(solution)/shard_map/stage/pallas_call | solution.py:281
  15.4 0.0 collective-permute-done.down
  15.4 0.0 collective-permute-done.1.up
  15.4 2.9 %collective-permute-start.3 = (bf16[2,128,256]{2,1,0:T(8,128)(2,1)S(1)}, bf16[2,128,256]{2,1,0:T(8,128)(2,1)S(1)}, u32[]{:S(2)}, u32[]{:S(2)}) collective-permute-start(bf16[2,128,256]{2,1,0:T(8,128)(2,1)S(1)} %pad_maximum_fusion.1), channel_id=1, source_target_pairs={{1,0},{2,1},{3,2},{4,3},{5,4},{6,5},{7,6},{0,7},{9,8},{10,9},{11,1... | collective-permute-start | bytes 393224 | tf_op jit(solution)/shard_map/ppermute | solution.py:291
  18.4 0.0 collective-permute-start.2
  18.4 0.0 collective-permute-done.4.left
  18.4 0.0 collective-permute-done.5.right
  18.4 2.4 %near.1 = (f32[512,256]{1,0:T(8,128)S(1)}, bf16[4,128,512]{2,1,0:T(8,128)(2,1)S(1)}, f32[64,128]{1,0:T(8,128)S(1)}, bf16[4,128,128]{2,1,0:T(8,128)(2,1)S(1)}, bf...) custom-call(s32[2,2]{1,0:T(2,128)S(1)} %get-tuple-element.56.map_in, ...), custom_call_target="tpu_custom_call" | custom-call | bytes 8388608 | tf_op jit(solution)/shard_map/near/pallas_call | solution.py:293
  20.8 0.0 copy-start.6
  20.8 0.0 collective-permute-done.3.corner_r
  20.8 0.0 collective-permute-done.2.corner_l
  20.9 0.0 copy-start.3
  20.9 0.0 copy-start.4
  20.9 1.1 %fine_level.1 = (bf16[512,256]{1,0:T(8,128)(2,1)S(1)}, bf16[1152,128]{1,0:T(8,128)(2,1)S(1)}) custom-call(bf16[2,128,256]{2,1,0:T(8,128)(2,1)S(1)} %collective-permute-done.2.corner_l, bf16[2,128,256]{2,1,0:T(8,128)(2,1)S(1)} %collective-permute-done.3.corner_r, f32[512,256]{1,0:T(8,128)S(1)} %get-tuple-element.63.mixed_in, ...), custom_call_target="tpu_custom_call" | custom-call | bytes 8388608 | tf_op jit(solution)/shard_map/fine_level/pallas_call | solution.py:307
  22.0 0.0 copy-start
  22.0 0.0 copy-start.1
  22.0 0.0 copy-start.2
  22.0 0.0 copy-start.5
  22.0 21.6 %all_to_all.15 = bf16[64,9,2,128]{3,2,1,0:T(2,128)(2,1)S(1)} all-to-all(bf16[64,9,2,128]{3,2,1,0:T(2,128)(2,1)S(1)} %bitcast.15), channel_id=1, replica_groups={{62,63,54,55,46,47,38,39,30,31,22,23,14,15,6,7,60,61,52,53,44,45,36,37,..., dimensions={0} | all-to-all | bytes 589824 | tf_op jit(solution)/shard_map/all_to_all | solution.py:318
  43.6 0.0 copy-done.6
  43.6 0.6 top_sum.1
  44.2 10.8 %all_to_all.16.got = bf16[8,40,256]{2,1,0:T(8,128)(2,1)S(1)} all-to-all(bf16[8,40,256]{2,1,0:T(8,128)(2,1)S(1)} %top_sum.1), channel_id=1, replica_groups={{56,48,40,32,24,16,8,0},{57,49,41,33,25,17,9,1},{58,50,42,34,26,18,10,2..., dimensions={0} | all-to-all | bytes 327680 | tf_op jit(solution)/shard_map/all_to_all | solution.py:327
  55.0 0.2 top_order.1
  55.2 10.7 %all_to_all.17.mine = bf16[4,20,16,256]{3,2,1,0:T(8,128)(2,1)S(1)} all-to-all(bf16[4,20,16,256]{3,2,1,0:T(8,128)(2,1)S(1)} %top_order.1), channel_id=1, replica_groups={{6,4,2,0},{7,5,3,1},{14,12,10,8},{15,13,11,9},{22,20,18,16},{23,21,19,1..., dimensions={0} | all-to-all | bytes 1310720 | tf_op jit(solution)/shard_map/all_to_all | solution.py:331
  65.9 5.2 %collective-permute-start.6 = (bf16[4,20,16,256]{3,2,1,0:T(8,128)(2,1)S(1)}, bf16[4,20,16,256]{3,2,1,0:T(8,128)(2,1)S(1)}, u32[]{:S(2)}, u32[]{:S(2)}) collective-permute-start(bf16[4,20,16,256]{3,2,1,0:T(8,128)(2,1)S(1)} %all_to_all.17.mine), channel_id=1, source_target_pairs={{0,1},{1,0},{2,3},{3,2},{4,5},{5,4},{6,7},{7,6},{8,9},{9,8},{10,11... | collective-permute-start | bytes 1966088 | tf_op jit(solution)/shard_map/ppermute | solution.py:332
  71.1 0.0 copy-done.3
  71.1 0.0 copy-done.4
  71.1 0.8 %top_half.1 = (f32[512,256]{1,0:T(8,128)S(1)}, bf16[4,64,256]{2,1,0:T(8,128)(2,1)S(1)}) custom-call(s32[2,2]{1,0:T(2,128)S(1)} %copy-done.3, s32[4,20]{1,0:T(4,128)S(1)} %bitcast.16, bf16[4,20,16,256]{3,2,1,0:T(8,128)(2,1)S(1)} %all_to_all.17.mine, bf16[4,128,256]{2,1,0:T(8,128)(2,1)S(1)} %get-tuple-element.74.near), custom_call_target="tpu_custom_call" | custom-call | bytes 8388608 | tf_op jit(solution)/shard_map/top_half/pallas_call | solution.py:334
  72.0 0.8 %collective-permute-done.6.other = bf16[4,20,16,256]{3,2,1,0:T(8,128)(2,1)S(1)} collective-permute-done((bf16[4,20,16,256]{3,2,1,0:T(8,128)(2,1)S(1)}, bf16[4,20,16,256]{3,2,1,0:T(8,128)(2,1)S(1)}, u32[]{:S(2)}, u32[]{:S(2)}) %collective-permute-start.6) | collective-permute-done | bytes 655392 | tf_op jit(solution)/shard_map/ppermute | solution.py:332
  72.8 0.0 copy-done
  72.8 0.0 copy-done.1
  72.8 0.0 copy-done.2
  72.8 0.0 copy-done.5
  72.8 2.3 %top_level.1 = bf16[1,2,2,128,256]{4,3,2,1,0:T(8,128)(2,1)} custom-call(s32[2,2]{1,0:T(2,128)S(1)} %copy-done.3, s32[4,20]{1,0:T(4,128)S(1)} %bitcast.17, bf16[4,20,16,256]{3,2,1,0:T(8,128)(2,1)S(1)} %collective-permute-done.6.other, bf16[4,128,256]{2,1,0:T(8,128)(2,1)S(1)} %get-tuple-element.73.away, f32[512,256]{1,0:T(8,128)S(1)} %get-tuple-element.75.mixed, ...), custom_call_target="tpu_custom_call" | custom-call | bytes 8388608 | tf_op jit(solution)/shard_map/top_level/pallas_call | solution.py:342
  (3 shorter events, 0.0 us)
Async XLA Ops:
  1.1 14.2 %collective-permute-start = (bf16[1,1,2,128,256]{4,3,2,1,0:T(8,128)(2,1)S(1)}, bf16[1,1,2,128,256]{4,3,2,1,0:T(8,128)(2,1)S(1)}, u32[]{:S(2)}, u32[]{:S(2)}) collective-permute-start(bf16[1,1,2,128,256]{4,3,2,1,0:T(8,128)(2,1)S(1)} %get-tuple-element.42), channel_id=1, source_target_pairs={{8,0},{16,8},{24,16},{32,24},{40,32},{48,40},{56,48},{9,1},{17,9},... | collective-permute-start | bytes 393224 | tf_op jit(solution)/shard_map/ppermute | solution.py:273
  2.4 12.9 %collective-permute-start.1 = (bf16[1,1,2,128,256]{4,3,2,1,0:T(8,128)(2,1)S(1)}, bf16[1,1,2,128,256]{4,3,2,1,0:T(8,128)(2,1)S(1)}, u32[]{:S(2)}, u32[]{:S(2)}) collective-permute-start(bf16[1,1,2,128,256]{4,3,2,1,0:T(8,128)(2,1)S(1)} %get-tuple-element.43), channel_id=1, source_target_pairs={{0,8},{8,16},{16,24},{24,32},{32,40},{40,48},{48,56},{1,9},{9,17},... | collective-permute-start | bytes 393224 | tf_op jit(solution)/shard_map/ppermute | solution.py:274
  7.9 10.5 %collective-permute-start.4 = (bf16[1,2,1,128,256]{4,3,2,1,0:T(8,128)(2,1)S(1)}, bf16[1,2,1,128,256]{4,3,2,1,0:T(8,128)(2,1)S(1)}, u32[]{:S(2)}, u32[]{:S(2)}) collective-permute-start(bf16[1,2,1,128,256]{4,3,2,1,0:T(8,128)(2,1)S(1)} %get-tuple-element.58), channel_id=1, source_target_pairs={{0,1},{1,2},{2,3},{3,4},{4,5},{5,6},{6,7},{7,0},{8,9},{9,10},{10,1... | collective-permute-start | bytes 393224 | tf_op jit(solution)/shard_map/ppermute | solution.py:275
  10.0 8.5 %collective-permute-start.5 = (bf16[1,2,1,128,256]{4,3,2,1,0:T(8,128)(2,1)S(1)}, bf16[1,2,1,128,256]{4,3,2,1,0:T(8,128)(2,1)S(1)}, u32[]{:S(2)}, u32[]{:S(2)}) collective-permute-start(bf16[1,2,1,128,256]{4,3,2,1,0:T(8,128)(2,1)S(1)} %get-tuple-element.59), channel_id=1, source_target_pairs={{1,0},{2,1},{3,2},{4,3},{5,4},{6,5},{7,6},{0,7},{9,8},{10,9},{11,1... | collective-permute-start | bytes 393224 | tf_op jit(solution)/shard_map/ppermute | solution.py:276
  15.4 5.4 %collective-permute-start.3 = (bf16[2,128,256]{2,1,0:T(8,128)(2,1)S(1)}, bf16[2,128,256]{2,1,0:T(8,128)(2,1)S(1)}, u32[]{:S(2)}, u32[]{:S(2)}) collective-permute-start(bf16[2,128,256]{2,1,0:T(8,128)(2,1)S(1)} %pad_maximum_fusion.1), channel_id=1, source_target_pairs={{1,0},{2,1},{3,2},{4,3},{5,4},{6,5},{7,6},{0,7},{9,8},{10,9},{11,1... | collective-permute-start | bytes 393224 | tf_op jit(solution)/shard_map/ppermute | solution.py:291
  18.4 2.5 %collective-permute-start.2 = (bf16[2,128,256]{2,1,0:T(8,128)(2,1)S(1)}, bf16[2,128,256]{2,1,0:T(8,128)(2,1)S(1)}, u32[]{:S(2)}, u32[]{:S(2)}) collective-permute-start(bf16[2,128,256]{2,1,0:T(8,128)(2,1)S(1)} %pad_maximum_fusion), channel_id=1, source_target_pairs={{0,1},{1,2},{2,3},{3,4},{4,5},{5,6},{6,7},{7,0},{8,9},{9,10},{10,1... | collective-permute-start | bytes 393224 | tf_op jit(solution)/shard_map/ppermute | solution.py:290
  20.8 22.8 %copy-start.6 = (f32[256]{0:T(256)S(1)}, f32[256]{0:T(256)}, u32[]{:S(2)}) copy-start(f32[256]{0:T(256)} %param.32) | copy-start | bytes 3076
  20.9 50.3 %copy-start.3 = (s32[2,2]{1,0:T(2,128)S(1)}, s32[2,2]{1,0:T(2,128)}, u32[]{:S(2)}) copy-start(s32[2,2]{1,0:T(2,128)} %map_in.5) | copy-start | bytes 52
  20.9 50.3 %copy-start.4 = (s32[20,4]{0,1:T(4,128)S(1)}, s32[20,4]{0,1:T(4,128)}, u32[]{:S(2)}) copy-start(s32[20,4]{0,1:T(4,128)} %param.23) | copy-start | bytes 964
  22.0 50.9 %copy-start = (bf16[256,256]{1,0:T(8,128)(2,1)S(1)}, bf16[256,256]{1,0:T(8,128)(2,1)}, u32[]{:S(2)}) copy-start(bf16[256,256]{1,0:T(8,128)(2,1)} %w_msg.1) | copy-start | bytes 393220
  22.0 50.8 %copy-start.1 = (bf16[256,256]{1,0:T(8,128)(2,1)S(1)}, bf16[256,256]{1,0:T(8,128)(2,1)}, u32[]{:S(2)}) copy-start(bf16[256,256]{1,0:T(8,128)(2,1)} %w_agg.1) | copy-start | bytes 393220
  22.0 50.8 %copy-start.2 = (bf16[256,256]{1,0:T(8,128)(2,1)S(1)}, bf16[256,256]{1,0:T(8,128)(2,1)}, u32[]{:S(2)}) copy-start(bf16[256,256]{1,0:T(8,128)(2,1)} %w_down.1) | copy-start | bytes 393220
  22.0 50.8 %copy-start.5 = (f32[256]{0:T(256)S(1)}, f32[256]{0:T(256)}, u32[]{:S(2)}) copy-start(f32[256]{0:T(256)} %param.33) | copy-start | bytes 3076
  65.9 6.9 %collective-permute-start.6 = (bf16[4,20,16,256]{3,2,1,0:T(8,128)(2,1)S(1)}, bf16[4,20,16,256]{3,2,1,0:T(8,128)(2,1)S(1)}, u32[]{:S(2)}, u32[]{:S(2)}) collective-permute-start(bf16[4,20,16,256]{3,2,1,0:T(8,128)(2,1)S(1)} %all_to_all.17.mine), channel_id=1, source_target_pairs={{0,1},{1,0},{2,3},{3,2},{4,5},{5,4},{6,7},{7,6},{8,9},{9,8},{10,11... | collective-permute-start | bytes 1966088 | tf_op jit(solution)/shard_map/ppermute | solution.py:332

commit v5 on v4

--- a/solution.py
+++ b/solution.py
@@ -69,11 +69,14 @@
 
 
 def near_kernel(
-    map_in, nbr_in, up, down, left, right, state, adj, tiles, top_adj,
-    mixed, corner_edges, label, sent, turned, near, away, frame, up_map, nbr, edges, sems,
+    up_map, nbr, up, down, right, left, state, adj, tiles, top_nbr_in, top_adj,
+    mixed, corner_edges, label, sent, turned, near, away, picks, frame, top_nbr, edges, sems,
     *, core_axis,
 ):
-    copies = start_all([(map_in, up_map), (nbr_in, nbr)], sems)
+    table = pltpu.make_async_copy(top_nbr_in, top_nbr, sems.at[4])
+    table.start()
+    joins = [up_map[...][b // 2, b % 2] for b in range(4)]
+    copies = start_all([(top_adj.at[joins[b]], edges.at[b]) for b in range(4)], sems)
     for c in range(2):
         frame[1 + c] = up[0, 0, c]
         frame[13 + c] = down[0, 0, c]
@@ -84,16 +87,12 @@
         frame[(1 + r) * 4 + 3] = right[0, r, 0]
         frame[12 * r] = jnp.zeros((128, 256), BF16)
         frame[12 * r + 3] = jnp.zeros((128, 256), BF16)
-    for copy in copies:
-        copy.wait()
-    pairs = [(top_adj.at[up_map[b // 2, b % 2]], edges.at[b]) for b in range(4)]
-    copies = start_all(pairs, sems.at[pl.ds(2, 4)])
     lane = lax.broadcasted_iota(jnp.int32, (64, 128), 1)
     block = lane >> 5
     joined = jnp.where(
         block < 2,
-        jnp.where(block == 0, up_map[0, 0], up_map[0, 1]),
-        jnp.where(block == 2, up_map[1, 0], up_map[1, 1]),
+        jnp.where(block == 0, joins[0], joins[1]),
+        jnp.where(block == 2, joins[2], joins[3]),
     )
     label[...] = jnp.where((lane & 31) == joined, 1.0, 0.0)
     row = lax.broadcasted_iota(jnp.int32, (128, 128), 0)
@@ -105,7 +104,7 @@
             b = 2 * y + x
             picked = []
             for k in range(4):
-                code = nbr[y, x, k]
+                code = nbr[y][x, k]
                 spot = (y + lax.div(code, 3)) * 4 + x + lax.rem(code, 3)
                 picked.append(frame[spot])
                 tile = adj[y, x, k]
@@ -122,6 +121,12 @@
         high = jnp.concatenate([edges[b, k][:, 64:] for k in range(4)], axis=1)
         near[b] = jnp.where(core == 0, low, high)
         away[b] = jnp.where(core == 0, high, low)
+    table.wait()
+    for b in range(4):
+        picks[pl.ds(b, 1), :] = jnp.full((1, 128), joins[b], jnp.int32)
+        for k in range(4):
+            source = jnp.full((1, 128), top_nbr[k, joins[b]], jnp.int32)
+            picks[pl.ds(4 + 4 * b + k, 1), :] = source
 
 
 def fine_kernel(
@@ -189,38 +194,35 @@
     return jnp.concatenate([source[x, at] for x in range(4)], axis=0)
 
 
-def gather_parts(up_map, top_nbr, edges, source):
+def pick(picks, line):
+    return picks[pl.ds(line, 1), pl.ds(0, 1)][0, 0]
+
+
+def gather_parts(picks, edges, source):
     mixed = []
     for b in range(4):
-        at = up_map[b // 2, b % 2]
-        picked = jnp.concatenate([half_block(source, top_nbr[k, at]) for k in range(4)], axis=0)
-        mixed.append(dot(edges[b], picked))
+        picked = [half_block(source, pick(picks, 4 + 4 * b + k)) for k in range(4)]
+        mixed.append(dot(edges[b], jnp.concatenate(picked, axis=0)))
     return jnp.concatenate(mixed, axis=0)
 
 
-def half_kernel(map_in, nbr_in, mine, near, mixed, chosen, up_map, top_nbr, sems):
-    for copy in start_all([(map_in, up_map), (nbr_in, top_nbr)], sems):
-        copy.wait()
-    for b in range(4):
-        chosen[b] = half_block(mine, up_map[b // 2, b % 2])
-    mixed[...] = gather_parts(up_map, top_nbr, near, mine)
+def half_kernel(picks, mine, near, mixed, chosen):
+    for b in range(4):
+        chosen[b] = half_block(mine, pick(picks, b))
+    mixed[...] = gather_parts(picks, near, mine)
 
 
 def top_kernel(
-    map_in, nbr_in, other, away, mixed, chosen, fine, turned, w_msg, w_agg, w_down, gain,
-    out, whole, up_map, top_nbr, sems, *, core_axis,
-):
-    copies = start_all([(map_in, up_map), (nbr_in, top_nbr)], sems)
+    picks, other, away, mixed, chosen, fine, turned, w_msg, w_agg, w_down, gain,
+    out, whole, sems, *, core_axis,
+):
     core = lax.axis_index(core_axis)
     here = pl.ds(pl.multiple_of(core * 64, 64), 64)
     there = pl.ds(pl.multiple_of((1 - core) * 64, 64), 64)
     for b in range(4):
         whole[b, here, :] = chosen[b]
-    for copy in copies:
-        copy.wait()
-    for b in range(4):
-        whole[b, there, :] = half_block(other, up_map[b // 2, b % 2])
-    both = mixed[...] + gather_parts(up_map, top_nbr, away, other)
+        whole[b, there, :] = half_block(other, pick(picks, b))
+    both = mixed[...] + gather_parts(picks, away, other)
     tagg = dot(both.astype(BF16), w_msg[...]).astype(BF16)
     zero = jnp.concatenate([whole[b] for b in range(4)], axis=0).astype(F32)
     one = (zero + jax.nn.silu(dot(tagg, w_agg[...]))).astype(BF16)
@@ -230,7 +232,7 @@
         lower = dot(turned[b // 2, b % 2], one[rows]).astype(BF16)
         final = norm(fine[rows].astype(F32) + dot(lower, w_down[...]), gain[...])
         whole[b] = final.astype(BF16)
-        copy = pltpu.make_async_copy(whole.at[b], out.at[0, b // 2, b % 2], sems.at[2 + b])
+        copy = pltpu.make_async_copy(whole.at[b], out.at[0, b // 2, b % 2], sems.at[b])
         copy.start()
         copies.append(copy)
     for copy in copies:
@@ -290,20 +292,20 @@
     corner_l = lax.ppermute(jnp.concatenate([down[0, :, 1], up[0, :, 1]]), sx, east)
     corner_r = lax.ppermute(jnp.concatenate([down[0, :, 0], up[0, :, 0]]), sx, west)
     state, own_part, map_here, nbr_here, adj, tiles, *weights = held
-    mixed, corner_edges, label, sent, turned, near, away = call(
+    mixed, corner_edges, label, sent, turned, near, away, picks = call(
         functools.partial(near_kernel, core_axis="core"),
-        [VMEM] * 9 + [HBM],
+        [VMEM] * 9 + [HBM] * 2,
         [
             part, ((4, 128, 512), BF16), ((64, 128), F32), ((4, 128, 128), BF16), tile_set,
-            half_set, half_set,
+            half_set, half_set, ((32, 128), jnp.int32),
         ],
         [
-            pltpu.VMEM((16, 128, 256), BF16), pltpu.SMEM((2, 2), jnp.int32),
-            pltpu.SMEM((2, 2, 4), jnp.int32), pltpu.VMEM((4, 4, 128, 128), BF16), dma((6,)),
+            pltpu.VMEM((16, 128, 256), BF16), pltpu.SMEM((4, 20), jnp.int32),
+            pltpu.VMEM((4, 4, 128, 128), BF16), dma((5,)),
         ],
         "near",
         1 << 23,
-    )(map_here, nbr_here, up, down, left, right, state, adj, tiles, far(top_adj))
+    )(map_here, nbr_here, up, down, right, left, state, adj, tiles, far(top_nbr.T), far(top_adj))
     fine, piece = call(
         fine_kernel,
         [VMEM] * 12,
@@ -330,26 +332,20 @@
     )(column)
     mine = lax.all_to_all(column, "x", 0, 0, axis_index_groups=[list(range(cols // 2 - 1, -1, -1))])
     other = lax.ppermute(mine, "core", twin)
-    tables = [pltpu.SMEM((2, 2), jnp.int32), pltpu.SMEM((4, 20), jnp.int32)]
     mixed, chosen = call(
-        half_kernel,
-        [HBM] * 2 + [VMEM] * 2,
-        [part, ((4, 64, 256), BF16)],
-        tables + [dma((2,))],
-        "top_half",
-        1 << 23,
-    )(up_map, top_nbr.T, mine, near)
+        half_kernel, [VMEM] * 3, [part, ((4, 64, 256), BF16)], [], "top_half", 1 << 23
+    )(picks, mine, near)
     (out,) = call(
         functools.partial(top_kernel, core_axis="core"),
-        [HBM] * 2 + [VMEM] * 10,
+        [VMEM] * 11,
         [(fine_state.shape, BF16)],
-        [pltpu.VMEM(*half_set)] + tables + [dma((6,))],
+        [pltpu.VMEM(*half_set), dma((4,))],
         "top_level",
         1 << 23,
         place=HBM,
     )(
-        up_map, top_nbr.T, other, away, mixed, chosen, fine, turned, w_top_msg, w_top_agg,
-        w_down, out_gain[None],
+        picks, other, away, mixed, chosen, fine, turned, w_top_msg, w_top_agg, w_down,
+        out_gain[None],
     )
     return out
 

time: 75.4 us -> 74.5 us (0.988)
  waiting for transfers between devices: 0.85 us -> 3.21 us
  Pallas kernels: 9.89 us -> 7.96 us
  starting transfers between devices: 20.9 us -> 19 us
    ppermute x1, starting transfers between devices: 2.06 us -> 0.01 us  [local(): left = lax.ppermute(last_col, sx, east)]
    ppermute x1, starting transfers between devices: 3.94 us -> 5.98 us  [local(): right = lax.ppermute(first_col, sx, west)]
    ppermute x1, starting transfers between devices: 2.94 us -> 1.02 us  [local(): lax.ppermute(jnp.concatenate([down[0, :, 0], up[0, :, 0]]), sx, west)]
    ppermute x1, waiting for transfers between devices: 0.01 us -> 1.78 us  [local(): lax.ppermute(jnp.concatenate([down[0, :, 0], up[0, :, 0]]), sx, west)]
    pallas_call x2, Pallas kernels: 3.11 us -> 1.98 us  [the longest x1 1.7 us: local(): call(functools.partial(top_kernel, core_axis='core'), [VMEM] * 11, [(fine...]
    pallas_call x1, Pallas kernels: 2.38 us -> 1.57 us  [local(): call(functools.partial(near_kernel, core_axis='core'), [VMEM] * 9 + [HBM]...]
  transfers between devices with their start and end apart: 7 -> 7, of which waited for: 1 -> 2; matrix products, arithmetic and copies ran while one was open for 0% -> 0% of each run, Pallas kernels for 6% -> 4%
where the time goes in v5:
time: 74.5 us; the launch traced here: 74.1 us
  blocking collectives  43.7 us (59%)
  starting transfers between devices  19 us (26%)
  Pallas kernels  7.96 us (11%)
  waiting for transfers between devices  3.21 us (4%)
    all_to_all x1, blocking collectives, local(): lax.all_to_all(piece, ('x', 'sy', 'core'), 0, 0, axis_index_groups=[back])  22.2 us
    all_to_all x1, blocking collectives, local(): lax.all_to_all(share, 'sy', 0, 0, axis_index_groups=[list(range(rows - 1,...  10.8 us
    all_to_all x1, blocking collectives, local(): lax.all_to_all(column, 'x', 0, 0, axis_index_groups=[list(range(cols // 2...  10.7 us
    ppermute x1, starting transfers between devices, local(): right = lax.ppermute(first_col, sx, west)  5.98 us
    ppermute x1, starting transfers between devices, local(): up = lax.ppermute(last_row, 'sy', south)  5.46 us
    ppermute x1, starting transfers between devices, local(): other = lax.ppermute(mine, 'core', twin)  5.2 us
    ppermute x1, waiting for transfers between devices, local(): lax.ppermute(jnp.concatenate([down[0, :, 0], up[0, :, 0]]), sx, west)  1.78 us
    pallas_call x1, Pallas kernels, local(): call(functools.partial(top_kernel, core_axis='core'), [VMEM] * 11, [(fine...  1.7 us
  transfers between devices with their start and end apart: 7, of which 2 were waited for; matrix products, arithmetic and copies ran while one was open for 0% of the time, Pallas kernels for 4%

profile of v5, /device:TPU:1, one launch (start us, length us, event | category | flops | bytes accessed | tf_op | source)
XLA Modules:
  0.0 74.1 jit_solution(8999445707299596821)
XLA Ops:
  0.0 1.1 %cut.1 = (bf16[1,1,2,128,256]{4,3,2,1,0:T(8,128)(2,1)S(1)}, bf16[1,1,2,128,256]{4,3,2,1,0:T(8,128)(2,1)S(1)}, bf16[1,2,1,128,256]{4,3,2,1,0:T(8,128)(2,1)S(1)}, bf16[1,2,1,128,256]{4,3,2,1,0:T(8,128)(2,1)S(1)}) custom-call(bf16[1,2,2,128,256]{4,3,2,1,0:T(8,128)(2,1)} %state_in.1), custom_call_target="tpu_custom_call" | custom-call | bytes 1048576 | tf_op jit(solution)/shard_map/cut/pallas_call | solution.py:272
  1.1 1.3 %collective-permute-start = (bf16[1,1,2,128,256]{4,3,2,1,0:T(8,128)(2,1)S(1)}, bf16[1,1,2,128,256]{4,3,2,1,0:T(8,128)(2,1)S(1)}, u32[]{:S(2)}, u32[]{:S(2)}) collective-permute-start(bf16[1,1,2,128,256]{4,3,2,1,0:T(8,128)(2,1)S(1)} %get-tuple-element.43), channel_id=1, source_target_pairs={{8,0},{16,8},{24,16},{32,24},{40,32},{48,40},{56,48},{9,1},{17,9},... | collective-permute-start | bytes 393224 | tf_op jit(solution)/shard_map/ppermute | solution.py:275
  2.4 5.5 %collective-permute-start.1 = (bf16[1,1,2,128,256]{4,3,2,1,0:T(8,128)(2,1)S(1)}, bf16[1,1,2,128,256]{4,3,2,1,0:T(8,128)(2,1)S(1)}, u32[]{:S(2)}, u32[]{:S(2)}) collective-permute-start(bf16[1,1,2,128,256]{4,3,2,1,0:T(8,128)(2,1)S(1)} %get-tuple-element.44), channel_id=1, source_target_pairs={{0,8},{8,16},{16,24},{24,32},{32,40},{40,48},{48,56},{1,9},{9,17},... | collective-permute-start | bytes 393224 | tf_op jit(solution)/shard_map/ppermute | solution.py:276
  7.9 6.0 %collective-permute-start.2 = (bf16[1,2,1,128,256]{4,3,2,1,0:T(8,128)(2,1)S(1)}, bf16[1,2,1,128,256]{4,3,2,1,0:T(8,128)(2,1)S(1)}, u32[]{:S(2)}, u32[]{:S(2)}) collective-permute-start(bf16[1,2,1,128,256]{4,3,2,1,0:T(8,128)(2,1)S(1)} %get-tuple-element.59), channel_id=1, source_target_pairs={{1,0},{2,1},{3,2},{4,3},{5,4},{6,5},{7,6},{0,7},{9,8},{10,9},{11,1... | collective-permute-start | bytes 393224 | tf_op jit(solution)/shard_map/ppermute | solution.py:278
  13.9 0.0 collective-permute-start.3
  13.9 1.4 %stage.1 = (bf16[1,2,2,128,256]{4,3,2,1,0:T(8,128)(2,1)S(1)}, f32[512,256]{1,0:T(8,128)S(1)}, s32[2,2]{1,0:T(2,128)S(1)}, s32[2,2,4]{2,1,0:T(2,128)S(1)}, bf16[2...) custom-call(bf16[1,2,2,128,256]{4,3,2,1,0:T(8,128)(2,1)} %state_in.1, ...), custom_call_target="tpu_custom_call" | custom-call | bytes 8388608 | tf_op jit(solution)/shard_map/stage/pallas_call | solution.py:283
  15.3 0.0 collective-permute-done.down
  15.3 0.0 collective-permute-done.1.up
  15.4 0.0 collective-permute-start.4
  15.5 1.0 %collective-permute-start.5 = (bf16[2,128,256]{2,1,0:T(8,128)(2,1)S(1)}, bf16[2,128,256]{2,1,0:T(8,128)(2,1)S(1)}, u32[]{:S(2)}, u32[]{:S(2)}) collective-permute-start(bf16[2,128,256]{2,1,0:T(8,128)(2,1)S(1)} %pad_maximum_fusion.1), channel_id=1, source_target_pairs={{1,0},{2,1},{3,2},{4,3},{5,4},{6,5},{7,6},{0,7},{9,8},{10,9},{11,1... | collective-permute-start | bytes 393224 | tf_op jit(solution)/shard_map/ppermute | solution.py:293
  16.5 0.0 collective-permute-done.2.right
  16.5 0.0 collective-permute-done.3.left
  16.5 1.6 %near.1 = (f32[512,256]{1,0:T(8,128)S(1)}, bf16[4,128,512]{2,1,0:T(8,128)(2,1)S(1)}, f32[64,128]{1,0:T(8,128)S(1)}, bf16[4,128,128]{2,1,0:T(8,128)(2,1)S(1)}, bf...) custom-call(s32[2,2]{1,0:T(2,128)S(1)} %get-tuple-element.55.up_map,, ...), custom_call_target="tpu_custom_call" | custom-call | bytes 8388608 | tf_op jit(solution)/shard_map/near/pallas_call | solution.py:295
  18.1 0.0 copy-start.3
  18.1 0.0 collective-permute-done.4.corner_l
  18.1 1.8 %collective-permute-done.5.corner_r = bf16[2,128,256]{2,1,0:T(8,128)(2,1)S(1)} collective-permute-done((bf16[2,128,256]{2,1,0:T(8,128)(2,1)S(1)}, bf16[2,128,256]{2,1,0:T(8,128)(2,1)S(1)}, u32[]{:S(2)}, u32[]{:S(2)}) %collective-permute-start.5) | collective-permute-done | bytes 131104 | tf_op jit(solution)/shard_map/ppermute | solution.py:293
  19.9 1.1 %fine_level.1 = (bf16[512,256]{1,0:T(8,128)(2,1)S(1)}, bf16[1152,128]{1,0:T(8,128)(2,1)S(1)}) custom-call(bf16[2,128,256]{2,1,0:T(8,128)(2,1)S(1)} %collective-permute-done.4.corner_l, bf16[2,128,256]{2,1,0:T(8,128)(2,1)S(1)} %collective-permute-done.5.corner_r, f32[512,256]{1,0:T(8,128)S(1)} %get-tuple-element.65.mixed_in, ...), custom_call_target="tpu_custom_call" | custom-call | bytes 8388608 | tf_op jit(solution)/shard_map/fine_level/pallas_call | solution.py:309
  21.0 0.0 copy-start
  21.0 0.0 copy-start.1
  21.0 0.0 copy-start.2
  21.0 0.0 copy-start.4
  21.0 22.2 %all_to_all.15 = bf16[64,9,2,128]{3,2,1,0:T(2,128)(2,1)S(1)} all-to-all(bf16[64,9,2,128]{3,2,1,0:T(2,128)(2,1)S(1)} %bitcast.15), channel_id=1, replica_groups={{62,63,54,55,46,47,38,39,30,31,22,23,14,15,6,7,60,61,52,53,44,45,36,37,..., dimensions={0} | all-to-all | bytes 589824 | tf_op jit(solution)/shard_map/all_to_all | solution.py:320
  43.2 0.0 copy-done.3
  43.2 0.6 top_sum.1
  43.8 10.8 %all_to_all.16.got = bf16[8,40,256]{2,1,0:T(8,128)(2,1)S(1)} all-to-all(bf16[8,40,256]{2,1,0:T(8,128)(2,1)S(1)} %top_sum.1), channel_id=1, replica_groups={{56,48,40,32,24,16,8,0},{57,49,41,33,25,17,9,1},{58,50,42,34,26,18,10,2..., dimensions={0} | all-to-all | bytes 327680 | tf_op jit(solution)/shard_map/all_to_all | solution.py:329
  54.6 0.2 top_order.1
  54.8 10.7 %all_to_all.17.mine = bf16[4,20,16,256]{3,2,1,0:T(8,128)(2,1)S(1)} all-to-all(bf16[4,20,16,256]{3,2,1,0:T(8,128)(2,1)S(1)} %top_order.1), channel_id=1, replica_groups={{6,4,2,0},{7,5,3,1},{14,12,10,8},{15,13,11,9},{22,20,18,16},{23,21,19,1..., dimensions={0} | all-to-all | bytes 1310720 | tf_op jit(solution)/shard_map/all_to_all | solution.py:333
  65.5 5.2 %collective-permute-start.6 = (bf16[4,20,16,256]{3,2,1,0:T(8,128)(2,1)S(1)}, bf16[4,20,16,256]{3,2,1,0:T(8,128)(2,1)S(1)}, u32[]{:S(2)}, u32[]{:S(2)}) collective-permute-start(bf16[4,20,16,256]{3,2,1,0:T(8,128)(2,1)S(1)} %all_to_all.17.mine), channel_id=1, source_target_pairs={{0,1},{1,0},{2,3},{3,2},{4,5},{5,4},{6,7},{7,6},{8,9},{9,8},{10,11... | collective-permute-start | bytes 1966088 | tf_op jit(solution)/shard_map/ppermute | solution.py:334
  70.7 0.3 top_half.1
  71.0 1.4 %collective-permute-done.6.other = bf16[4,20,16,256]{3,2,1,0:T(8,128)(2,1)S(1)} collective-permute-done((bf16[4,20,16,256]{3,2,1,0:T(8,128)(2,1)S(1)}, bf16[4,20,16,256]{3,2,1,0:T(8,128)(2,1)S(1)}, u32[]{:S(2)}, u32[]{:S(2)}) %collective-permute-start.6) | collective-permute-done | bytes 655392 | tf_op jit(solution)/shard_map/ppermute | solution.py:334
  72.4 0.0 copy-done
  72.4 0.0 copy-done.1
  72.4 0.0 copy-done.2
  72.4 0.0 copy-done.4
  72.4 1.7 %top_level.1 = bf16[1,2,2,128,256]{4,3,2,1,0:T(8,128)(2,1)} custom-call(s32[32,128]{1,0:T(8,128)S(1)} %get-tuple-element.64.picks, bf16[4,20,16,256]{3,2,1,0:T(8,128)(2,1)S(1)} %collective-permute-done.6.other, bf16[4,128,256]{2,1,0:T(8,128)(2,1)S(1)} %get-tuple-element.75.away, f32[512,256]{1,0:T(8,128)S(1)} %get-tuple-element.77.mixed, ...), custom_call_target="tpu_custom_call" | custom-call | bytes 8388608 | tf_op jit(solution)/shard_map/top_level/pallas_call | solution.py:338
  (3 shorter events, 0.1 us)
Async XLA Ops:
  1.1 14.2 %collective-permute-start = (bf16[1,1,2,128,256]{4,3,2,1,0:T(8,128)(2,1)S(1)}, bf16[1,1,2,128,256]{4,3,2,1,0:T(8,128)(2,1)S(1)}, u32[]{:S(2)}, u32[]{:S(2)}) collective-permute-start(bf16[1,1,2,128,256]{4,3,2,1,0:T(8,128)(2,1)S(1)} %get-tuple-element.43), channel_id=1, source_target_pairs={{8,0},{16,8},{24,16},{32,24},{40,32},{48,40},{56,48},{9,1},{17,9},... | collective-permute-start | bytes 393224 | tf_op jit(solution)/shard_map/ppermute | solution.py:275
  2.4 12.9 %collective-permute-start.1 = (bf16[1,1,2,128,256]{4,3,2,1,0:T(8,128)(2,1)S(1)}, bf16[1,1,2,128,256]{4,3,2,1,0:T(8,128)(2,1)S(1)}, u32[]{:S(2)}, u32[]{:S(2)}) collective-permute-start(bf16[1,1,2,128,256]{4,3,2,1,0:T(8,128)(2,1)S(1)} %get-tuple-element.44), channel_id=1, source_target_pairs={{0,8},{8,16},{16,24},{24,32},{32,40},{40,48},{48,56},{1,9},{9,17},... | collective-permute-start | bytes 393224 | tf_op jit(solution)/shard_map/ppermute | solution.py:276
  7.9 8.6 %collective-permute-start.2 = (bf16[1,2,1,128,256]{4,3,2,1,0:T(8,128)(2,1)S(1)}, bf16[1,2,1,128,256]{4,3,2,1,0:T(8,128)(2,1)S(1)}, u32[]{:S(2)}, u32[]{:S(2)}) collective-permute-start(bf16[1,2,1,128,256]{4,3,2,1,0:T(8,128)(2,1)S(1)} %get-tuple-element.59), channel_id=1, source_target_pairs={{1,0},{2,1},{3,2},{4,3},{5,4},{6,5},{7,6},{0,7},{9,8},{10,9},{11,1... | collective-permute-start | bytes 393224 | tf_op jit(solution)/shard_map/ppermute | solution.py:278
  13.9 2.6 %collective-permute-start.3 = (bf16[1,2,1,128,256]{4,3,2,1,0:T(8,128)(2,1)S(1)}, bf16[1,2,1,128,256]{4,3,2,1,0:T(8,128)(2,1)S(1)}, u32[]{:S(2)}, u32[]{:S(2)}) collective-permute-start(bf16[1,2,1,128,256]{4,3,2,1,0:T(8,128)(2,1)S(1)} %get-tuple-element.60), channel_id=1, source_target_pairs={{0,1},{1,2},{2,3},{3,4},{4,5},{5,6},{6,7},{7,0},{8,9},{9,10},{10,1... | collective-permute-start | bytes 393224 | tf_op jit(solution)/shard_map/ppermute | solution.py:277
  15.4 2.7 %collective-permute-start.4 = (bf16[2,128,256]{2,1,0:T(8,128)(2,1)S(1)}, bf16[2,128,256]{2,1,0:T(8,128)(2,1)S(1)}, u32[]{:S(2)}, u32[]{:S(2)}) collective-permute-start(bf16[2,128,256]{2,1,0:T(8,128)(2,1)S(1)} %pad_maximum_fusion), channel_id=1, source_target_pairs={{0,1},{1,2},{2,3},{3,4},{4,5},{5,6},{6,7},{7,0},{8,9},{9,10},{10,1... | collective-permute-start | bytes 393224 | tf_op jit(solution)/shard_map/ppermute | solution.py:292
  15.5 4.4 %collective-permute-start.5 = (bf16[2,128,256]{2,1,0:T(8,128)(2,1)S(1)}, bf16[2,128,256]{2,1,0:T(8,128)(2,1)S(1)}, u32[]{:S(2)}, u32[]{:S(2)}) collective-permute-start(bf16[2,128,256]{2,1,0:T(8,128)(2,1)S(1)} %pad_maximum_fusion.1), channel_id=1, source_target_pairs={{1,0},{2,1},{3,2},{4,3},{5,4},{6,5},{7,6},{0,7},{9,8},{10,9},{11,1... | collective-permute-start | bytes 393224 | tf_op jit(solution)/shard_map/ppermute | solution.py:293
  18.1 25.1 %copy-start.3 = (f32[256]{0:T(256)S(1)}, f32[256]{0:T(256)}, u32[]{:S(2)}) copy-start(f32[256]{0:T(256)} %param.32) | copy-start | bytes 3076
  21.0 51.5 %copy-start = (bf16[256,256]{1,0:T(8,128)(2,1)S(1)}, bf16[256,256]{1,0:T(8,128)(2,1)}, u32[]{:S(2)}) copy-start(bf16[256,256]{1,0:T(8,128)(2,1)} %w_msg.1) | copy-start | bytes 393220
  21.0 51.5 %copy-start.1 = (bf16[256,256]{1,0:T(8,128)(2,1)S(1)}, bf16[256,256]{1,0:T(8,128)(2,1)}, u32[]{:S(2)}) copy-start(bf16[256,256]{1,0:T(8,128)(2,1)} %w_agg.1) | copy-start | bytes 393220
  21.0 51.5 %copy-start.2 = (bf16[256,256]{1,0:T(8,128)(2,1)S(1)}, bf16[256,256]{1,0:T(8,128)(2,1)}, u32[]{:S(2)}) copy-start(bf16[256,256]{1,0:T(8,128)(2,1)} %w_down.1) | copy-start | bytes 393220
  21.0 51.4 %copy-start.4 = (f32[256]{0:T(256)S(1)}, f32[256]{0:T(256)}, u32[]{:S(2)}) copy-start(f32[256]{0:T(256)} %param.33) | copy-start | bytes 3076
  65.5 6.9 %collective-permute-start.6 = (bf16[4,20,16,256]{3,2,1,0:T(8,128)(2,1)S(1)}, bf16[4,20,16,256]{3,2,1,0:T(8,128)(2,1)S(1)}, u32[]{:S(2)}, u32[]{:S(2)}) collective-permute-start(bf16[4,20,16,256]{3,2,1,0:T(8,128)(2,1)S(1)} %all_to_all.17.mine), channel_id=1, source_target_pairs={{0,1},{1,0},{2,3},{3,2},{4,5},{5,4},{6,7},{7,6},{8,9},{9,8},{10,11... | collective-permute-start | bytes 1966088 | tf_op jit(solution)/shard_map/ppermute | solution.py:334

commit v6 on v5

--- a/solution.py
+++ b/solution.py
@@ -39,14 +39,22 @@
     return copies
 
 
-def cut_kernel(state, last_row, first_row, last_col, first_col, sems):
-    pairs = [
-        (state.at[:, 1:2], last_row),
-        (state.at[:, 0:1], first_row),
-        (state.at[:, :, 1:2], last_col),
-        (state.at[:, :, 0:1], first_col),
-    ]
-    for copy in start_all(pairs, sems):
+def cut_kernel(state, map_in, last_row, first_row, last_col, first_col, up_map, sems):
+    pairs = [(map_in, up_map), (state.at[:, 1:2], last_row), (state.at[:, 0:1], first_row)]
+    for r in range(2):
+        pairs.append((state.at[0, r, 1], last_col.at[pl.ds(128 * r, 128)]))
+        pairs.append((state.at[0, r, 0], first_col.at[pl.ds(128 * r, 128)]))
+    copies = start_all(pairs, sems)
+    copies[0].wait()
+    joins = up_map[...]
+    line = lax.broadcasted_iota(jnp.int32, (16, 256), 0)
+    value = jnp.zeros((16, 256), jnp.int32)
+    for b in range(4):
+        value = jnp.where(line == b, joins[b // 2, b % 2], value)
+    value = value.astype(F32).astype(BF16)
+    last_col[256:272, :] = value
+    first_col[256:272, :] = value
+    for copy in copies[1:]:
         copy.wait()
 
 
@@ -70,21 +78,25 @@
 
 def near_kernel(
     up_map, nbr, up, down, right, left, state, adj, tiles, top_nbr_in, top_adj,
-    mixed, corner_edges, label, sent, turned, near, away, picks, frame, top_nbr, edges, sems,
+    mixed, corner_edges, label, sent, turned, keep, give, picks, frame, top_nbr, edges, sems,
     *, core_axis,
 ):
-    table = pltpu.make_async_copy(top_nbr_in, top_nbr, sems.at[4])
+    table = pltpu.make_async_copy(top_nbr_in, top_nbr, sems.at[8])
     table.start()
+    core = lax.axis_index(core_axis)
     joins = [up_map[...][b // 2, b % 2] for b in range(4)]
-    copies = start_all([(top_adj.at[joins[b]], edges.at[b]) for b in range(4)], sems)
+    twin = jnp.where(core == 0, right[256:272, :].astype(F32), left[256:272, :].astype(F32))
+    twin = twin.astype(jnp.int32)
+    joins += [twin[b, 0] for b in range(4)]
+    copies = start_all([(top_adj.at[joins[b]], edges.at[b]) for b in range(8)], sems)
     for c in range(2):
         frame[1 + c] = up[0, 0, c]
         frame[13 + c] = down[0, 0, c]
         for r in range(2):
             frame[(1 + r) * 4 + 1 + c] = state[0, r, c]
     for r in range(2):
-        frame[(1 + r) * 4] = left[0, r, 0]
-        frame[(1 + r) * 4 + 3] = right[0, r, 0]
+        frame[(1 + r) * 4] = left[128 * r : 128 * r + 128, :]
+        frame[(1 + r) * 4 + 3] = right[128 * r : 128 * r + 128, :]
         frame[12 * r] = jnp.zeros((128, 256), BF16)
         frame[12 * r + 3] = jnp.zeros((128, 256), BF16)
     lane = lax.broadcasted_iota(jnp.int32, (64, 128), 1)
@@ -112,21 +124,20 @@
                 corner_edges[b, :, 128 * k : 128 * k + 128] = corner
             tile_row = jnp.concatenate([adj[y, x, k] for k in range(4)], axis=1)
             mixed[128 * b : 128 * b + 128] = dot(tile_row, jnp.concatenate(picked, axis=0))
-    core = lax.axis_index(core_axis)
     for b in range(4):
         turned[b // 2, b % 2] = tiles[b // 2, b % 2].T
         sent[b] = dot(order, tiles[b // 2, b % 2]).astype(BF16)
+    for b in range(8):
         copies[b].wait()
         low = jnp.concatenate([edges[b, k][:, :64] for k in range(4)], axis=1)
         high = jnp.concatenate([edges[b, k][:, 64:] for k in range(4)], axis=1)
-        near[b] = jnp.where(core == 0, low, high)
-        away[b] = jnp.where(core == 0, high, low)
+        (keep if b < 4 else give)[b % 4] = jnp.where(core == 1, low, high)
     table.wait()
-    for b in range(4):
+    for b in range(8):
         picks[pl.ds(b, 1), :] = jnp.full((1, 128), joins[b], jnp.int32)
         for k in range(4):
             source = jnp.full((1, 128), top_nbr[k, joins[b]], jnp.int32)
-            picks[pl.ds(4 + 4 * b + k, 1), :] = source
+            picks[pl.ds(8 + 4 * b + k, 1), :] = source
 
 
 def fine_kernel(
@@ -198,31 +209,37 @@
     return picks[pl.ds(line, 1), pl.ds(0, 1)][0, 0]
 
 
-def gather_parts(picks, edges, source):
+def gather_parts(picks, first, edges, source):
     mixed = []
     for b in range(4):
-        picked = [half_block(source, pick(picks, 4 + 4 * b + k)) for k in range(4)]
+        lines = [8 + 4 * (first + b) + k for k in range(4)]
+        picked = [half_block(source, pick(picks, line)) for line in lines]
         mixed.append(dot(edges[b], jnp.concatenate(picked, axis=0)))
     return jnp.concatenate(mixed, axis=0)
 
 
-def half_kernel(picks, mine, near, mixed, chosen):
+def give_kernel(picks, mine, give, parcel):
+    for b in range(4):
+        parcel[512 + 64 * b : 576 + 64 * b, :] = half_block(mine, pick(picks, 4 + b))
+    parcel[0:512, :] = gather_parts(picks, 4, give, mine).astype(BF16)
+
+
+def keep_kernel(picks, mine, keep, mixed, chosen):
     for b in range(4):
         chosen[b] = half_block(mine, pick(picks, b))
-    mixed[...] = gather_parts(picks, near, mine)
+    mixed[...] = gather_parts(picks, 0, keep, mine)
 
 
 def top_kernel(
-    picks, other, away, mixed, chosen, fine, turned, w_msg, w_agg, w_down, gain,
-    out, whole, sems, *, core_axis,
+    parcel, mixed, chosen, fine, turned, w_msg, w_agg, w_down, gain, out, whole, sems, *, core_axis
 ):
     core = lax.axis_index(core_axis)
-    here = pl.ds(pl.multiple_of(core * 64, 64), 64)
-    there = pl.ds(pl.multiple_of((1 - core) * 64, 64), 64)
+    here = pl.ds(pl.multiple_of((1 - core) * 64, 64), 64)
+    there = pl.ds(pl.multiple_of(core * 64, 64), 64)
     for b in range(4):
         whole[b, here, :] = chosen[b]
-        whole[b, there, :] = half_block(other, pick(picks, b))
-    both = mixed[...] + gather_parts(picks, away, other)
+        whole[b, there, :] = parcel[512 + 64 * b : 576 + 64 * b, :]
+    both = mixed[...] + parcel[0:512, :].astype(F32)
     tagg = dot(both.astype(BF16), w_msg[...]).astype(BF16)
     zero = jnp.concatenate([whole[b] for b in range(4)], axis=0).astype(F32)
     one = (zero + jax.nn.silu(dot(tagg, w_agg[...]))).astype(BF16)
@@ -267,11 +284,16 @@
     tile_set = ((2, 2, 128, 128), BF16)
     part = ((512, 256), F32)
     gain = ((1, 256), F32)
-    row_cut, col_cut = ((1, 1, 2, 128, 256), BF16), ((1, 2, 1, 128, 256), BF16)
+    row_cut, col_cut = ((1, 1, 2, 128, 256), BF16), ((272, 256), BF16)
     dma = pltpu.SemaphoreType.DMA
     last_row, first_row, last_col, first_col = call(
-        cut_kernel, [HBM], [row_cut, row_cut, col_cut, col_cut], [dma((4,))], "cut", 1 << 20
-    )(far(fine_state))
+        cut_kernel,
+        [HBM] * 2,
+        [row_cut, row_cut, col_cut, col_cut],
+        [pltpu.VMEM((2, 2), jnp.int32), dma((7,))],
+        "cut",
+        1 << 20,
+    )(far(fine_state), far(up_map))
     down = lax.ppermute(first_row, "sy", north)
     up = lax.ppermute(last_row, "sy", south)
     left = lax.ppermute(last_col, sx, east)
@@ -292,16 +314,16 @@
     corner_l = lax.ppermute(jnp.concatenate([down[0, :, 1], up[0, :, 1]]), sx, east)
     corner_r = lax.ppermute(jnp.concatenate([down[0, :, 0], up[0, :, 0]]), sx, west)
     state, own_part, map_here, nbr_here, adj, tiles, *weights = held
-    mixed, corner_edges, label, sent, turned, near, away, picks = call(
+    mixed, corner_edges, label, sent, turned, keep, give, picks = call(
         functools.partial(near_kernel, core_axis="core"),
         [VMEM] * 9 + [HBM] * 2,
         [
             part, ((4, 128, 512), BF16), ((64, 128), F32), ((4, 128, 128), BF16), tile_set,
-            half_set, half_set, ((32, 128), jnp.int32),
+            half_set, half_set, ((40, 128), jnp.int32),
         ],
         [
             pltpu.VMEM((16, 128, 256), BF16), pltpu.SMEM((4, 20), jnp.int32),
-            pltpu.VMEM((4, 4, 128, 128), BF16), dma((5,)),
+            pltpu.VMEM((8, 4, 128, 128), BF16), dma((9,)),
         ],
         "near",
         1 << 23,
@@ -316,7 +338,7 @@
     )(corner_l, corner_r, mixed, corner_edges, label, sent, state, own_part, *weights)
     piece = piece.reshape(64, 9, 2, 128)
     chips = lax.axis_size("x") * rows
-    back = [2 * chip + core for chip in range(chips - 1, -1, -1) for core in range(2)]
+    back = [2 * chip + core for chip in range(chips - 1, -1, -1) for core in (1, 0)]
     got = lax.all_to_all(piece, ("x", "sy", "core"), 0, 0, axis_index_groups=[back])
     (share,) = call(
         sum_kernel,
@@ -331,22 +353,22 @@
         order_kernel, [VMEM], [((4, 20, 16, 256), BF16)], [], "top_order", 1 << 20
     )(column)
     mine = lax.all_to_all(column, "x", 0, 0, axis_index_groups=[list(range(cols // 2 - 1, -1, -1))])
-    other = lax.ppermute(mine, "core", twin)
+    (parcel,) = call(
+        give_kernel, [VMEM] * 3, [((768, 256), BF16)], [], "top_give", 1 << 20
+    )(picks, mine, give)
+    parcel = lax.ppermute(parcel, "core", twin)
     mixed, chosen = call(
-        half_kernel, [VMEM] * 3, [part, ((4, 64, 256), BF16)], [], "top_half", 1 << 23
-    )(picks, mine, near)
+        keep_kernel, [VMEM] * 3, [part, ((4, 64, 256), BF16)], [], "top_keep", 1 << 23
+    )(picks, mine, keep)
     (out,) = call(
         functools.partial(top_kernel, core_axis="core"),
-        [VMEM] * 11,
+        [VMEM] * 9,
         [(fine_state.shape, BF16)],
         [pltpu.VMEM(*half_set), dma((4,))],
         "top_level",
         1 << 23,
         place=HBM,
-    )(
-        picks, other, away, mixed, chosen, fine, turned, w_top_msg, w_top_agg, w_down,
-        out_gain[None],
-    )
+    )(parcel, mixed, chosen, fine, turned, w_top_msg, w_top_agg, w_down, out_gain[None])
     return out
 
 

time: 74.5 us -> 73.5 us (0.987)
    all_to_all x1, blocking collectives: 10.8 us -> 10 us  [local(): lax.all_to_all(share, 'sy', 0, 0, axis_index_groups=[list(range(rows - 1,...]
    pallas_call x3 -> x4, Pallas kernels: 3.1 us -> 3.21 us  [the longest x1 1.53 us: local(): call(functools.partial(top_kernel, core_axis='core'), [VMEM] * 9, [(fine_...]
  transfers between devices with their start and end apart: 7 -> 7, of which waited for: 2 -> 2; matrix products, arithmetic and copies ran while one was open for 0% -> 0% of each run, Pallas kernels for 4% -> 5%
where the time goes in v6:
time: 73.5 us; the launch traced here: 73.2 us
  blocking collectives  43.1 us (59%)
  starting transfers between devices  18.9 us (26%)
  Pallas kernels  8.4 us (11%)
  waiting for transfers between devices  2.51 us (3%)
    all_to_all x1, blocking collectives, local(): lax.all_to_all(piece, ('x', 'sy', 'core'), 0, 0, axis_index_groups=[back])  22 us
    all_to_all x1, blocking collectives, local(): lax.all_to_all(column, 'x', 0, 0, axis_index_groups=[list(range(cols // 2...  11.1 us
    all_to_all x1, blocking collectives, local(): lax.all_to_all(share, 'sy', 0, 0, axis_index_groups=[list(range(rows - 1,...  10 us
    ppermute x1, starting transfers between devices, local(): right = lax.ppermute(first_col, sx, west)  5.98 us
    ppermute x1, starting transfers between devices, local(): up = lax.ppermute(last_row, 'sy', south)  5.46 us
    ppermute x1, starting transfers between devices, local(): parcel = lax.ppermute(parcel, 'core', twin)  5.17 us
    pallas_call x1, Pallas kernels, local(): call(functools.partial(near_kernel, core_axis='core'), [VMEM] * 9 + [HBM]...  1.9 us
    pallas_call x1, Pallas kernels, local(): call(functools.partial(top_kernel, core_axis='core'), [VMEM] * 9, [(fine_...  1.53 us
  transfers between devices with their start and end apart: 7, of which 2 were waited for; matrix products, arithmetic and copies ran while one was open for 0% of the time, Pallas kernels for 5%

profile of v6, /device:TPU:1, one launch (start us, length us, event | category | flops | bytes accessed | tf_op | source)
XLA Modules:
  0.0 73.2 jit_solution(6262492115569483965)
XLA Ops:
  0.0 1.1 %cut.1 = (bf16[1,1,2,128,256]{4,3,2,1,0:T(8,128)(2,1)S(1)}, bf16[1,1,2,128,256]{4,3,2,1,0:T(8,128)(2,1)S(1)}, bf16[272,256]{1,0:T(8,128)(2,1)S(1)}, bf16[272,256]{1,0:T(8,128)(2,1)S(1)}) custom-call(bf16[1,2,2,128,256]{4,3,2,1,0:T(8,128)(2,1)} %state_in.1, s32[2,2]{1,0:T(2,128)} %map_in.3), custom_call_target="tpu_custom_call" | custom-call | bytes 1048576 | tf_op jit(solution)/shard_map/cut/pallas_call | solution.py:289
  1.1 1.3 %collective-permute-start = (bf16[1,1,2,128,256]{4,3,2,1,0:T(8,128)(2,1)S(1)}, bf16[1,1,2,128,256]{4,3,2,1,0:T(8,128)(2,1)S(1)}, u32[]{:S(2)}, u32[]{:S(2)}) collective-permute-start(bf16[1,1,2,128,256]{4,3,2,1,0:T(8,128)(2,1)S(1)} %get-tuple-element.43), channel_id=1, source_target_pairs={{8,0},{16,8},{24,16},{32,24},{40,32},{48,40},{56,48},{9,1},{17,9},... | collective-permute-start | bytes 393224 | tf_op jit(solution)/shard_map/ppermute | solution.py:297
  2.4 5.5 %collective-permute-start.1 = (bf16[1,1,2,128,256]{4,3,2,1,0:T(8,128)(2,1)S(1)}, bf16[1,1,2,128,256]{4,3,2,1,0:T(8,128)(2,1)S(1)}, u32[]{:S(2)}, u32[]{:S(2)}) collective-permute-start(bf16[1,1,2,128,256]{4,3,2,1,0:T(8,128)(2,1)S(1)} %get-tuple-element.44), channel_id=1, source_target_pairs={{0,8},{8,16},{16,24},{24,32},{32,40},{40,48},{48,56},{1,9},{9,17},... | collective-permute-start | bytes 393224 | tf_op jit(solution)/shard_map/ppermute | solution.py:298
  7.9 6.0 %collective-permute-start.2 = (bf16[272,256]{1,0:T(8,128)(2,1)S(1)}, bf16[272,256]{1,0:T(8,128)(2,1)S(1)}, u32[]{:S(2)}, u32[]{:S(2)}) collective-permute-start(bf16[272,256]{1,0:T(8,128)(2,1)S(1)} %get-tuple-element.59), channel_id=1, source_target_pairs={{1,0},{2,1},{3,2},{4,3},{5,4},{6,5},{7,6},{0,7},{9,8},{10,9},{11,1... | collective-permute-start | bytes 417800 | tf_op jit(solution)/shard_map/ppermute | solution.py:300
  13.9 0.0 collective-permute-start.3
  13.9 1.4 %stage.1 = (bf16[1,2,2,128,256]{4,3,2,1,0:T(8,128)(2,1)S(1)}, f32[512,256]{1,0:T(8,128)S(1)}, s32[2,2]{1,0:T(2,128)S(1)}, s32[2,2,4]{2,1,0:T(2,128)S(1)}, bf16[2...) custom-call(bf16[1,2,2,128,256]{4,3,2,1,0:T(8,128)(2,1)} %state_in.1, ...), custom_call_target="tpu_custom_call" | custom-call | bytes 8388608 | tf_op jit(solution)/shard_map/stage/pallas_call | solution.py:305
  15.3 0.0 collective-permute-done.down
  15.4 0.0 collective-permute-done.1.up
  15.4 0.0 collective-permute-start.4
  15.5 1.0 %collective-permute-start.5 = (bf16[2,128,256]{2,1,0:T(8,128)(2,1)S(1)}, bf16[2,128,256]{2,1,0:T(8,128)(2,1)S(1)}, u32[]{:S(2)}, u32[]{:S(2)}) collective-permute-start(bf16[2,128,256]{2,1,0:T(8,128)(2,1)S(1)} %pad_maximum_fusion.1), channel_id=1, source_target_pairs={{1,0},{2,1},{3,2},{4,3},{5,4},{6,5},{7,6},{0,7},{9,8},{10,9},{11,1... | collective-permute-start | bytes 393224 | tf_op jit(solution)/shard_map/ppermute | solution.py:315
  16.5 0.0 collective-permute-done.2.right
  16.5 0.0 collective-permute-done.3.left
  16.5 1.9 %near.1 = (f32[512,256]{1,0:T(8,128)S(1)}, bf16[4,128,512]{2,1,0:T(8,128)(2,1)S(1)}, f32[64,128]{1,0:T(8,128)S(1)}, bf16[4,128,128]{2,1,0:T(8,128)(2,1)S(1)}, bf...) custom-call(s32[2,2]{1,0:T(2,128)S(1)} %get-tuple-element.55.up_map,, ...), custom_call_target="tpu_custom_call" | custom-call | bytes 8388608 | tf_op jit(solution)/shard_map/near/pallas_call | solution.py:317
  18.4 0.0 copy-start.3
  18.4 0.0 collective-permute-done.4.corner_l
  18.4 1.5 %collective-permute-done.5.corner_r = bf16[2,128,256]{2,1,0:T(8,128)(2,1)S(1)} collective-permute-done((bf16[2,128,256]{2,1,0:T(8,128)(2,1)S(1)}, bf16[2,128,256]{2,1,0:T(8,128)(2,1)S(1)}, u32[]{:S(2)}, u32[]{:S(2)}) %collective-permute-start.5) | collective-permute-done | bytes 131104 | tf_op jit(solution)/shard_map/ppermute | solution.py:315
  19.9 1.1 %fine_level.1 = (bf16[512,256]{1,0:T(8,128)(2,1)S(1)}, bf16[1152,128]{1,0:T(8,128)(2,1)S(1)}) custom-call(bf16[2,128,256]{2,1,0:T(8,128)(2,1)S(1)} %collective-permute-done.4.corner_l, bf16[2,128,256]{2,1,0:T(8,128)(2,1)S(1)} %collective-permute-done.5.corner_r, f32[512,256]{1,0:T(8,128)S(1)} %get-tuple-element.65.mixed_in, ...), custom_call_target="tpu_custom_call" | custom-call | bytes 8388608 | tf_op jit(solution)/shard_map/fine_level/pallas_call | solution.py:331
  21.0 22.0 %all_to_all.15 = bf16[64,9,2,128]{3,2,1,0:T(2,128)(2,1)S(1)} all-to-all(bf16[64,9,2,128]{3,2,1,0:T(2,128)(2,1)S(1)} %bitcast.15), channel_id=1, replica_groups={{63,62,55,54,47,46,39,38,31,30,23,22,15,14,7,6,61,60,53,52,45,44,37,36,..., dimensions={0} | all-to-all | bytes 589824 | tf_op jit(solution)/shard_map/all_to_all | solution.py:342
  42.9 0.0 copy-start
  42.9 0.0 copy-start.1
  42.9 0.0 copy-start.2
  42.9 0.0 copy-start.4
  42.9 0.0 copy-done.3
  42.9 0.6 top_sum.1
  43.5 10.0 %all_to_all.16.got = bf16[8,40,256]{2,1,0:T(8,128)(2,1)S(1)} all-to-all(bf16[8,40,256]{2,1,0:T(8,128)(2,1)S(1)} %top_sum.1), channel_id=1, replica_groups={{56,48,40,32,24,16,8,0},{57,49,41,33,25,17,9,1},{58,50,42,34,26,18,10,2..., dimensions={0} | all-to-all | bytes 327680 | tf_op jit(solution)/shard_map/all_to_all | solution.py:351
  53.5 0.2 top_order.1
  53.7 11.1 %all_to_all.17.mine = bf16[4,20,16,256]{3,2,1,0:T(8,128)(2,1)S(1)} all-to-all(bf16[4,20,16,256]{3,2,1,0:T(8,128)(2,1)S(1)} %top_order.1), channel_id=1, replica_groups={{6,4,2,0},{7,5,3,1},{14,12,10,8},{15,13,11,9},{22,20,18,16},{23,21,19,1..., dimensions={0} | all-to-all | bytes 1310720 | tf_op jit(solution)/shard_map/all_to_all | solution.py:355
  64.9 0.3 top_give.1
  65.1 5.2 %collective-permute-start.6 = (bf16[768,256]{1,0:T(8,128)(2,1)S(1)}, bf16[768,256]{1,0:T(8,128)(2,1)S(1)}, u32[]{:S(2)}, u32[]{:S(2)}) collective-permute-start(bf16[768,256]{1,0:T(8,128)(2,1)S(1)} %top_give.1), channel_id=1, source_target_pairs={{0,1},{1,0},{2,3},{3,2},{4,5},{5,4},{6,7},{7,6},{8,9},{9,8},{10,11... | collective-permute-start | bytes 1179656 | tf_op jit(solution)/shard_map/ppermute | solution.py:359
  70.3 0.3 top_keep.1
  70.6 1.0 %collective-permute-done.6.parcel = bf16[768,256]{1,0:T(8,128)(2,1)S(1)} collective-permute-done((bf16[768,256]{1,0:T(8,128)(2,1)S(1)}, bf16[768,256]{1,0:T(8,128)(2,1)S(1)}, u32[]{:S(2)}, u32[]{:S(2)}) %collective-permute-start.6) | collective-permute-done | bytes 393248 | tf_op jit(solution)/shard_map/ppermute | solution.py:359
  71.6 0.0 copy-done
  71.6 0.0 copy-done.1
  71.6 0.0 copy-done.2
  71.6 0.0 copy-done.4
  71.7 1.5 %top_level.1 = bf16[1,2,2,128,256]{4,3,2,1,0:T(8,128)(2,1)} custom-call(bf16[768,256]{1,0:T(8,128)(2,1)S(1)} %collective-permute-done.6.parcel, f32[512,256]{1,0:T(8,128)S(1)} %get-tuple-element.77.mixed, bf16[4,64,256]{2,1,0:T(8,128)(2,1)S(1)} %get-tuple-element.78.chosen, bf16[512,256]{1,0:T(8,128)(2,1)S(1)} %get-tuple-element.79.fine, ...), custom_call_target="tpu_custom_call" | custom-call | bytes 8388608 | tf_op jit(solution)/shard_map/top_level/pallas_call | solution.py:363
  (3 shorter events, 0.1 us)
Async XLA Ops:
  1.1 14.2 %collective-permute-start = (bf16[1,1,2,128,256]{4,3,2,1,0:T(8,128)(2,1)S(1)}, bf16[1,1,2,128,256]{4,3,2,1,0:T(8,128)(2,1)S(1)}, u32[]{:S(2)}, u32[]{:S(2)}) collective-permute-start(bf16[1,1,2,128,256]{4,3,2,1,0:T(8,128)(2,1)S(1)} %get-tuple-element.43), channel_id=1, source_target_pairs={{8,0},{16,8},{24,16},{32,24},{40,32},{48,40},{56,48},{9,1},{17,9},... | collective-permute-start | bytes 393224 | tf_op jit(solution)/shard_map/ppermute | solution.py:297
  2.4 12.9 %collective-permute-start.1 = (bf16[1,1,2,128,256]{4,3,2,1,0:T(8,128)(2,1)S(1)}, bf16[1,1,2,128,256]{4,3,2,1,0:T(8,128)(2,1)S(1)}, u32[]{:S(2)}, u32[]{:S(2)}) collective-permute-start(bf16[1,1,2,128,256]{4,3,2,1,0:T(8,128)(2,1)S(1)} %get-tuple-element.44), channel_id=1, source_target_pairs={{0,8},{8,16},{16,24},{24,32},{32,40},{40,48},{48,56},{1,9},{9,17},... | collective-permute-start | bytes 393224 | tf_op jit(solution)/shard_map/ppermute | solution.py:298
  7.9 8.6 %collective-permute-start.2 = (bf16[272,256]{1,0:T(8,128)(2,1)S(1)}, bf16[272,256]{1,0:T(8,128)(2,1)S(1)}, u32[]{:S(2)}, u32[]{:S(2)}) collective-permute-start(bf16[272,256]{1,0:T(8,128)(2,1)S(1)} %get-tuple-element.59), channel_id=1, source_target_pairs={{1,0},{2,1},{3,2},{4,3},{5,4},{6,5},{7,6},{0,7},{9,8},{10,9},{11,1... | collective-permute-start | bytes 417800 | tf_op jit(solution)/shard_map/ppermute | solution.py:300
  13.9 2.6 %collective-permute-start.3 = (bf16[272,256]{1,0:T(8,128)(2,1)S(1)}, bf16[272,256]{1,0:T(8,128)(2,1)S(1)}, u32[]{:S(2)}, u32[]{:S(2)}) collective-permute-start(bf16[272,256]{1,0:T(8,128)(2,1)S(1)} %get-tuple-element.60), channel_id=1, source_target_pairs={{0,1},{1,2},{2,3},{3,4},{4,5},{5,6},{6,7},{7,0},{8,9},{9,10},{10,1... | collective-permute-start | bytes 417800 | tf_op jit(solution)/shard_map/ppermute | solution.py:299
  15.4 3.0 %collective-permute-start.4 = (bf16[2,128,256]{2,1,0:T(8,128)(2,1)S(1)}, bf16[2,128,256]{2,1,0:T(8,128)(2,1)S(1)}, u32[]{:S(2)}, u32[]{:S(2)}) collective-permute-start(bf16[2,128,256]{2,1,0:T(8,128)(2,1)S(1)} %pad_maximum_fusion), channel_id=1, source_target_pairs={{0,1},{1,2},{2,3},{3,4},{4,5},{5,6},{6,7},{7,0},{8,9},{9,10},{10,1... | collective-permute-start | bytes 393224 | tf_op jit(solution)/shard_map/ppermute | solution.py:314
  15.5 4.4 %collective-permute-start.5 = (bf16[2,128,256]{2,1,0:T(8,128)(2,1)S(1)}, bf16[2,128,256]{2,1,0:T(8,128)(2,1)S(1)}, u32[]{:S(2)}, u32[]{:S(2)}) collective-permute-start(bf16[2,128,256]{2,1,0:T(8,128)(2,1)S(1)} %pad_maximum_fusion.1), channel_id=1, source_target_pairs={{1,0},{2,1},{3,2},{4,3},{5,4},{6,5},{7,6},{0,7},{9,8},{10,9},{11,1... | collective-permute-start | bytes 393224 | tf_op jit(solution)/shard_map/ppermute | solution.py:315
  18.4 24.5 %copy-start.3 = (f32[256]{0:T(256)S(1)}, f32[256]{0:T(256)}, u32[]{:S(2)}) copy-start(f32[256]{0:T(256)} %param.32) | copy-start | bytes 3076
  42.9 28.7 %copy-start = (bf16[256,256]{1,0:T(8,128)(2,1)S(1)}, bf16[256,256]{1,0:T(8,128)(2,1)}, u32[]{:S(2)}) copy-start(bf16[256,256]{1,0:T(8,128)(2,1)} %w_msg.1) | copy-start | bytes 393220
  42.9 28.7 %copy-start.1 = (bf16[256,256]{1,0:T(8,128)(2,1)S(1)}, bf16[256,256]{1,0:T(8,128)(2,1)}, u32[]{:S(2)}) copy-start(bf16[256,256]{1,0:T(8,128)(2,1)} %w_agg.1) | copy-start | bytes 393220
  42.9 28.7 %copy-start.2 = (bf16[256,256]{1,0:T(8,128)(2,1)S(1)}, bf16[256,256]{1,0:T(8,128)(2,1)}, u32[]{:S(2)}) copy-start(bf16[256,256]{1,0:T(8,128)(2,1)} %w_down.1) | copy-start | bytes 393220
  42.9 28.7 %copy-start.4 = (f32[256]{0:T(256)S(1)}, f32[256]{0:T(256)}, u32[]{:S(2)}) copy-start(f32[256]{0:T(256)} %param.33) | copy-start | bytes 3076
  65.1 6.5 %collective-permute-start.6 = (bf16[768,256]{1,0:T(8,128)(2,1)S(1)}, bf16[768,256]{1,0:T(8,128)(2,1)S(1)}, u32[]{:S(2)}, u32[]{:S(2)}) collective-permute-start(bf16[768,256]{1,0:T(8,128)(2,1)S(1)} %top_give.1), channel_id=1, source_target_pairs={{0,1},{1,0},{2,3},{3,2},{4,5},{5,4},{6,7},{7,6},{8,9},{9,8},{10,11... | collective-permute-start | bytes 1179656 | tf_op jit(solution)/shard_map/ppermute | solution.py:359

commit v7 on v6

--- a/solution.py
+++ b/solution.py
@@ -100,13 +100,9 @@
         frame[12 * r] = jnp.zeros((128, 256), BF16)
         frame[12 * r + 3] = jnp.zeros((128, 256), BF16)
     lane = lax.broadcasted_iota(jnp.int32, (64, 128), 1)
-    block = lane >> 5
-    joined = jnp.where(
-        block < 2,
-        jnp.where(block == 0, joins[0], joins[1]),
-        jnp.where(block == 2, joins[2], joins[3]),
-    )
-    label[...] = jnp.where((lane & 31) == joined, 1.0, 0.0)
+    for j in range(2):
+        joined = jnp.where(lane < 64, joins[2 * j], joins[2 * j + 1])
+        label[j] = jnp.where((lane & 63) == 2 * joined, 1.0, 0.0)
     row = lax.broadcasted_iota(jnp.int32, (128, 128), 0)
     col = lax.broadcasted_iota(jnp.int32, (128, 128), 1)
     want = (row & 1) * 64 + (row & 62) + (row >> 6)
@@ -165,29 +161,26 @@
             for i in range(2):
                 part = contrib[64 * i : 64 * i + 64, 128 * h : 128 * h + 128]
                 lines[pl.ds(8 * h + 2 * b + i, 64, stride=18), :] = part
-    lines[pl.ds(16, 64, stride=18), :] = label[...]
-    lines[pl.ds(17, 64, stride=18), :] = jnp.zeros((64, 128), F32)
-    piece_out[...] = lines[...].astype(BF16)
+    for j in range(2):
+        lines[pl.ds(16 + j, 64, stride=18), :] = label[j]
+    piece_out[...] = lines[0:1152, :].astype(BF16)
 
 
 def sum_kernel(got, gain, share_out, lines):
-    lines[...] = got[...].astype(F32)
+    lines[0:1152, :] = got[...].astype(F32)
     take = lambda n: lines[pl.ds(n, 64, stride=18), :]
-    label = take(16)
+    labels = [take(16), take(17)]
     member, values = [], []
     for b in range(4):
-        member.append(pltpu.roll(label, (128 - 32 * b) % 128, 1) if b else label)
-        wide = [take(8 * h + 2 * b + i) for i in range(2) for h in range(2)]
-        values.append(jnp.concatenate(wide, axis=1))
+        for i in range(2):
+            turn = 64 * (b % 2) + i
+            member.append(pltpu.roll(labels[b // 2], turn, 1) if turn else labels[b // 2])
+            wide = [take(8 * h + 2 * b + i) for h in range(2)]
+            values.append(jnp.concatenate(wide, axis=1))
     member = jnp.concatenate(member, axis=0).astype(BF16)
     values = jnp.concatenate(values, axis=0).astype(BF16)
-    total = dot_t(member, values)[:32]
-    both = [norm(total[:, 256 * i : 256 * i + 256], gain[...]) for i in range(2)]
-    both = jnp.concatenate(both, axis=0).astype(BF16)
-    row = lax.broadcasted_iota(jnp.int32, (40, 64), 0)
-    col = lax.broadcasted_iota(jnp.int32, (40, 64), 1)
-    order = jnp.where(col == (row & 1) * 32 + (row >> 1), 1.0, 0.0).astype(BF16)
-    share = dot(order, both).astype(BF16)
+    total = dot_t(member, values)[:40]
+    share = norm(total, gain[...]).astype(BF16)
     share_out[...] = jnp.broadcast_to(share[None], share_out.shape)
 
 
@@ -318,7 +311,7 @@
         functools.partial(near_kernel, core_axis="core"),
         [VMEM] * 9 + [HBM] * 2,
         [
-            part, ((4, 128, 512), BF16), ((64, 128), F32), ((4, 128, 128), BF16), tile_set,
+            part, ((4, 128, 512), BF16), ((2, 64, 128), F32), ((4, 128, 128), BF16), tile_set,
             half_set, half_set, ((40, 128), jnp.int32),
         ],
         [
@@ -332,7 +325,7 @@
         fine_kernel,
         [VMEM] * 12,
         [((512, 256), BF16), ((64 * 18, 128), BF16)],
-        [pltpu.VMEM((64 * 18, 128), F32)],
+        [pltpu.VMEM((64 * 18 + 24, 128), F32)],
         "fine_level",
         1 << 23,
     )(corner_l, corner_r, mixed, corner_edges, label, sent, state, own_part, *weights)
@@ -344,7 +337,7 @@
         sum_kernel,
         [VMEM] * 2,
         [((8, 40, 256), BF16)],
-        [pltpu.VMEM((64 * 18, 128), F32)],
+        [pltpu.VMEM((64 * 18 + 24, 128), F32)],
         "top_sum",
         1 << 20,
     )(got.reshape(64 * 18, 128), top_gain[None])

time: 73.5 us -> 73.4 us (level)
  no operation moved by 1% of the time
where the time goes in v7:
time: 73.4 us; the launch traced here: 73.1 us
  blocking collectives  43.1 us (59%)
  starting transfers between devices  18.9 us (26%)
  Pallas kernels  8.3 us (11%)
  waiting for transfers between devices  2.51 us (3%)
    all_to_all x1, blocking collectives, local(): lax.all_to_all(piece, ('x', 'sy', 'core'), 0, 0, axis_index_groups=[back])  22 us
    all_to_all x1, blocking collectives, local(): lax.all_to_all(column, 'x', 0, 0, axis_index_groups=[list(range(cols // 2...  11.1 us
    all_to_all x1, blocking collectives, local(): lax.all_to_all(share, 'sy', 0, 0, axis_index_groups=[list(range(rows - 1,...  10 us
    ppermute x1, starting transfers between devices, local(): right = lax.ppermute(first_col, sx, west)  5.98 us
    ppermute x1, starting transfers between devices, local(): up = lax.ppermute(last_row, 'sy', south)  5.46 us
    ppermute x1, starting transfers between devices, local(): parcel = lax.ppermute(parcel, 'core', twin)  5.17 us
    pallas_call x1, Pallas kernels, local(): call(functools.partial(near_kernel, core_axis='core'), [VMEM] * 9 + [HBM]...  1.9 us
    pallas_call x1, Pallas kernels, local(): call(functools.partial(top_kernel, core_axis='core'), [VMEM] * 9, [(fine_...  1.53 us
  transfers between devices with their start and end apart: 7, of which 2 were waited for; matrix products, arithmetic and copies ran while one was open for 0% of the time, Pallas kernels for 5%

profile of v7, /device:TPU:1, one launch (start us, length us, event | category | flops | bytes accessed | tf_op | source)
XLA Modules:
  0.0 73.1 jit_solution(613028393687525431)
XLA Ops:
  0.0 1.1 %cut.1 = (bf16[1,1,2,128,256]{4,3,2,1,0:T(8,128)(2,1)S(1)}, bf16[1,1,2,128,256]{4,3,2,1,0:T(8,128)(2,1)S(1)}, bf16[272,256]{1,0:T(8,128)(2,1)S(1)}, bf16[272,256]{1,0:T(8,128)(2,1)S(1)}) custom-call(bf16[1,2,2,128,256]{4,3,2,1,0:T(8,128)(2,1)} %state_in.1, s32[2,2]{1,0:T(2,128)} %map_in.3), custom_call_target="tpu_custom_call" | custom-call | bytes 1048576 | tf_op jit(solution)/shard_map/cut/pallas_call | solution.py:282
  1.1 1.3 %collective-permute-start = (bf16[1,1,2,128,256]{4,3,2,1,0:T(8,128)(2,1)S(1)}, bf16[1,1,2,128,256]{4,3,2,1,0:T(8,128)(2,1)S(1)}, u32[]{:S(2)}, u32[]{:S(2)}) collective-permute-start(bf16[1,1,2,128,256]{4,3,2,1,0:T(8,128)(2,1)S(1)} %get-tuple-element.43), channel_id=1, source_target_pairs={{8,0},{16,8},{24,16},{32,24},{40,32},{48,40},{56,48},{9,1},{17,9},... | collective-permute-start | bytes 393224 | tf_op jit(solution)/shard_map/ppermute | solution.py:290
  2.4 5.5 %collective-permute-start.1 = (bf16[1,1,2,128,256]{4,3,2,1,0:T(8,128)(2,1)S(1)}, bf16[1,1,2,128,256]{4,3,2,1,0:T(8,128)(2,1)S(1)}, u32[]{:S(2)}, u32[]{:S(2)}) collective-permute-start(bf16[1,1,2,128,256]{4,3,2,1,0:T(8,128)(2,1)S(1)} %get-tuple-element.44), channel_id=1, source_target_pairs={{0,8},{8,16},{16,24},{24,32},{32,40},{40,48},{48,56},{1,9},{9,17},... | collective-permute-start | bytes 393224 | tf_op jit(solution)/shard_map/ppermute | solution.py:291
  7.9 6.0 %collective-permute-start.2 = (bf16[272,256]{1,0:T(8,128)(2,1)S(1)}, bf16[272,256]{1,0:T(8,128)(2,1)S(1)}, u32[]{:S(2)}, u32[]{:S(2)}) collective-permute-start(bf16[272,256]{1,0:T(8,128)(2,1)S(1)} %get-tuple-element.59), channel_id=1, source_target_pairs={{1,0},{2,1},{3,2},{4,3},{5,4},{6,5},{7,6},{0,7},{9,8},{10,9},{11,1... | collective-permute-start | bytes 417800 | tf_op jit(solution)/shard_map/ppermute | solution.py:293
  13.9 0.0 collective-permute-start.3
  13.9 1.4 %stage.1 = (bf16[1,2,2,128,256]{4,3,2,1,0:T(8,128)(2,1)S(1)}, f32[512,256]{1,0:T(8,128)S(1)}, s32[2,2]{1,0:T(2,128)S(1)}, s32[2,2,4]{2,1,0:T(2,128)S(1)}, bf16[2...) custom-call(bf16[1,2,2,128,256]{4,3,2,1,0:T(8,128)(2,1)} %state_in.1, ...), custom_call_target="tpu_custom_call" | custom-call | bytes 8388608 | tf_op jit(solution)/shard_map/stage/pallas_call | solution.py:298
  15.3 0.0 collective-permute-done.down
  15.4 0.0 collective-permute-done.1.up
  15.4 0.0 collective-permute-start.4
  15.5 1.0 %collective-permute-start.5 = (bf16[2,128,256]{2,1,0:T(8,128)(2,1)S(1)}, bf16[2,128,256]{2,1,0:T(8,128)(2,1)S(1)}, u32[]{:S(2)}, u32[]{:S(2)}) collective-permute-start(bf16[2,128,256]{2,1,0:T(8,128)(2,1)S(1)} %pad_maximum_fusion.1), channel_id=1, source_target_pairs={{1,0},{2,1},{3,2},{4,3},{5,4},{6,5},{7,6},{0,7},{9,8},{10,9},{11,1... | collective-permute-start | bytes 393224 | tf_op jit(solution)/shard_map/ppermute | solution.py:308
  16.5 0.0 collective-permute-done.2.right
  16.5 0.0 collective-permute-done.3.left
  16.5 1.9 %near.1 = (f32[512,256]{1,0:T(8,128)S(1)}, bf16[4,128,512]{2,1,0:T(8,128)(2,1)S(1)}, f32[2,64,128]{2,1,0:T(8,128)S(1)}, bf16[4,128,128]{2,1,0:T(8,128)(2,1)S(1)}...) custom-call(s32[2,2]{1,0:T(2,128)S(1)} %get-tuple-element.55.up_map,, ...), custom_call_target="tpu_custom_call" | custom-call | bytes 8388608 | tf_op jit(solution)/shard_map/near/pallas_call | solution.py:310
  18.4 0.0 copy-start.3
  18.4 0.0 collective-permute-done.4.corner_l
  18.4 1.5 %collective-permute-done.5.corner_r = bf16[2,128,256]{2,1,0:T(8,128)(2,1)S(1)} collective-permute-done((bf16[2,128,256]{2,1,0:T(8,128)(2,1)S(1)}, bf16[2,128,256]{2,1,0:T(8,128)(2,1)S(1)}, u32[]{:S(2)}, u32[]{:S(2)}) %collective-permute-start.5) | collective-permute-done | bytes 131104 | tf_op jit(solution)/shard_map/ppermute | solution.py:308
  19.9 1.1 %fine_level.1 = (bf16[512,256]{1,0:T(8,128)(2,1)S(1)}, bf16[1152,128]{1,0:T(8,128)(2,1)S(1)}) custom-call(bf16[2,128,256]{2,1,0:T(8,128)(2,1)S(1)} %collective-permute-done.4.corner_l, bf16[2,128,256]{2,1,0:T(8,128)(2,1)S(1)} %collective-permute-done.5.corner_r, f32[512,256]{1,0:T(8,128)S(1)} %get-tuple-element.65.mixed_in, ...), custom_call_target="tpu_custom_call" | custom-call | bytes 8388608 | tf_op jit(solution)/shard_map/fine_level/pallas_call | solution.py:324
  21.0 22.0 %all_to_all.15 = bf16[64,9,2,128]{3,2,1,0:T(2,128)(2,1)S(1)} all-to-all(bf16[64,9,2,128]{3,2,1,0:T(2,128)(2,1)S(1)} %bitcast.15), channel_id=1, replica_groups={{63,62,55,54,47,46,39,38,31,30,23,22,15,14,7,6,61,60,53,52,45,44,37,36,..., dimensions={0} | all-to-all | bytes 589824 | tf_op jit(solution)/shard_map/all_to_all | solution.py:335
  42.9 0.0 copy-start
  42.9 0.0 copy-start.1
  42.9 0.0 copy-start.2
  42.9 0.0 copy-start.4
  42.9 0.0 copy-done.3
  42.9 0.5 top_sum.1
  43.4 10.0 %all_to_all.16.got = bf16[8,40,256]{2,1,0:T(8,128)(2,1)S(1)} all-to-all(bf16[8,40,256]{2,1,0:T(8,128)(2,1)S(1)} %top_sum.1), channel_id=1, replica_groups={{56,48,40,32,24,16,8,0},{57,49,41,33,25,17,9,1},{58,50,42,34,26,18,10,2..., dimensions={0} | all-to-all | bytes 327680 | tf_op jit(solution)/shard_map/all_to_all | solution.py:344
  53.4 0.2 top_order.1
  53.6 11.1 %all_to_all.17.mine = bf16[4,20,16,256]{3,2,1,0:T(8,128)(2,1)S(1)} all-to-all(bf16[4,20,16,256]{3,2,1,0:T(8,128)(2,1)S(1)} %top_order.1), channel_id=1, replica_groups={{6,4,2,0},{7,5,3,1},{14,12,10,8},{15,13,11,9},{22,20,18,16},{23,21,19,1..., dimensions={0} | all-to-all | bytes 1310720 | tf_op jit(solution)/shard_map/all_to_all | solution.py:348
  64.8 0.3 top_give.1
  65.0 5.2 %collective-permute-start.6 = (bf16[768,256]{1,0:T(8,128)(2,1)S(1)}, bf16[768,256]{1,0:T(8,128)(2,1)S(1)}, u32[]{:S(2)}, u32[]{:S(2)}) collective-permute-start(bf16[768,256]{1,0:T(8,128)(2,1)S(1)} %top_give.1), channel_id=1, source_target_pairs={{0,1},{1,0},{2,3},{3,2},{4,5},{5,4},{6,7},{7,6},{8,9},{9,8},{10,11... | collective-permute-start | bytes 1179656 | tf_op jit(solution)/shard_map/ppermute | solution.py:352
  70.2 0.3 top_keep.1
  70.5 1.0 %collective-permute-done.6.parcel = bf16[768,256]{1,0:T(8,128)(2,1)S(1)} collective-permute-done((bf16[768,256]{1,0:T(8,128)(2,1)S(1)}, bf16[768,256]{1,0:T(8,128)(2,1)S(1)}, u32[]{:S(2)}, u32[]{:S(2)}) %collective-permute-start.6) | collective-permute-done | bytes 393248 | tf_op jit(solution)/shard_map/ppermute | solution.py:352
  71.5 0.0 copy-done
  71.5 0.0 copy-done.1
  71.5 0.0 copy-done.2
  71.5 0.0 copy-done.4
  71.6 1.5 %top_level.1 = bf16[1,2,2,128,256]{4,3,2,1,0:T(8,128)(2,1)} custom-call(bf16[768,256]{1,0:T(8,128)(2,1)S(1)} %collective-permute-done.6.parcel, f32[512,256]{1,0:T(8,128)S(1)} %get-tuple-element.77.mixed, bf16[4,64,256]{2,1,0:T(8,128)(2,1)S(1)} %get-tuple-element.78.chosen, bf16[512,256]{1,0:T(8,128)(2,1)S(1)} %get-tuple-element.79.fine, ...), custom_call_target="tpu_custom_call" | custom-call | bytes 8388608 | tf_op jit(solution)/shard_map/top_level/pallas_call | solution.py:356
  (3 shorter events, 0.1 us)
Async XLA Ops:
  1.1 14.2 %collective-permute-start = (bf16[1,1,2,128,256]{4,3,2,1,0:T(8,128)(2,1)S(1)}, bf16[1,1,2,128,256]{4,3,2,1,0:T(8,128)(2,1)S(1)}, u32[]{:S(2)}, u32[]{:S(2)}) collective-permute-start(bf16[1,1,2,128,256]{4,3,2,1,0:T(8,128)(2,1)S(1)} %get-tuple-element.43), channel_id=1, source_target_pairs={{8,0},{16,8},{24,16},{32,24},{40,32},{48,40},{56,48},{9,1},{17,9},... | collective-permute-start | bytes 393224 | tf_op jit(solution)/shard_map/ppermute | solution.py:290
  2.4 12.9 %collective-permute-start.1 = (bf16[1,1,2,128,256]{4,3,2,1,0:T(8,128)(2,1)S(1)}, bf16[1,1,2,128,256]{4,3,2,1,0:T(8,128)(2,1)S(1)}, u32[]{:S(2)}, u32[]{:S(2)}) collective-permute-start(bf16[1,1,2,128,256]{4,3,2,1,0:T(8,128)(2,1)S(1)} %get-tuple-element.44), channel_id=1, source_target_pairs={{0,8},{8,16},{16,24},{24,32},{32,40},{40,48},{48,56},{1,9},{9,17},... | collective-permute-start | bytes 393224 | tf_op jit(solution)/shard_map/ppermute | solution.py:291
  7.9 8.6 %collective-permute-start.2 = (bf16[272,256]{1,0:T(8,128)(2,1)S(1)}, bf16[272,256]{1,0:T(8,128)(2,1)S(1)}, u32[]{:S(2)}, u32[]{:S(2)}) collective-permute-start(bf16[272,256]{1,0:T(8,128)(2,1)S(1)} %get-tuple-element.59), channel_id=1, source_target_pairs={{1,0},{2,1},{3,2},{4,3},{5,4},{6,5},{7,6},{0,7},{9,8},{10,9},{11,1... | collective-permute-start | bytes 417800 | tf_op jit(solution)/shard_map/ppermute | solution.py:293
  13.9 2.6 %collective-permute-start.3 = (bf16[272,256]{1,0:T(8,128)(2,1)S(1)}, bf16[272,256]{1,0:T(8,128)(2,1)S(1)}, u32[]{:S(2)}, u32[]{:S(2)}) collective-permute-start(bf16[272,256]{1,0:T(8,128)(2,1)S(1)} %get-tuple-element.60), channel_id=1, source_target_pairs={{0,1},{1,2},{2,3},{3,4},{4,5},{5,6},{6,7},{7,0},{8,9},{9,10},{10,1... | collective-permute-start | bytes 417800 | tf_op jit(solution)/shard_map/ppermute | solution.py:292
  15.4 3.0 %collective-permute-start.4 = (bf16[2,128,256]{2,1,0:T(8,128)(2,1)S(1)}, bf16[2,128,256]{2,1,0:T(8,128)(2,1)S(1)}, u32[]{:S(2)}, u32[]{:S(2)}) collective-permute-start(bf16[2,128,256]{2,1,0:T(8,128)(2,1)S(1)} %pad_maximum_fusion), channel_id=1, source_target_pairs={{0,1},{1,2},{2,3},{3,4},{4,5},{5,6},{6,7},{7,0},{8,9},{9,10},{10,1... | collective-permute-start | bytes 393224 | tf_op jit(solution)/shard_map/ppermute | solution.py:307
  15.5 4.4 %collective-permute-start.5 = (bf16[2,128,256]{2,1,0:T(8,128)(2,1)S(1)}, bf16[2,128,256]{2,1,0:T(8,128)(2,1)S(1)}, u32[]{:S(2)}, u32[]{:S(2)}) collective-permute-start(bf16[2,128,256]{2,1,0:T(8,128)(2,1)S(1)} %pad_maximum_fusion.1), channel_id=1, source_target_pairs={{1,0},{2,1},{3,2},{4,3},{5,4},{6,5},{7,6},{0,7},{9,8},{10,9},{11,1... | collective-permute-start | bytes 393224 | tf_op jit(solution)/shard_map/ppermute | solution.py:308
  18.4 24.5 %copy-start.3 = (f32[256]{0:T(256)S(1)}, f32[256]{0:T(256)}, u32[]{:S(2)}) copy-start(f32[256]{0:T(256)} %param.32) | copy-start | bytes 3076
  42.9 28.6 %copy-start = (bf16[256,256]{1,0:T(8,128)(2,1)S(1)}, bf16[256,256]{1,0:T(8,128)(2,1)}, u32[]{:S(2)}) copy-start(bf16[256,256]{1,0:T(8,128)(2,1)} %w_msg.1) | copy-start | bytes 393220
  42.9 28.6 %copy-start.1 = (bf16[256,256]{1,0:T(8,128)(2,1)S(1)}, bf16[256,256]{1,0:T(8,128)(2,1)}, u32[]{:S(2)}) copy-start(bf16[256,256]{1,0:T(8,128)(2,1)} %w_agg.1) | copy-start | bytes 393220
  42.9 28.6 %copy-start.2 = (bf16[256,256]{1,0:T(8,128)(2,1)S(1)}, bf16[256,256]{1,0:T(8,128)(2,1)}, u32[]{:S(2)}) copy-start(bf16[256,256]{1,0:T(8,128)(2,1)} %w_down.1) | copy-start | bytes 393220
  42.9 28.6 %copy-start.4 = (f32[256]{0:T(256)S(1)}, f32[256]{0:T(256)}, u32[]{:S(2)}) copy-start(f32[256]{0:T(256)} %param.33) | copy-start | bytes 3076
  65.0 6.5 %collective-permute-start.6 = (bf16[768,256]{1,0:T(8,128)(2,1)S(1)}, bf16[768,256]{1,0:T(8,128)(2,1)S(1)}, u32[]{:S(2)}, u32[]{:S(2)}) collective-permute-start(bf16[768,256]{1,0:T(8,128)(2,1)S(1)} %top_give.1), channel_id=1, source_target_pairs={{0,1},{1,0},{2,3},{3,2},{4,5},{5,4},{6,7},{7,6},{8,9},{9,8},{10,11... | collective-permute-start | bytes 1179656 | tf_op jit(solution)/shard_map/ppermute | solution.py:352

commit v8 on v7

--- a/solution.py
+++ b/solution.py
@@ -117,7 +117,8 @@
                 picked.append(frame[spot])
                 tile = adj[y, x, k]
                 corner = jnp.where(code == 6 * y + 2 * x, tile, jnp.zeros_like(tile))
-                corner_edges[b, :, 128 * k : 128 * k + 128] = corner
+                joint = corner.astype(F32) if k == 0 else joint + corner.astype(F32)
+            corner_edges[b] = joint.astype(BF16)
             tile_row = jnp.concatenate([adj[y, x, k] for k in range(4)], axis=1)
             mixed[128 * b : 128 * b + 128] = dot(tile_row, jnp.concatenate(picked, axis=0))
     for b in range(4):
@@ -145,8 +146,7 @@
         for x in range(2):
             b = 2 * y + x
             corner = (corner_r if x else corner_l)[1 - y]
-            picked = jnp.concatenate([corner] * 4, axis=0)
-            total = mixed_in[128 * b : 128 * b + 128] + dot(corner_edges[b], picked)
+            total = mixed_in[128 * b : 128 * b + 128] + dot(corner_edges[b], corner)
             mixed.append(total.astype(BF16))
             own.append(state[0, y, x])
     own = jnp.concatenate(own, axis=0)
@@ -311,7 +311,7 @@
         functools.partial(near_kernel, core_axis="core"),
         [VMEM] * 9 + [HBM] * 2,
         [
-            part, ((4, 128, 512), BF16), ((2, 64, 128), F32), ((4, 128, 128), BF16), tile_set,
+            part, ((4, 128, 128), BF16), ((2, 64, 128), F32), ((4, 128, 128), BF16), tile_set,
             half_set, half_set, ((40, 128), jnp.int32),
         ],
         [

time: 73.4 us -> 73.4 us (level)
  no operation moved by 1% of the time
where the time goes in v8:
time: 73.4 us; the launch traced here: 73 us
  blocking collectives  43.1 us (59%)
  starting transfers between devices  18.9 us (26%)
  Pallas kernels  8.25 us (11%)
  waiting for transfers between devices  2.52 us (3%)
    all_to_all x1, blocking collectives, local(): lax.all_to_all(piece, ('x', 'sy', 'core'), 0, 0, axis_index_groups=[back])  22 us
    all_to_all x1, blocking collectives, local(): lax.all_to_all(column, 'x', 0, 0, axis_index_groups=[list(range(cols // 2...  11.1 us
    all_to_all x1, blocking collectives, local(): lax.all_to_all(share, 'sy', 0, 0, axis_index_groups=[list(range(rows - 1,...  10 us
    ppermute x1, starting transfers between devices, local(): right = lax.ppermute(first_col, sx, west)  5.98 us
    ppermute x1, starting transfers between devices, local(): up = lax.ppermute(last_row, 'sy', south)  5.46 us
    ppermute x1, starting transfers between devices, local(): parcel = lax.ppermute(parcel, 'core', twin)  5.17 us
    pallas_call x1, Pallas kernels, local(): call(functools.partial(near_kernel, core_axis='core'), [VMEM] * 9 + [HBM]...  1.9 us
    pallas_call x1, Pallas kernels, local(): call(functools.partial(top_kernel, core_axis='core'), [VMEM] * 9, [(fine_...  1.53 us
  transfers between devices with their start and end apart: 7, of which 2 were waited for; matrix products, arithmetic and copies ran while one was open for 0% of the time, Pallas kernels for 5%

profile of v8, /device:TPU:1, one launch (start us, length us, event | category | flops | bytes accessed | tf_op | source)
XLA Modules:
  0.0 73.0 jit_solution(2387776487803481883)
XLA Ops:
  0.0 1.1 %cut.1 = (bf16[1,1,2,128,256]{4,3,2,1,0:T(8,128)(2,1)S(1)}, bf16[1,1,2,128,256]{4,3,2,1,0:T(8,128)(2,1)S(1)}, bf16[272,256]{1,0:T(8,128)(2,1)S(1)}, bf16[272,256]{1,0:T(8,128)(2,1)S(1)}) custom-call(bf16[1,2,2,128,256]{4,3,2,1,0:T(8,128)(2,1)} %state_in.1, s32[2,2]{1,0:T(2,128)} %map_in.3), custom_call_target="tpu_custom_call" | custom-call | bytes 1048576 | tf_op jit(solution)/shard_map/cut/pallas_call | solution.py:282
  1.1 1.3 %collective-permute-start = (bf16[1,1,2,128,256]{4,3,2,1,0:T(8,128)(2,1)S(1)}, bf16[1,1,2,128,256]{4,3,2,1,0:T(8,128)(2,1)S(1)}, u32[]{:S(2)}, u32[]{:S(2)}) collective-permute-start(bf16[1,1,2,128,256]{4,3,2,1,0:T(8,128)(2,1)S(1)} %get-tuple-element.43), channel_id=1, source_target_pairs={{8,0},{16,8},{24,16},{32,24},{40,32},{48,40},{56,48},{9,1},{17,9},... | collective-permute-start | bytes 393224 | tf_op jit(solution)/shard_map/ppermute | solution.py:290
  2.4 5.5 %collective-permute-start.1 = (bf16[1,1,2,128,256]{4,3,2,1,0:T(8,128)(2,1)S(1)}, bf16[1,1,2,128,256]{4,3,2,1,0:T(8,128)(2,1)S(1)}, u32[]{:S(2)}, u32[]{:S(2)}) collective-permute-start(bf16[1,1,2,128,256]{4,3,2,1,0:T(8,128)(2,1)S(1)} %get-tuple-element.44), channel_id=1, source_target_pairs={{0,8},{8,16},{16,24},{24,32},{32,40},{40,48},{48,56},{1,9},{9,17},... | collective-permute-start | bytes 393224 | tf_op jit(solution)/shard_map/ppermute | solution.py:291
  7.9 6.0 %collective-permute-start.2 = (bf16[272,256]{1,0:T(8,128)(2,1)S(1)}, bf16[272,256]{1,0:T(8,128)(2,1)S(1)}, u32[]{:S(2)}, u32[]{:S(2)}) collective-permute-start(bf16[272,256]{1,0:T(8,128)(2,1)S(1)} %get-tuple-element.59), channel_id=1, source_target_pairs={{1,0},{2,1},{3,2},{4,3},{5,4},{6,5},{7,6},{0,7},{9,8},{10,9},{11,1... | collective-permute-start | bytes 417800 | tf_op jit(solution)/shard_map/ppermute | solution.py:293
  13.9 0.0 collective-permute-start.3
  13.9 1.4 %stage.1 = (bf16[1,2,2,128,256]{4,3,2,1,0:T(8,128)(2,1)S(1)}, f32[512,256]{1,0:T(8,128)S(1)}, s32[2,2]{1,0:T(2,128)S(1)}, s32[2,2,4]{2,1,0:T(2,128)S(1)}, bf16[2...) custom-call(bf16[1,2,2,128,256]{4,3,2,1,0:T(8,128)(2,1)} %state_in.1, ...), custom_call_target="tpu_custom_call" | custom-call | bytes 8388608 | tf_op jit(solution)/shard_map/stage/pallas_call | solution.py:298
  15.3 0.0 collective-permute-done.down
  15.4 0.0 collective-permute-done.1.up
  15.4 0.0 collective-permute-start.4
  15.5 1.0 %collective-permute-start.5 = (bf16[2,128,256]{2,1,0:T(8,128)(2,1)S(1)}, bf16[2,128,256]{2,1,0:T(8,128)(2,1)S(1)}, u32[]{:S(2)}, u32[]{:S(2)}) collective-permute-start(bf16[2,128,256]{2,1,0:T(8,128)(2,1)S(1)} %pad_maximum_fusion.1), channel_id=1, source_target_pairs={{1,0},{2,1},{3,2},{4,3},{5,4},{6,5},{7,6},{0,7},{9,8},{10,9},{11,1... | collective-permute-start | bytes 393224 | tf_op jit(solution)/shard_map/ppermute | solution.py:308
  16.5 0.0 collective-permute-done.2.right
  16.5 0.0 collective-permute-done.3.left
  16.5 0.0 copy-start.3
  16.5 1.9 %near.1 = (f32[512,256]{1,0:T(8,128)S(1)}, bf16[4,128,128]{2,1,0:T(8,128)(2,1)S(1)}, f32[2,64,128]{2,1,0:T(8,128)S(1)}, bf16[4,128,128]{2,1,0:T(8,128)(2,1)S(1)}...) custom-call(s32[2,2]{1,0:T(2,128)S(1)} %get-tuple-element.55.up_map,, ...), custom_call_target="tpu_custom_call" | custom-call | bytes 8388608 | tf_op jit(solution)/shard_map/near/pallas_call | solution.py:310
  18.4 0.0 collective-permute-done.4.corner_l
  18.4 1.5 %collective-permute-done.5.corner_r = bf16[2,128,256]{2,1,0:T(8,128)(2,1)S(1)} collective-permute-done((bf16[2,128,256]{2,1,0:T(8,128)(2,1)S(1)}, bf16[2,128,256]{2,1,0:T(8,128)(2,1)S(1)}, u32[]{:S(2)}, u32[]{:S(2)}) %collective-permute-start.5) | collective-permute-done | bytes 131104 | tf_op jit(solution)/shard_map/ppermute | solution.py:308
  19.9 1.0 %fine_level.1 = (bf16[512,256]{1,0:T(8,128)(2,1)S(1)}, bf16[1152,128]{1,0:T(8,128)(2,1)S(1)}) custom-call(bf16[2,128,256]{2,1,0:T(8,128)(2,1)S(1)} %collective-permute-done.4.corner_l, bf16[2,128,256]{2,1,0:T(8,128)(2,1)S(1)} %collective-permute-done.5.corner_r, f32[512,256]{1,0:T(8,128)S(1)} %get-tuple-element.65.mixed_in, ...), custom_call_target="tpu_custom_call" | custom-call | bytes 8388608 | tf_op jit(solution)/shard_map/fine_level/pallas_call | solution.py:324
  20.9 22.0 %all_to_all.15 = bf16[64,9,2,128]{3,2,1,0:T(2,128)(2,1)S(1)} all-to-all(bf16[64,9,2,128]{3,2,1,0:T(2,128)(2,1)S(1)} %bitcast.15), channel_id=1, replica_groups={{63,62,55,54,47,46,39,38,31,30,23,22,15,14,7,6,61,60,53,52,45,44,37,36,..., dimensions={0} | all-to-all | bytes 589824 | tf_op jit(solution)/shard_map/all_to_all | solution.py:335
  42.9 0.0 copy-start
  42.9 0.0 copy-start.1
  42.9 0.0 copy-start.2
  42.9 0.0 copy-start.4
  42.9 0.0 copy-done.3
  42.9 0.5 top_sum.1
  43.4 10.0 %all_to_all.16.got = bf16[8,40,256]{2,1,0:T(8,128)(2,1)S(1)} all-to-all(bf16[8,40,256]{2,1,0:T(8,128)(2,1)S(1)} %top_sum.1), channel_id=1, replica_groups={{56,48,40,32,24,16,8,0},{57,49,41,33,25,17,9,1},{58,50,42,34,26,18,10,2..., dimensions={0} | all-to-all | bytes 327680 | tf_op jit(solution)/shard_map/all_to_all | solution.py:344
  53.4 0.2 top_order.1
  53.6 11.1 %all_to_all.17.mine = bf16[4,20,16,256]{3,2,1,0:T(8,128)(2,1)S(1)} all-to-all(bf16[4,20,16,256]{3,2,1,0:T(8,128)(2,1)S(1)} %top_order.1), channel_id=1, replica_groups={{6,4,2,0},{7,5,3,1},{14,12,10,8},{15,13,11,9},{22,20,18,16},{23,21,19,1..., dimensions={0} | all-to-all | bytes 1310720 | tf_op jit(solution)/shard_map/all_to_all | solution.py:348
  64.7 0.3 top_give.1
  65.0 5.2 %collective-permute-start.6 = (bf16[768,256]{1,0:T(8,128)(2,1)S(1)}, bf16[768,256]{1,0:T(8,128)(2,1)S(1)}, u32[]{:S(2)}, u32[]{:S(2)}) collective-permute-start(bf16[768,256]{1,0:T(8,128)(2,1)S(1)} %top_give.1), channel_id=1, source_target_pairs={{0,1},{1,0},{2,3},{3,2},{4,5},{5,4},{6,7},{7,6},{8,9},{9,8},{10,11... | collective-permute-start | bytes 1179656 | tf_op jit(solution)/shard_map/ppermute | solution.py:352
  70.2 0.3 top_keep.1
  70.4 1.0 %collective-permute-done.6.parcel = bf16[768,256]{1,0:T(8,128)(2,1)S(1)} collective-permute-done((bf16[768,256]{1,0:T(8,128)(2,1)S(1)}, bf16[768,256]{1,0:T(8,128)(2,1)S(1)}, u32[]{:S(2)}, u32[]{:S(2)}) %collective-permute-start.6) | collective-permute-done | bytes 393248 | tf_op jit(solution)/shard_map/ppermute | solution.py:352
  71.5 0.0 copy-done
  71.5 0.0 copy-done.1
  71.5 0.0 copy-done.2
  71.5 0.0 copy-done.4
  71.5 1.5 %top_level.1 = bf16[1,2,2,128,256]{4,3,2,1,0:T(8,128)(2,1)} custom-call(bf16[768,256]{1,0:T(8,128)(2,1)S(1)} %collective-permute-done.6.parcel, f32[512,256]{1,0:T(8,128)S(1)} %get-tuple-element.77.mixed, bf16[4,64,256]{2,1,0:T(8,128)(2,1)S(1)} %get-tuple-element.78.chosen, bf16[512,256]{1,0:T(8,128)(2,1)S(1)} %get-tuple-element.79.fine, ...), custom_call_target="tpu_custom_call" | custom-call | bytes 8388608 | tf_op jit(solution)/shard_map/top_level/pallas_call | solution.py:356
  (3 shorter events, 0.1 us)
Async XLA Ops:
  1.1 14.2 %collective-permute-start = (bf16[1,1,2,128,256]{4,3,2,1,0:T(8,128)(2,1)S(1)}, bf16[1,1,2,128,256]{4,3,2,1,0:T(8,128)(2,1)S(1)}, u32[]{:S(2)}, u32[]{:S(2)}) collective-permute-start(bf16[1,1,2,128,256]{4,3,2,1,0:T(8,128)(2,1)S(1)} %get-tuple-element.43), channel_id=1, source_target_pairs={{8,0},{16,8},{24,16},{32,24},{40,32},{48,40},{56,48},{9,1},{17,9},... | collective-permute-start | bytes 393224 | tf_op jit(solution)/shard_map/ppermute | solution.py:290
  2.4 12.9 %collective-permute-start.1 = (bf16[1,1,2,128,256]{4,3,2,1,0:T(8,128)(2,1)S(1)}, bf16[1,1,2,128,256]{4,3,2,1,0:T(8,128)(2,1)S(1)}, u32[]{:S(2)}, u32[]{:S(2)}) collective-permute-start(bf16[1,1,2,128,256]{4,3,2,1,0:T(8,128)(2,1)S(1)} %get-tuple-element.44), channel_id=1, source_target_pairs={{0,8},{8,16},{16,24},{24,32},{32,40},{40,48},{48,56},{1,9},{9,17},... | collective-permute-start | bytes 393224 | tf_op jit(solution)/shard_map/ppermute | solution.py:291
  7.9 8.6 %collective-permute-start.2 = (bf16[272,256]{1,0:T(8,128)(2,1)S(1)}, bf16[272,256]{1,0:T(8,128)(2,1)S(1)}, u32[]{:S(2)}, u32[]{:S(2)}) collective-permute-start(bf16[272,256]{1,0:T(8,128)(2,1)S(1)} %get-tuple-element.59), channel_id=1, source_target_pairs={{1,0},{2,1},{3,2},{4,3},{5,4},{6,5},{7,6},{0,7},{9,8},{10,9},{11,1... | collective-permute-start | bytes 417800 | tf_op jit(solution)/shard_map/ppermute | solution.py:293
  13.9 2.6 %collective-permute-start.3 = (bf16[272,256]{1,0:T(8,128)(2,1)S(1)}, bf16[272,256]{1,0:T(8,128)(2,1)S(1)}, u32[]{:S(2)}, u32[]{:S(2)}) collective-permute-start(bf16[272,256]{1,0:T(8,128)(2,1)S(1)} %get-tuple-element.60), channel_id=1, source_target_pairs={{0,1},{1,2},{2,3},{3,4},{4,5},{5,6},{6,7},{7,0},{8,9},{9,10},{10,1... | collective-permute-start | bytes 417800 | tf_op jit(solution)/shard_map/ppermute | solution.py:292
  15.4 3.0 %collective-permute-start.4 = (bf16[2,128,256]{2,1,0:T(8,128)(2,1)S(1)}, bf16[2,128,256]{2,1,0:T(8,128)(2,1)S(1)}, u32[]{:S(2)}, u32[]{:S(2)}) collective-permute-start(bf16[2,128,256]{2,1,0:T(8,128)(2,1)S(1)} %pad_maximum_fusion), channel_id=1, source_target_pairs={{0,1},{1,2},{2,3},{3,4},{4,5},{5,6},{6,7},{7,0},{8,9},{9,10},{10,1... | collective-permute-start | bytes 393224 | tf_op jit(solution)/shard_map/ppermute | solution.py:307
  15.5 4.4 %collective-permute-start.5 = (bf16[2,128,256]{2,1,0:T(8,128)(2,1)S(1)}, bf16[2,128,256]{2,1,0:T(8,128)(2,1)S(1)}, u32[]{:S(2)}, u32[]{:S(2)}) collective-permute-start(bf16[2,128,256]{2,1,0:T(8,128)(2,1)S(1)} %pad_maximum_fusion.1), channel_id=1, source_target_pairs={{1,0},{2,1},{3,2},{4,3},{5,4},{6,5},{7,6},{0,7},{9,8},{10,9},{11,1... | collective-permute-start | bytes 393224 | tf_op jit(solution)/shard_map/ppermute | solution.py:308
  16.5 26.4 %copy-start.3 = (f32[256]{0:T(256)S(1)}, f32[256]{0:T(256)}, u32[]{:S(2)}) copy-start(f32[256]{0:T(256)} %param.32) | copy-start | bytes 3076
  42.9 28.6 %copy-start = (bf16[256,256]{1,0:T(8,128)(2,1)S(1)}, bf16[256,256]{1,0:T(8,128)(2,1)}, u32[]{:S(2)}) copy-start(bf16[256,256]{1,0:T(8,128)(2,1)} %w_msg.1) | copy-start | bytes 393220
  42.9 28.6 %copy-start.1 = (bf16[256,256]{1,0:T(8,128)(2,1)S(1)}, bf16[256,256]{1,0:T(8,128)(2,1)}, u32[]{:S(2)}) copy-start(bf16[256,256]{1,0:T(8,128)(2,1)} %w_agg.1) | copy-start | bytes 393220
  42.9 28.6 %copy-start.2 = (bf16[256,256]{1,0:T(8,128)(2,1)S(1)}, bf16[256,256]{1,0:T(8,128)(2,1)}, u32[]{:S(2)}) copy-start(bf16[256,256]{1,0:T(8,128)(2,1)} %w_down.1) | copy-start | bytes 393220
  42.9 28.6 %copy-start.4 = (f32[256]{0:T(256)S(1)}, f32[256]{0:T(256)}, u32[]{:S(2)}) copy-start(f32[256]{0:T(256)} %param.33) | copy-start | bytes 3076
  65.0 6.5 %collective-permute-start.6 = (bf16[768,256]{1,0:T(8,128)(2,1)S(1)}, bf16[768,256]{1,0:T(8,128)(2,1)S(1)}, u32[]{:S(2)}, u32[]{:S(2)}) collective-permute-start(bf16[768,256]{1,0:T(8,128)(2,1)S(1)} %top_give.1), channel_id=1, source_target_pairs={{0,1},{1,0},{2,3},{3,2},{4,5},{5,4},{6,7},{7,6},{8,9},{9,8},{10,11... | collective-permute-start | bytes 1179656 | tf_op jit(solution)/shard_map/ppermute | solution.py:352
